TPU v7x, 128 devices: a whole 4x4x4 slice. The times are simulated.
128 devices in a mesh: gx: 16 (over y, z), gy: 8 (over x, core).
Axes of the slice: x: 4, y: 4, z: 4, core: 2. Of those that a mesh axis runs over, the one named last changes fastest.
Arguments:
- phase_one: float32 [4, 2, 2048, 1024], P(None, None, 'gx', 'gy'), may hold values from -3.140625 to 3.140625
- phase_two: float32 [4, 2, 2048, 1024], P(None, None, 'gx', 'gy'), may hold values from -3.140625 to 3.140625
- hop_one: float32 [3, 2048, 1024], P(None, 'gx', 'gy'), may hold values from 0.08 to 0.16
- hop_two: float32 [3, 2048, 1024], P(None, 'gx', 'gy'), may hold values from 0.08 to 0.16
- onsite_one: float32 [2, 2048, 1024], P(None, 'gx', 'gy'), may hold values from -0.25 to 0.25
- onsite_two: float32 [2, 2048, 1024], P(None, 'gx', 'gy'), may hold values from -0.25 to 0.25
- coupling: float32 [16, 8, 8, 2, 16, 2, 16], P('gx', 'gy'), may hold values from -0.3 to 0.3
- owner: int32 [16, 8, 8], P('gx', 'gy'), may hold values from 0 to 127, as said below
- target_row: int32 [16, 8, 8], P('gx', 'gy'), may hold values from 0 to 112
- live_strips: int32 [16, 8], P('gx', 'gy'), may hold values from 1 to 8, as said below
Outputs:
- first_two: float32 [4, 2, 2, 2048, 1024], P(None, None, None, 'gx', 'gy')
- second_two: float32 [4, 2, 2, 2048, 1024], P(None, None, None, 'gx', 'gy')
- first_three: float32 [4, 2, 2, 2048, 1024], P(None, None, None, 'gx', 'gy')
- second_three: float32 [4, 2, 2, 2048, 1024], P(None, None, None, 'gx', 'gy')
Inputs may be any that keep to these rules, and one draw needn't show every extreme that they name: owner[i, j, k] = gi * 8 + gj, where gi and gj differ from i and j by at most one. `live_strips`: some block holds all 8 strips.
All inputs are finite; a program needn't handle non-finite values.
Results may differ from a plain program's by a relative error of at most 0.003.
Values may be sent and summed in bfloat16 or wider, within the bound.
No kernel may reach another device: no remote copies, remote signals or barrier semaphores. Data moves between devices by JAX's collectives and lax.ppermute only.
A program may use at most 128 MiB of HBM per device.

v0:
```python
import math

import jax
import jax.numpy as jnp
from jax import lax
from jax.experimental import pallas as pl
from jax.experimental.pallas import tpu as pltpu
from jax.sharding import PartitionSpec as P

RING = 4
T = 128
KS = 8
SR = 16
HALO = RING + 2
HOMES = HALO * 3
F32 = jnp.float32
BF16 = jnp.bfloat16
I16 = jnp.int16
PHASE_UNIT = math.pi / 32768.0
HOP_MID, HOP_UNIT = 0.12, 0.04 / 32767.0
SITE_UNIT = 0.25 / 32767.0
COUPLING_UNIT = 0.3 / 32767.0
VMEM_LIMIT = 28 * 1024 * 1024


PHASE_ROWS = 4 * T
ROW_EDGE, COL_EDGE, CODE, AT = 64, 66, 68, 69
SMALL_ROWS = 80
CARGO = PHASE_ROWS + SMALL_ROWS
LAND, ANY, SRC_ROW, SRC_COL, USED = 0, 24, 48, 72, 96
IDX_ROWS = 120


def coded(values, unit):
    return jnp.clip(jnp.round(values * (1.0 / unit)), -32768.0, 32767.0).astype(jnp.int32).astype(I16)


def decoded(code):
    return code.astype(jnp.int32).astype(F32)


def moved(array, axis, by):
    size = lax.axis_size(axis)
    return lax.ppermute(array, axis, [(i, i + by) for i in range(size) if 0 <= i + by < size])


def ring_moved(array, by):
    size = lax.axis_size("gx")
    pairs = [(i, i // RING * RING + (i + by) % RING) for i in range(size)]
    return lax.ppermute(array, "gx", pairs)


def lane_iota(shape, dim):
    return lax.broadcasted_iota(jnp.int32, shape, dim)


def encode_kernel(flags, phase_one, phase_two, small, *outs):
    z = flags[0, 0]
    for d, out in enumerate(outs):
        state = (z + d) % RING
        for layer, phase in enumerate((phase_one, phase_two)):
            for a in range(2):
                at = (layer * 2 + a) * T
                out[at : at + T, :] = coded(phase[state, a], PHASE_UNIT)
        out[PHASE_ROWS:, :] = small[...]


def pack_kernel(hop_one, hop_two, onsite_one, onsite_two, out):
    for layer, (hop, site) in enumerate(((hop_one, onsite_one), (hop_two, onsite_two))):
        for n in range(5):
            at = (layer * 5 + n) * T
            value = coded(hop[n] - HOP_MID, HOP_UNIT) if n < 3 else coded(site[n - 3], SITE_UNIT)
            out[at : at + T, :] = value


def region_kernel(flags, part0, part1, part2, part3, region, first_block, last_block):
    z = flags[0, 0]
    for d, part in enumerate((part0, part1, part2, part3)):
        region[(z + RING - d) % RING] = part[...]
    first_block[...] = region[0]
    last_block[...] = region[RING - 1]


def operators_kernel(flags, part0, part1, part2, part3, ops):
    z = flags[0, 0]
    for d, part in enumerate((part0, part1, part2, part3)):
        at = pl.ds(pl.multiple_of((z + RING - d) % RING * T, T), T)
        for layer in range(2):
            for n in range(5):
                base = (layer * 5 + n) * T
                raw = decoded(part[base : base + T, :])
                ops[layer, n, at, :] = raw * HOP_UNIT + HOP_MID if n < 3 else raw * SITE_UNIT


def neighbourhood(own, left, right, top, bottom, lcorner, rcorner):
    def block(rb, cb):
        if 1 <= rb <= RING:
            return (left, own, right)[cb].at[rb - 1]
        if cb == 1:
            return top if rb == 0 else bottom
        return (lcorner if cb == 0 else rcorner).at[0 if rb == 0 else 1]

    return block


def build_kernel(own, left, right, top, bottom, lcorner, rcorner, ops_in, idx, bd1, bd2, ops, codes):
    block = neighbourhood(own, left, right, top, bottom, lcorner, rcorner)
    rows, cols = lane_iota((32, 256), 0), lane_iota((32, 256), 1)
    place = ((rows // 16 == cols // 128) & (rows % 16 == cols % 16)).astype(BF16)
    i, j = lane_iota((256, 256), 0), lane_iota((256, 256), 1)
    mask1 = (i // 32) == ((j // 16) % 8)
    mask2 = ((i // 16) % 8) == (j // 32)
    first = (((0,), (0,)), ((), ()))

    def spread(a, b, mask):
        full = lax.dot_general(a, b, first, preferred_element_type=F32)
        return jnp.where(mask, full, 0.0).astype(BF16)

    codes[...] = jnp.zeros_like(codes)
    for home in range(HOMES):
        rb, cb = divmod(home, 3)
        ref = block(rb, cb)
        c = jnp.concatenate([decoded(ref[PHASE_ROWS + n : PHASE_ROWS + n + 32, :]) for n in (0, 32)], 1)
        c = c * COUPLING_UNIT
        high = c.astype(BF16)
        low = (c - high.astype(F32)).astype(BF16)
        bd1[home, 0:256, :] = spread(high, place, mask1)
        bd1[home, 256:512, :] = spread(low, place, mask1)
        if cb == 1 and 1 <= rb <= RING:
            bd2[rb - 1, 0:256, :] = spread(place, high, mask2)
            bd2[rb - 1, 256:512, :] = spread(place, low, mask2)
        words = ref[PHASE_ROWS + 64 : PHASE_ROWS + 80, :].astype(jnp.int32)
        codes[0, home : home + 1, :] = words[CODE - 64 : CODE - 63, :]
        codes[1, home : home + 1, :] = words[AT - 64 : AT - 63, :]

    code, at = codes[0], codes[1]
    home = lane_iota((24, T), 0)
    active = code >= 16
    rb = home // 3 + jnp.where(active, ((code >> 2) & 3) - 1, 0)
    cb = home % 3 + jnp.where(active, (code & 3) - 1, 0)
    lands = active & (cb == 1) & (rb >= 1) & (rb <= RING)
    idx[LAND : LAND + 24, :] = jnp.where(lands, (rb - 1) * T + at, -1)
    some = jnp.max(jnp.where(lands, 1.0, 0.0), axis=1, keepdims=True)
    idx[ANY : ANY + 24, :] = jnp.broadcast_to(some, (24, T)).astype(jnp.int32)
    idx[SRC_ROW : SRC_ROW + 24, :] = jnp.clip(rb * T + at, 0, HALO * T - SR)
    idx[SRC_COL : SRC_COL + 24, :] = jnp.clip(cb, 0, 2)
    mine = active & (home % 3 == 1) & (home // 3 >= 1) & (home // 3 <= RING)
    source = jnp.where(mine, rb * 3 + cb, -1)
    idx[USED : USED + 24, :] = jnp.zeros((24, T), jnp.int32)
    for n in range(HOMES):
        hit = jnp.where(source == n, 1.0, 0.0)
        used = jnp.max(jnp.max(hit, axis=1, keepdims=True), axis=0, keepdims=True)
        idx[USED + n : USED + n + 1, :] = jnp.broadcast_to(used, (1, T)).astype(jnp.int32)

    ops[:, 0:5] = ops_in[...]
    lane = lane_iota((T, T), 1)

    def edge(ref, row):
        words = decoded(ref[PHASE_ROWS + 64 : PHASE_ROWS + 80, :])
        return words[row - 64 : row - 63, :] * HOP_UNIT + HOP_MID

    for layer in range(2):
        ops[layer, 5, 0 : RING * T - 1, :] = ops_in[layer, 1, 1 : RING * T, :]
        ops[layer, 5, RING * T - 1 : RING * T, :] = edge(bottom, ROW_EDGE + layer)
        for r in range(RING):
            rows = slice(r * T, (r + 1) * T)
            column = jnp.broadcast_to(edge(right.at[r], COL_EDGE + layer), (T, T)).T
            ops[layer, 6, rows, :] = jnp.where(lane == T - 1, column, pltpu.roll(ops_in[layer, 2, rows, :], T - 1, 1))


def cos_sin(code):
    q = code.astype(jnp.int32)
    quarter = (q + 8192) >> 14
    r = (q - (quarter << 14)).astype(F32) * PHASE_UNIT
    r2 = r * r
    s = r * (1.0 + r2 * (-1.6666654611e-1 + r2 * (8.3321608736e-3 + r2 * -1.9515295891e-4)))
    c = 1.0 + r2 * (-0.5 + r2 * (4.166664568298827e-2 + r2 * (-1.388731625493765e-3 + r2 * 2.443315711809948e-5)))
    odd = (quarter & 1) == 1
    cos_v = jnp.where(odd, s, c)
    sin_v = jnp.where(odd, c, s)
    cos_v = jnp.where(((quarter + 1) & 2) == 2, -cos_v, cos_v)
    sin_v = jnp.where((quarter & 2) == 2, -sin_v, sin_v)
    return cos_v, sin_v


def zero_kernel(region, zero_out, narrow_out):
    for rb in range(RING):
        rows = slice(rb * T, (rb + 1) * T)
        for layer in range(2):
            for a in range(2):
                at = (layer * 2 + a) * T
                pair = cos_sin(region[rb, at : at + T, :])
                for p in range(2):
                    zero_out[layer, a, p, rows, :] = pair[p]
                    narrow_out[rb, layer, a * T : (a + 1) * T, p * T : (p + 1) * T] = pair[p].astype(BF16)


def step_kernel(first, last, *refs):
    refs = list(refs)
    flags, idx, own, left, right, top, bottom, lcorner, rcorner, bd1, bd2, ops = refs[:12]
    refs = refs[12:]
    around = neighbourhood(own, left, right, top, bottom, lcorner, rcorner)
    prev = None if first else refs.pop(0)
    wide_out = refs.pop(0) if first else None
    if last:
        parts = refs[:RING]
        refs = refs[RING:]
        narrow_out = refs.pop()
    else:
        narrow_out, first_out, last_out = refs[:3]
        refs = refs[3:]
        parts = []
        if not first:
            parts = refs[:RING]
            refs = refs[RING:]
    fu, fv, gathered, terms, acc1, acc2 = refs[:6]
    xv = refs[6] if first else None

    def keep(rb, cb):
        if cb != 1:
            return flags[0, 3 if cb == 0 else 4].astype(F32)
        return flags[0, 1 if rb == 0 else 2].astype(F32)

    def store(layer, rb, cb, a, pair):
        for p in range(2):
            if layer == 1:
                xv[rb * 3 + cb, a * T : (a + 1) * T, p * T : (p + 1) * T] = pair[p]
            if layer == 0:
                fu[cb, a, p, rb * T : (rb + 1) * T, :] = pair[p].astype(F32)
            elif cb == 1:
                fv[a, p, rb * T : (rb + 1) * T, :] = pair[p].astype(F32)

    def decode(layer, rb, cb, a):
        at = (layer * 2 + a) * T
        pair = cos_sin(around(rb, cb)[at : at + T, :])
        factor = keep(rb, cb)
        store(layer, rb, cb, a, tuple((v * factor).astype(BF16) for v in pair))

    for cb in range(3):
        for rb in range(HALO):
            inner = 1 <= rb <= RING
            for layer in range(2):
                if first and not (cb == 1 and inner):
                    edge = None
                    if cb == 1:
                        edge = 1 if rb == 0 else 0
                    elif inner:
                        edge = 1 if cb == 0 else 0
                    if edge is not None:
                        decode(layer, rb, cb, edge)
                    home = rb * 3 + cb

                    @pl.when(idx[USED + home if layer == 0 else ANY + home, 0] > 0)
                    def _():
                        for a in range(2):
                            if a != edge:
                                decode(layer, rb, cb, a)

                    continue
                if layer == 1 and cb != 1:
                    continue
                ref = around(rb, cb).at[layer]
                for a in range(2):
                    for p in range(2):
                        value = ref[a * T : (a + 1) * T, p * T : (p + 1) * T].astype(F32)
                        if layer == 0:
                            fu[cb, a, p, rb * T : (rb + 1) * T, :] = value
                        else:
                            fv[a, p, rb * T : (rb + 1) * T, :] = value

    for r in range(RING):
        home = (r + 1) * 3 + 1
        for k in range(KS):
            row = idx[SRC_ROW + home, k]
            col = idx[SRC_COL + home, k]
            for a in range(2):
                for p in range(2):
                    piece = fu[col, a, p, pl.ds(row, SR), :].astype(BF16)
                    gathered[k * 32 + a * SR : k * 32 + (a + 1) * SR, p * T : (p + 1) * T] = piece
        both = jnp.dot(bd2[r], gathered[...], preferred_element_type=F32)
        summed = both[:256] + both[256:]
        for b in range(2):
            for p in range(2):
                acc2[b, p, r * T : (r + 1) * T, :] = summed[b * T : (b + 1) * T, p * T : (p + 1) * T]

    acc1[...] = jnp.zeros_like(acc1)
    for home in range(HOMES):
        rb, cb = divmod(home, 3)

        @pl.when(idx[ANY + home, 0] > 0)
        def _():
            decoded_here = first and not (cb == 1 and 1 <= rb <= RING)
            source = xv[home] if decoded_here else around(rb, cb)[1]
            both = jnp.dot(bd1[home], source, preferred_element_type=F32)
            terms[...] = both[:256] + both[256:]
            for k in range(KS):
                row = idx[LAND + home, k]

                @pl.when(row >= 0)
                def _():
                    for a in range(2):
                        for p in range(2):
                            at = (a, p, pl.ds(row, SR), slice(None))
                            acc1[at] = acc1[at] + terms[
                                k * 32 + a * SR : k * 32 + (a + 1) * SR, p * T : (p + 1) * T
                            ]

    lane = lane_iota((T, T), 1)
    for layer in range(2):
        acc = (acc1, acc2)[layer]

        def field(a, p, low):
            if layer == 0:
                return fu[1, a, p, low : low + T, :]
            return fv[a, p, low : low + T, :]

        def beside(a, p, r, cb):
            if layer == 0:
                return fu[cb, a, p, (r + 1) * T : (r + 2) * T, :]
            where = (slice(a * T, (a + 1) * T), slice(p * T, (p + 1) * T))
            if first:
                return xv[(r + 1) * 3 + cb, where[0], where[1]].astype(F32)
            return around(r + 1, cb)[1, where[0], where[1]].astype(F32)

        for r in range(RING):
            rows = slice(r * T, (r + 1) * T)
            h0, h1, h2, e0, e1, h1s, h2s = [ops[layer, n, rows, :] for n in range(7)]
            for p in range(2):
                base = (r + 1) * T
                w0, w1 = field(0, p, base), field(1, p, base)
                before = jnp.where(lane == 0, pltpu.roll(beside(1, p, r, 0), 1, 1), pltpu.roll(w1, 1, 1))
                after = jnp.where(
                    lane == T - 1, pltpu.roll(beside(0, p, r, 2), T - 1, 1), pltpu.roll(w0, T - 1, 1)
                )
                upper = e0 * w0 + h0 * w1 + h1 * field(1, p, base - 1) + h2 * before + acc[0, p, rows, :]
                lower = e1 * w1 + h0 * w0 + h1s * field(0, p, base + 1) + h2s * after + acc[1, p, rows, :]
                for a, value in enumerate((upper, lower)):
                    if first:
                        wide_out[layer, a, p, rows, :] = value
                    else:
                        value = 2.0 * value - prev[layer, a, p, rows, :]
                    narrow_out[r, layer, a * T : (a + 1) * T, p * T : (p + 1) * T] = value.astype(BF16)

    if not last:
        first_out[...] = narrow_out[0]
        last_out[...] = narrow_out[RING - 1]
    for d, part in enumerate(parts):
        part[...] = narrow_out[(flags[0, 0] + d) % RING]


def result_kernel(flags, part0, part1, part2, part3, out_one, out_two):
    z = flags[0, 0]
    for d, part in enumerate((part0, part1, part2, part3)):
        state = (z + RING - d) % RING
        for layer, out in enumerate((out_one, out_two)):
            for p in range(2):
                for a in range(2):
                    out[state, p, a] = part[layer, a * T : (a + 1) * T, p * T : (p + 1) * T].astype(F32)


SMEM = pl.BlockSpec(memory_space=pltpu.SMEM)
VMEM = pl.BlockSpec(memory_space=pltpu.VMEM)
PARAMS = pltpu.CompilerParams(vmem_limit_bytes=VMEM_LIMIT)
WIDE = jax.ShapeDtypeStruct((2, 2, 2, RING * T, T), F32)
NARROW = jax.ShapeDtypeStruct((RING, 2, 2 * T, 2 * T), BF16)
BLOCK = jax.ShapeDtypeStruct((2, 2 * T, 2 * T), BF16)


def local(kernel, out_shape, scalars, *operands, scratch=()):
    return pl.pallas_call(
        kernel,
        out_shape=out_shape,
        in_specs=[SMEM] * len(scalars) + [VMEM] * len(operands),
        out_specs=jax.tree.map(lambda _: VMEM, out_shape),
        scratch_shapes=list(scratch),
        compiler_params=PARAMS,
    )(*scalars, *operands)


def step(first, last, flags, idx, halo, bd1, bd2, ops, prev=None):
    scratch = [
        pltpu.VMEM((3, 2, 2, HALO * T, T), F32),
        pltpu.VMEM((2, 2, HALO * T, T), F32),
        pltpu.VMEM((2 * T, 2 * T), BF16),
        pltpu.VMEM((2 * T, 2 * T), F32),
        pltpu.VMEM((2, 2, RING * T, T), F32),
        pltpu.VMEM((2, 2, RING * T, T), F32),
    ]
    if first:
        scratch.append(pltpu.VMEM((HOMES, 2 * T, 2 * T), BF16))
        out = (WIDE, NARROW, BLOCK, BLOCK)
    elif last:
        scratch.append(pltpu.VMEM(NARROW.shape, BF16))
        out = (BLOCK,) * RING
    else:
        out = (NARROW, BLOCK, BLOCK) + (BLOCK,) * RING
    operands = [*halo, bd1, bd2, ops] + ([] if first else [prev])
    return local(lambda *refs: step_kernel(first, last, *refs), out, (flags, idx), *operands, scratch=scratch)


def halo_of(region, first_block, last_block):
    top = moved(last_block, "gx", RING)
    bottom = moved(first_block, "gx", -RING)
    left = moved(region, "gy", 1)
    right = moved(region, "gy", -1)
    ends = jnp.stack([top, bottom])
    return (region, left, right, top, bottom, moved(ends, "gy", 1), moved(ends, "gy", -1))


def results(flags, parts):
    parts = [parts[0]] + [ring_moved(parts[d], d) for d in range(1, RING)]
    shape = jax.ShapeDtypeStruct((RING, 2, 2, T, T), F32)
    return local(result_kernel, (shape, shape), (flags,), *parts)


def body(phase_one, phase_two, hop_one, hop_two, onsite_one, onsite_two, coupling, owner, target_row, live_strips):
    grid_row, grid_col = lax.axis_index("gx"), lax.axis_index("gy")
    rows_n, cols_n = lax.axis_size("gx"), lax.axis_size("gy")
    flags = jnp.stack(
        [grid_row % RING, grid_row >= RING, grid_row < rows_n - RING, grid_col > 0, grid_col < cols_n - 1]
    )
    flags = flags.astype(jnp.int32).reshape(1, 5)

    active = jnp.arange(KS, dtype=jnp.int32) < live_strips[0, 0]
    masked = jnp.where(active[:, None, None, None, None], coupling[0, 0], 0.0)
    weights = masked.reshape(2, 4, 2, SR, 2, SR).transpose(0, 4, 5, 1, 2, 3).reshape(64, T)
    drow, dcol = owner[0, 0] // cols_n - grid_row, owner[0, 0] % cols_n - grid_col
    code = jnp.where(active, 16 + (drow + 1) * 4 + dcol + 1, 0)
    at = jnp.where(active, target_row[0, 0], 0)
    places = jnp.pad(jnp.stack([code, at]), ((0, 10), (0, T - KS))).astype(I16)
    edges = jnp.stack([hop_one[1, 0, :], hop_two[1, 0, :], hop_one[2, :, 0], hop_two[2, :, 0]])
    small = jnp.concatenate([coded(weights, COUPLING_UNIT), coded(edges - HOP_MID, HOP_UNIT), places], 0)

    cargo = jax.ShapeDtypeStruct((CARGO, T), I16)
    sends = local(encode_kernel, (cargo,) * RING, (flags,), phase_one, phase_two, small)
    parts = [sends[0]] + [ring_moved(sends[d], d) for d in range(1, RING)]
    packed = local(
        pack_kernel, jax.ShapeDtypeStruct((10 * T, T), I16), (), hop_one, hop_two, onsite_one, onsite_two
    )
    packs = [packed] + [ring_moved(packed, d) for d in range(1, RING)]

    region = local(
        region_kernel, (jax.ShapeDtypeStruct((RING, CARGO, T), I16), cargo, cargo), (flags,), *parts
    )
    halo = halo_of(*region)
    zero, zero_narrow = local(zero_kernel, (WIDE, NARROW), (), region[0])
    ops = local(operators_kernel, jax.ShapeDtypeStruct((2, 5, RING * T, T), F32), (flags,), *packs)
    idx, bd1, bd2, ops = local(
        build_kernel,
        (
            jax.ShapeDtypeStruct((IDX_ROWS, T), jnp.int32),
            jax.ShapeDtypeStruct((HOMES, 512, 256), BF16),
            jax.ShapeDtypeStruct((RING, 512, 256), BF16),
            jax.ShapeDtypeStruct((2, 7, RING * T, T), F32),
        ),
        (),
        *halo,
        ops,
        scratch=[pltpu.VMEM((2, 24, T), jnp.int32)],
    )

    one, *one_blocks = step(True, False, flags, idx, (zero_narrow, *halo[1:]), bd1, bd2, ops)
    *two_blocks, part0, part1, part2, part3 = step(
        False, False, flags, idx, halo_of(*one_blocks), bd1, bd2, ops, zero
    )
    three_parts = step(False, True, flags, idx, halo_of(*two_blocks), bd1, bd2, ops, one)
    two_a, two_b = results(flags, (part0, part1, part2, part3))
    three_a, three_b = results(flags, three_parts)
    return two_a, two_b, three_a, three_b


def solution(mesh):
    field = P(None, None, "gx", "gy")
    site = P(None, "gx", "gy")
    out = P(None, None, None, "gx", "gy")
    return jax.shard_map(
        body,
        mesh=mesh,
        in_specs=(
            field,
            field,
            site,
            site,
            site,
            site,
            P("gx", "gy", None, None, None, None, None),
            P("gx", "gy", None),
            P("gx", "gy", None),
            P("gx", "gy"),
        ),
        out_specs=(out, out, out, out),
        check_vma=False,
    )
```

profile of v0, /device:TPU:10, one launch (start us, length us, event | category | flops | bytes accessed | tf_op | source)
XLA Modules:
  0.0 154.9 jit_solution(12355308074409257421)
XLA Ops:
  11.2 3.6 %collective-permute-start.1 = (s16[592,128]{1,0:T(8,128)(2,1)S(1)}, s16[592,128]{1,0:T(8,128)(2,1)S(1)}, u32[]{:S(2)}, u32[]{:S(2)}) collective-permute-start(s16[592,128]{1,0:T(8,128)(2,1)S(1)} %get-tuple-element.38), channel_id=1, source_target_pairs={{0,16},{8,24},{16,0},{24,8},{32,48},{40,56},{48,32},{56,40},{64,80... | collective-permute-start | bytes 454664 | tf_op jit(solution)/shard_map/ppermute | solution.py:50
  17.2 4.4 %collective-permute-done.1.part2 = s16[592,128]{1,0:T(8,128)(2,1)S(1)} collective-permute-done((s16[592,128]{1,0:T(8,128)(2,1)S(1)}, s16[592,128]{1,0:T(8,128)(2,1)S(1)}, u32[]{:S(2)}, u32[]{:S(2)}) %collective-permute-start.1) | collective-permute-done | bytes 151584 | tf_op jit(solution)/shard_map/ppermute | solution.py:50
  22.3 3.5 %collective-permute-start.5 = (s16[592,128]{1,0:T(8,128)(2,1)S(1)}, s16[592,128]{1,0:T(8,128)(2,1)S(1)}, u32[]{:S(2)}, u32[]{:S(2)}) collective-permute-start(s16[592,128]{1,0:T(8,128)(2,1)S(1)} %get-tuple-element.41), channel_id=1, source_target_pairs={{0,32},{8,40},{16,48},{24,56},{32,64},{40,72},{48,80},{56,88},{64,... | collective-permute-start | bytes 454664 | tf_op jit(solution)/shard_map/ppermute | solution.py:44
  31.2 2.4 %collective-permute-start.3 = (s16[4,592,128]{2,1,0:T(8,128)(2,1)S(1)}, s16[4,592,128]{2,1,0:T(8,128)(2,1)S(1)}, u32[]{:S(2)}, u32[]{:S(2)}) collective-permute-start(s16[4,592,128]{2,1,0:T(8,128)(2,1)S(1)} %get-tuple-element.40.own.region), channel_id=1, source_target_pairs={{0,1},{1,2},{2,3},{3,4},{4,5},{5,6},{6,7},{8,9},{9,10},{10,11},{11... | collective-permute-start | bytes 1818632 | tf_op jit(solution)/shard_map/ppermute | solution.py:44
  33.7 2.4 %collective-permute-start.6 = (s16[592,128]{1,0:T(8,128)(2,1)S(1)}, s16[592,128]{1,0:T(8,128)(2,1)S(1)}, u32[]{:S(2)}, u32[]{:S(2)}) collective-permute-start(s16[592,128]{1,0:T(8,128)(2,1)S(1)} %get-tuple-element.42), channel_id=1, source_target_pairs={{32,0},{40,8},{48,16},{56,24},{64,32},{72,40},{80,48},{88,56},{96,... | collective-permute-start | bytes 454664 | tf_op jit(solution)/shard_map/ppermute | solution.py:44
  36.0 6.2 %collective-permute-done.6.bottom.refs_6_ = s16[592,128]{1,0:T(8,128)(2,1)S(1)} collective-permute-done((s16[592,128]{1,0:T(8,128)(2,1)S(1)}, s16[592,128]{1,0:T(8,128)(2,1)S(1)}, u32[]{:S(2)}, u32[]{:S(2)}) %collective-permute-start.6) | collective-permute-done | bytes 151584 | tf_op jit(solution)/shard_map/ppermute | solution.py:44
  48.3 5.0 %collective-permute-done.9.part1 = s16[1280,128]{1,0:T(8,128)(2,1)S(1)} collective-permute-done((s16[1280,128]{1,0:T(8,128)(2,1)S(1)}, s16[1280,128]{1,0:T(8,128)(2,1)S(1)}, u32[]{:S(2)}, u32[]{:S(2)}) %collective-permute-start.9) | collective-permute-done | bytes 327712 | tf_op jit(solution)/shard_map/ppermute | solution.py:50
  56.1 7.8 %shard_map.135 = (f32[2,2,2,512,128]{4,3,2,1,0:T(8,128)S(1)}, bf16[4,2,256,256]{3,2,1,0:T(8,128)(2,1)S(1)}, bf16[2,256,256]{2,1,0:T(8,128)(2,1)S(1)}, bf16[2,256,256]{2,1,0:T(8,128)(2,1)S(1)}) custom-call(s32[1,5]{1,0:T(1,128)S(1)} %bitcast.50, s32[120,128]{1,0:T(8,128)S(1)} %get-tuple-element.43.refs_1_, ...), custom_call_target="tpu_custom_call" | custom-call | tf_op jit(solution)/shard_map/pallas_call | solution.py:370
  65.8 2.4 %collective-permute-start.12 = (bf16[4,2,256,256]{3,2,1,0:T(8,128)(2,1)S(1)}, bf16[4,2,256,256]{3,2,1,0:T(8,128)(2,1)S(1)}, u32[]{:S(2)}, u32[]{:S(2)}) collective-permute-start(bf16[4,2,256,256]{3,2,1,0:T(8,128)(2,1)S(1)} %get-tuple-element.48.refs_2_), channel_id=1, source_target_pairs={{0,1},{1,2},{2,3},{3,4},{4,5},{5,6},{6,7},{8,9},{9,10},{10,11},{11... | collective-permute-start | bytes 3145736 | tf_op jit(solution)/shard_map/ppermute | solution.py:44
  68.2 3.8 %collective-permute-start.14 = (bf16[2,256,256]{2,1,0:T(8,128)(2,1)S(1)}, bf16[2,256,256]{2,1,0:T(8,128)(2,1)S(1)}, u32[]{:S(2)}, u32[]{:S(2)}) collective-permute-start(bf16[2,256,256]{2,1,0:T(8,128)(2,1)S(1)} %get-tuple-element.49), channel_id=1, source_target_pairs={{0,32},{8,40},{16,48},{24,56},{32,64},{40,72},{48,80},{56,88},{64,... | collective-permute-start | bytes 786440 | tf_op jit(solution)/shard_map/ppermute | solution.py:44
  74.1 4.8 %collective-permute-done.14.refs_5_ = bf16[2,256,256]{2,1,0:T(8,128)(2,1)S(1)} collective-permute-done((bf16[2,256,256]{2,1,0:T(8,128)(2,1)S(1)}, bf16[2,256,256]{2,1,0:T(8,128)(2,1)S(1)}, u32[]{:S(2)}, u32[]{:S(2)}) %collective-permute-start.14) | collective-permute-done | bytes 262176 | tf_op jit(solution)/shard_map/ppermute | solution.py:44
  78.8 3.9 %collective-permute-done.15.refs_6_ = bf16[2,256,256]{2,1,0:T(8,128)(2,1)S(1)} collective-permute-done((bf16[2,256,256]{2,1,0:T(8,128)(2,1)S(1)}, bf16[2,256,256]{2,1,0:T(8,128)(2,1)S(1)}, u32[]{:S(2)}, u32[]{:S(2)}) %collective-permute-start.15) | collective-permute-done | bytes 262176 | tf_op jit(solution)/shard_map/ppermute | solution.py:44
  84.7 2.4 %collective-permute-start.16 = (bf16[2,2,256,256]{3,2,1,0:T(8,128)(2,1)S(1)}, bf16[2,2,256,256]{3,2,1,0:T(8,128)(2,1)S(1)}, u32[]{:S(2)}, u32[]{:S(2)}) collective-permute-start(bf16[2,2,256,256]{3,2,1,0:T(8,128)(2,1)S(1)} %pad_maximum_fusion), channel_id=1, source_target_pairs={{0,1},{1,2},{2,3},{3,4},{4,5},{5,6},{6,7},{8,9},{9,10},{10,11},{11... | collective-permute-start | bytes 1572872 | tf_op jit(solution)/shard_map/ppermute | solution.py:44
  87.2 4.3 %collective-permute-done.17.refs_8_ = bf16[2,2,256,256]{3,2,1,0:T(8,128)(2,1)S(1)} collective-permute-done((bf16[2,2,256,256]{3,2,1,0:T(8,128)(2,1)S(1)}, bf16[2,2,256,256]{3,2,1,0:T(8,128)(2,1)S(1)}, u32[]{:S(2)}, u32[]{:S(2)}) %collective-permute-start.17) | collective-permute-done | bytes 524320 | tf_op jit(solution)/shard_map/ppermute | solution.py:44
  91.4 3.8 %collective-permute-done.16.refs_7_ = bf16[2,2,256,256]{3,2,1,0:T(8,128)(2,1)S(1)} collective-permute-done((bf16[2,2,256,256]{3,2,1,0:T(8,128)(2,1)S(1)}, bf16[2,2,256,256]{3,2,1,0:T(8,128)(2,1)S(1)}, u32[]{:S(2)}, u32[]{:S(2)}) %collective-permute-start.16) | collective-permute-done | bytes 524320 | tf_op jit(solution)/shard_map/ppermute | solution.py:44
  95.2 5.3 %shard_map.136 = (bf16[4,2,256,256]{3,2,1,0:T(8,128)(2,1)S(1)}, bf16[2,256,256]{2,1,0:T(8,128)(2,1)S(1)}, bf16[2,256,256]{2,1,0:T(8,128)(2,1)S(1)}, bf16[2,256,2...) custom-call(s32[1,5]{1,0:T(1,128)S(1)} %bitcast.51, ...), custom_call_target="tpu_custom_call" | custom-call | tf_op jit(solution)/shard_map/pallas_call | solution.py:370
  102.5 2.4 %collective-permute-start.21 = (bf16[4,2,256,256]{3,2,1,0:T(8,128)(2,1)S(1)}, bf16[4,2,256,256]{3,2,1,0:T(8,128)(2,1)S(1)}, u32[]{:S(2)}, u32[]{:S(2)}) collective-permute-start(bf16[4,2,256,256]{3,2,1,0:T(8,128)(2,1)S(1)} %get-tuple-element.58.refs_2_), channel_id=1, source_target_pairs={{0,1},{1,2},{2,3},{3,4},{4,5},{5,6},{6,7},{8,9},{9,10},{10,11},{11... | collective-permute-start | bytes 3145736 | tf_op jit(solution)/shard_map/ppermute | solution.py:44
  107.1 3.7 %collective-permute-start.24 = (bf16[2,256,256]{2,1,0:T(8,128)(2,1)S(1)}, bf16[2,256,256]{2,1,0:T(8,128)(2,1)S(1)}, u32[]{:S(2)}, u32[]{:S(2)}) collective-permute-start(bf16[2,256,256]{2,1,0:T(8,128)(2,1)S(1)} %get-tuple-element.60), channel_id=1, source_target_pairs={{32,0},{40,8},{48,16},{56,24},{64,32},{72,40},{80,48},{88,56},{96,... | collective-permute-start | bytes 786440 | tf_op jit(solution)/shard_map/ppermute | solution.py:44
  110.8 5.1 %collective-permute-done.23.refs_5_ = bf16[2,256,256]{2,1,0:T(8,128)(2,1)S(1)} collective-permute-done((bf16[2,256,256]{2,1,0:T(8,128)(2,1)S(1)}, bf16[2,256,256]{2,1,0:T(8,128)(2,1)S(1)}, u32[]{:S(2)}, u32[]{:S(2)}) %collective-permute-start.23) | collective-permute-done | bytes 262176 | tf_op jit(solution)/shard_map/ppermute | solution.py:44
  119.9 2.4 %collective-permute-start.25 = (bf16[2,2,256,256]{3,2,1,0:T(8,128)(2,1)S(1)}, bf16[2,2,256,256]{3,2,1,0:T(8,128)(2,1)S(1)}, u32[]{:S(2)}, u32[]{:S(2)}) collective-permute-start(bf16[2,2,256,256]{3,2,1,0:T(8,128)(2,1)S(1)} %pad_maximum_fusion.1), channel_id=1, source_target_pairs={{0,1},{1,2},{2,3},{3,4},{4,5},{5,6},{6,7},{8,9},{9,10},{10,11},{11... | collective-permute-start | bytes 1572872 | tf_op jit(solution)/shard_map/ppermute | solution.py:44
  123.1 3.4 %collective-permute-done.26.refs_8_ = bf16[2,2,256,256]{3,2,1,0:T(8,128)(2,1)S(1)} collective-permute-done((bf16[2,2,256,256]{3,2,1,0:T(8,128)(2,1)S(1)}, bf16[2,2,256,256]{3,2,1,0:T(8,128)(2,1)S(1)}, u32[]{:S(2)}, u32[]{:S(2)}) %collective-permute-start.26) | collective-permute-done | bytes 524320 | tf_op jit(solution)/shard_map/ppermute | solution.py:44
  127.5 2.9 %collective-permute-done.25.refs_7_ = bf16[2,2,256,256]{3,2,1,0:T(8,128)(2,1)S(1)} collective-permute-done((bf16[2,2,256,256]{3,2,1,0:T(8,128)(2,1)S(1)}, bf16[2,2,256,256]{3,2,1,0:T(8,128)(2,1)S(1)}, u32[]{:S(2)}, u32[]{:S(2)}) %collective-permute-start.25) | collective-permute-done | bytes 524320 | tf_op jit(solution)/shard_map/ppermute | solution.py:44
  131.8 5.2 %shard_map.138 = (bf16[2,256,256]{2,1,0:T(8,128)(2,1)S(1)}, bf16[2,256,256]{2,1,0:T(8,128)(2,1)S(1)}, bf16[2,256,256]{2,1,0:T(8,128)(2,1)S(1)}, bf16[2,256,256]{2,1,0:T(8,128)(2,1)S(1)}) custom-call(s32[1,5]{1,0:T(1,128)S(1)} %bitcast.52, s32[120,128]{1,0:T(8,128)S(1)} %get-tuple-element.43.refs_1_, bf16[4,2,256,256]{3,2,1,0:T(8,128)(2,1)S(1)} %get-tuple-element.58.refs_2_, ...), custom_call_target="tpu_custom_call" | custom-call | tf_op jit(solution)/shard_map/pallas_call | solution.py:370
  142.9 9.0 %collective-permute-done.27.part1 = bf16[2,256,256]{2,1,0:T(8,128)(2,1)S(1)} collective-permute-done((bf16[2,256,256]{2,1,0:T(8,128)(2,1)S(1)}, bf16[2,256,256]{2,1,0:T(8,128)(2,1)S(1)}, u32[]{:S(2)}, u32[]{:S(2)}) %collective-permute-start.27) | collective-permute-done | bytes 262176 | tf_op jit(solution)/shard_map/ppermute | solution.py:50
  (75 shorter events, 53.2 us)
Async XLA Ops:
  11.2 10.5 %collective-permute-start.1 = (s16[592,128]{1,0:T(8,128)(2,1)S(1)}, s16[592,128]{1,0:T(8,128)(2,1)S(1)}, u32[]{:S(2)}, u32[]{:S(2)}) collective-permute-start(s16[592,128]{1,0:T(8,128)(2,1)S(1)} %get-tuple-element.38), channel_id=1, source_target_pairs={{0,16},{8,24},{16,0},{24,8},{32,48},{40,56},{48,32},{56,40},{64,80... | collective-permute-start | bytes 454664 | tf_op jit(solution)/shard_map/ppermute | solution.py:50
  22.3 11.4 %collective-permute-start.5 = (s16[592,128]{1,0:T(8,128)(2,1)S(1)}, s16[592,128]{1,0:T(8,128)(2,1)S(1)}, u32[]{:S(2)}, u32[]{:S(2)}) collective-permute-start(s16[592,128]{1,0:T(8,128)(2,1)S(1)} %get-tuple-element.41), channel_id=1, source_target_pairs={{0,32},{8,40},{16,48},{24,56},{32,64},{40,72},{48,80},{56,88},{64,... | collective-permute-start | bytes 454664 | tf_op jit(solution)/shard_map/ppermute | solution.py:44
  26.0 16.7 %collective-permute-start.11 = (s16[1280,128]{1,0:T(8,128)(2,1)S(1)}, s16[1280,128]{1,0:T(8,128)(2,1)S(1)}, u32[]{:S(2)}, u32[]{:S(2)}) collective-permute-start(s16[1280,128]{1,0:T(8,128)(2,1)S(1)} %shard_map.131.part0), channel_id=1, source_target_pairs={{0,24},{8,0},{16,8},{24,16},{32,56},{40,32},{48,40},{56,48},{64,88... | collective-permute-start | bytes 983048 | tf_op jit(solution)/shard_map/ppermute | solution.py:50
  28.2 16.5 %collective-permute-start.10 = (s16[1280,128]{1,0:T(8,128)(2,1)S(1)}, s16[1280,128]{1,0:T(8,128)(2,1)S(1)}, u32[]{:S(2)}, u32[]{:S(2)}) collective-permute-start(s16[1280,128]{1,0:T(8,128)(2,1)S(1)} %shard_map.131.part0), channel_id=1, source_target_pairs={{0,16},{8,24},{16,0},{24,8},{32,48},{40,56},{48,32},{56,40},{64,80... | collective-permute-start | bytes 983048 | tf_op jit(solution)/shard_map/ppermute | solution.py:50
  29.3 24.9 %collective-permute-start.4 = (s16[4,592,128]{2,1,0:T(8,128)(2,1)S(1)}, s16[4,592,128]{2,1,0:T(8,128)(2,1)S(1)}, u32[]{:S(2)}, u32[]{:S(2)}) collective-permute-start(s16[4,592,128]{2,1,0:T(8,128)(2,1)S(1)} %get-tuple-element.40.own.region), channel_id=1, source_target_pairs={{1,0},{2,1},{3,2},{4,3},{5,4},{6,5},{7,6},{9,8},{10,9},{11,10},{12... | collective-permute-start | bytes 1818632 | tf_op jit(solution)/shard_map/ppermute | solution.py:44
  31.2 23.0 %collective-permute-start.3 = (s16[4,592,128]{2,1,0:T(8,128)(2,1)S(1)}, s16[4,592,128]{2,1,0:T(8,128)(2,1)S(1)}, u32[]{:S(2)}, u32[]{:S(2)}) collective-permute-start(s16[4,592,128]{2,1,0:T(8,128)(2,1)S(1)} %get-tuple-element.40.own.region), channel_id=1, source_target_pairs={{0,1},{1,2},{2,3},{3,4},{4,5},{5,6},{6,7},{8,9},{9,10},{10,11},{11... | collective-permute-start | bytes 1818632 | tf_op jit(solution)/shard_map/ppermute | solution.py:44
  42.2 11.1 %collective-permute-start.9 = (s16[1280,128]{1,0:T(8,128)(2,1)S(1)}, s16[1280,128]{1,0:T(8,128)(2,1)S(1)}, u32[]{:S(2)}, u32[]{:S(2)}) collective-permute-start(s16[1280,128]{1,0:T(8,128)(2,1)S(1)} %shard_map.131.part0), channel_id=1, source_target_pairs={{0,8},{8,16},{16,24},{24,0},{32,40},{40,48},{48,56},{56,32},{64,72... | collective-permute-start | bytes 983048 | tf_op jit(solution)/shard_map/ppermute | solution.py:50
  42.6 11.5 %collective-permute-start.8 = (s16[2,592,128]{2,1,0:T(8,128)(2,1)S(1)}, s16[2,592,128]{2,1,0:T(8,128)(2,1)S(1)}, u32[]{:S(2)}, u32[]{:S(2)}) collective-permute-start(s16[2,592,128]{2,1,0:T(8,128)(2,1)S(1)} %pad_add_fusion), channel_id=1, source_target_pairs={{1,0},{2,1},{3,2},{4,3},{5,4},{6,5},{7,6},{9,8},{10,9},{11,10},{12... | collective-permute-start | bytes 909320 | tf_op jit(solution)/shard_map/ppermute | solution.py:44
  63.9 31.4 %collective-permute-start.13 = (bf16[4,2,256,256]{3,2,1,0:T(8,128)(2,1)S(1)}, bf16[4,2,256,256]{3,2,1,0:T(8,128)(2,1)S(1)}, u32[]{:S(2)}, u32[]{:S(2)}) collective-permute-start(bf16[4,2,256,256]{3,2,1,0:T(8,128)(2,1)S(1)} %get-tuple-element.48.refs_2_), channel_id=1, source_target_pairs={{1,0},{2,1},{3,2},{4,3},{5,4},{6,5},{7,6},{9,8},{10,9},{11,10},{12... | collective-permute-start | bytes 3145736 | tf_op jit(solution)/shard_map/ppermute | solution.py:44
  65.8 29.5 %collective-permute-start.12 = (bf16[4,2,256,256]{3,2,1,0:T(8,128)(2,1)S(1)}, bf16[4,2,256,256]{3,2,1,0:T(8,128)(2,1)S(1)}, u32[]{:S(2)}, u32[]{:S(2)}) collective-permute-start(bf16[4,2,256,256]{3,2,1,0:T(8,128)(2,1)S(1)} %get-tuple-element.48.refs_2_), channel_id=1, source_target_pairs={{0,1},{1,2},{2,3},{3,4},{4,5},{5,6},{6,7},{8,9},{9,10},{10,11},{11... | collective-permute-start | bytes 3145736 | tf_op jit(solution)/shard_map/ppermute | solution.py:44
  68.2 10.6 %collective-permute-start.14 = (bf16[2,256,256]{2,1,0:T(8,128)(2,1)S(1)}, bf16[2,256,256]{2,1,0:T(8,128)(2,1)S(1)}, u32[]{:S(2)}, u32[]{:S(2)}) collective-permute-start(bf16[2,256,256]{2,1,0:T(8,128)(2,1)S(1)} %get-tuple-element.49), channel_id=1, source_target_pairs={{0,32},{8,40},{16,48},{24,56},{32,64},{40,72},{48,80},{56,88},{64,... | collective-permute-start | bytes 786440 | tf_op jit(solution)/shard_map/ppermute | solution.py:44
  72.0 10.7 %collective-permute-start.15 = (bf16[2,256,256]{2,1,0:T(8,128)(2,1)S(1)}, bf16[2,256,256]{2,1,0:T(8,128)(2,1)S(1)}, u32[]{:S(2)}, u32[]{:S(2)}) collective-permute-start(bf16[2,256,256]{2,1,0:T(8,128)(2,1)S(1)} %get-tuple-element.50), channel_id=1, source_target_pairs={{32,0},{40,8},{48,16},{56,24},{64,32},{72,40},{80,48},{88,56},{96,... | collective-permute-start | bytes 786440 | tf_op jit(solution)/shard_map/ppermute | solution.py:44
  84.7 10.5 %collective-permute-start.16 = (bf16[2,2,256,256]{3,2,1,0:T(8,128)(2,1)S(1)}, bf16[2,2,256,256]{3,2,1,0:T(8,128)(2,1)S(1)}, u32[]{:S(2)}, u32[]{:S(2)}) collective-permute-start(bf16[2,2,256,256]{3,2,1,0:T(8,128)(2,1)S(1)} %pad_maximum_fusion), channel_id=1, source_target_pairs={{0,1},{1,2},{2,3},{3,4},{4,5},{5,6},{6,7},{8,9},{9,10},{10,11},{11... | collective-permute-start | bytes 1572872 | tf_op jit(solution)/shard_map/ppermute | solution.py:44
  100.6 31.2 %collective-permute-start.22 = (bf16[4,2,256,256]{3,2,1,0:T(8,128)(2,1)S(1)}, bf16[4,2,256,256]{3,2,1,0:T(8,128)(2,1)S(1)}, u32[]{:S(2)}, u32[]{:S(2)}) collective-permute-start(bf16[4,2,256,256]{3,2,1,0:T(8,128)(2,1)S(1)} %get-tuple-element.58.refs_2_), channel_id=1, source_target_pairs={{1,0},{2,1},{3,2},{4,3},{5,4},{6,5},{7,6},{9,8},{10,9},{11,10},{12... | collective-permute-start | bytes 3145736 | tf_op jit(solution)/shard_map/ppermute | solution.py:44
  102.5 29.3 %collective-permute-start.21 = (bf16[4,2,256,256]{3,2,1,0:T(8,128)(2,1)S(1)}, bf16[4,2,256,256]{3,2,1,0:T(8,128)(2,1)S(1)}, u32[]{:S(2)}, u32[]{:S(2)}) collective-permute-start(bf16[4,2,256,256]{3,2,1,0:T(8,128)(2,1)S(1)} %get-tuple-element.58.refs_2_), channel_id=1, source_target_pairs={{0,1},{1,2},{2,3},{3,4},{4,5},{5,6},{6,7},{8,9},{9,10},{10,11},{11... | collective-permute-start | bytes 3145736 | tf_op jit(solution)/shard_map/ppermute | solution.py:44
  104.9 11.0 %collective-permute-start.23 = (bf16[2,256,256]{2,1,0:T(8,128)(2,1)S(1)}, bf16[2,256,256]{2,1,0:T(8,128)(2,1)S(1)}, u32[]{:S(2)}, u32[]{:S(2)}) collective-permute-start(bf16[2,256,256]{2,1,0:T(8,128)(2,1)S(1)} %get-tuple-element.59), channel_id=1, source_target_pairs={{0,32},{8,40},{16,48},{24,56},{32,64},{40,72},{48,80},{56,88},{64,... | collective-permute-start | bytes 786440 | tf_op jit(solution)/shard_map/ppermute | solution.py:44
  107.1 10.8 %collective-permute-start.24 = (bf16[2,256,256]{2,1,0:T(8,128)(2,1)S(1)}, bf16[2,256,256]{2,1,0:T(8,128)(2,1)S(1)}, u32[]{:S(2)}, u32[]{:S(2)}) collective-permute-start(bf16[2,256,256]{2,1,0:T(8,128)(2,1)S(1)} %get-tuple-element.60), channel_id=1, source_target_pairs={{32,0},{40,8},{48,16},{56,24},{64,32},{72,40},{80,48},{88,56},{96,... | collective-permute-start | bytes 786440 | tf_op jit(solution)/shard_map/ppermute | solution.py:44
  119.9 10.5 %collective-permute-start.25 = (bf16[2,2,256,256]{3,2,1,0:T(8,128)(2,1)S(1)}, bf16[2,2,256,256]{3,2,1,0:T(8,128)(2,1)S(1)}, u32[]{:S(2)}, u32[]{:S(2)}) collective-permute-start(bf16[2,2,256,256]{3,2,1,0:T(8,128)(2,1)S(1)} %pad_maximum_fusion.1), channel_id=1, source_target_pairs={{0,1},{1,2},{2,3},{3,4},{4,5},{5,6},{6,7},{8,9},{9,10},{10,11},{11... | collective-permute-start | bytes 1572872 | tf_op jit(solution)/shard_map/ppermute | solution.py:44
  122.3 16.4 %collective-permute-start.18 = (bf16[2,256,256]{2,1,0:T(8,128)(2,1)S(1)}, bf16[2,256,256]{2,1,0:T(8,128)(2,1)S(1)}, u32[]{:S(2)}, u32[]{:S(2)}) collective-permute-start(bf16[2,256,256]{2,1,0:T(8,128)(2,1)S(1)} %get-tuple-element.53), channel_id=1, source_target_pairs={{0,8},{8,16},{16,24},{24,0},{32,40},{40,48},{48,56},{56,32},{64,72... | collective-permute-start | bytes 786440 | tf_op jit(solution)/shard_map/ppermute | solution.py:50
  126.6 14.4 %collective-permute-start.19 = (bf16[2,256,256]{2,1,0:T(8,128)(2,1)S(1)}, bf16[2,256,256]{2,1,0:T(8,128)(2,1)S(1)}, u32[]{:S(2)}, u32[]{:S(2)}) collective-permute-start(bf16[2,256,256]{2,1,0:T(8,128)(2,1)S(1)} %get-tuple-element.54), channel_id=1, source_target_pairs={{0,16},{8,24},{16,0},{24,8},{32,48},{40,56},{48,32},{56,40},{64,80... | collective-permute-start | bytes 786440 | tf_op jit(solution)/shard_map/ppermute | solution.py:50
  130.4 10.5 %collective-permute-start.20 = (bf16[2,256,256]{2,1,0:T(8,128)(2,1)S(1)}, bf16[2,256,256]{2,1,0:T(8,128)(2,1)S(1)}, u32[]{:S(2)}, u32[]{:S(2)}) collective-permute-start(bf16[2,256,256]{2,1,0:T(8,128)(2,1)S(1)} %get-tuple-element.55), channel_id=1, source_target_pairs={{0,24},{8,0},{16,8},{24,16},{32,56},{40,32},{48,40},{56,48},{64,88... | collective-permute-start | bytes 786440 | tf_op jit(solution)/shard_map/ppermute | solution.py:50
  137.0 14.9 %collective-permute-start.27 = (bf16[2,256,256]{2,1,0:T(8,128)(2,1)S(1)}, bf16[2,256,256]{2,1,0:T(8,128)(2,1)S(1)}, u32[]{:S(2)}, u32[]{:S(2)}) collective-permute-start(bf16[2,256,256]{2,1,0:T(8,128)(2,1)S(1)} %get-tuple-element.63), channel_id=1, source_target_pairs={{0,8},{8,16},{16,24},{24,0},{32,40},{40,48},{48,56},{56,32},{64,72... | collective-permute-start | bytes 786440 | tf_op jit(solution)/shard_map/ppermute | solution.py:50
  137.7 14.2 %collective-permute-start.28 = (bf16[2,256,256]{2,1,0:T(8,128)(2,1)S(1)}, bf16[2,256,256]{2,1,0:T(8,128)(2,1)S(1)}, u32[]{:S(2)}, u32[]{:S(2)}) collective-permute-start(bf16[2,256,256]{2,1,0:T(8,128)(2,1)S(1)} %get-tuple-element.64), channel_id=1, source_target_pairs={{0,16},{8,24},{16,0},{24,8},{32,48},{40,56},{48,32},{56,40},{64,80... | collective-permute-start | bytes 786440 | tf_op jit(solution)/shard_map/ppermute | solution.py:50
  138.7 14.2 %collective-permute-start.29 = (bf16[2,256,256]{2,1,0:T(8,128)(2,1)S(1)}, bf16[2,256,256]{2,1,0:T(8,128)(2,1)S(1)}, u32[]{:S(2)}, u32[]{:S(2)}) collective-permute-start(bf16[2,256,256]{2,1,0:T(8,128)(2,1)S(1)} %get-tuple-element.65), channel_id=1, source_target_pairs={{0,24},{8,0},{16,8},{24,16},{32,56},{40,32},{48,40},{56,48},{64,88... | collective-permute-start | bytes 786440 | tf_op jit(solution)/shard_map/ppermute | solution.py:50
  (12 other events, 152.8 us)
where the time goes:
time: 157 us; the launch traced here: 155 us
  starting transfers between devices  60.9 us (39%)
  waiting for transfers between devices  57.3 us (36%)
  Pallas kernels  27.8 us (18%)
  local copies, waits for them, and re-layouts  6.18 us (4%)
  between operations  1.71 us (1%)
    ppermute x18, starting transfers between devices, moved(): lax.ppermute(array, axis, [(i, i + by) for i in range(size) if 0 <= i + b...  43.5 us
    ppermute x18, waiting for transfers between devices, moved(): lax.ppermute(array, axis, [(i, i + by) for i in range(size) if 0 <= i + b...  36.4 us
    pallas_call x11, Pallas kernels, local(): pl.pallas_call(kernel, out_shape=out_shape, in_specs=[SMEM] * len(scalars...  27.8 us
    ppermute x12, waiting for transfers between devices, ring_moved(): return lax.ppermute(array, 'gx', pairs)  20.8 us
    ppermute x12, starting transfers between devices, ring_moved(): return lax.ppermute(array, 'gx', pairs)  17.4 us
  transfers between devices with their start and end apart: 30, of which 14 were waited for; matrix products, arithmetic and copies ran while one was open for 0% of the time, Pallas kernels for 6%

commit v1 on v0

v1 whole, which is shorter than its diff:
```python
import math

import jax
import jax.numpy as jnp
from jax import lax
from jax.experimental import pallas as pl
from jax.experimental.pallas import tpu as pltpu
from jax.sharding import PartitionSpec as P

RING = 4
T = 128
KS = 8
SR = 16
HALO = RING + 2
HOMES = HALO * 3
F32 = jnp.float32
BF16 = jnp.bfloat16
I16 = jnp.int16
PHASE_UNIT = math.pi / 32768.0
HOP_MID, HOP_UNIT = 0.12, 0.04 / 32767.0
SITE_UNIT = 0.25 / 32767.0
COUPLING_UNIT = 0.3 / 32767.0
VMEM_LIMIT = 28 * 1024 * 1024


PHASE_ROWS = 4 * T
ROW_EDGE, COL_EDGE, CODE, AT = 64, 66, 68, 69
SMALL_ROWS = 80
CARGO = PHASE_ROWS + SMALL_ROWS
LAND, ANY, SRC_ROW, SRC_COL, USED = 0, 24, 48, 72, 96
IDX_ROWS = 120


def coded(values, unit):
    return jnp.clip(jnp.round(values * (1.0 / unit)), -32768.0, 32767.0).astype(jnp.int32).astype(I16)


def decoded(code):
    return code.astype(jnp.int32).astype(F32)


def moved(array, axis, by):
    size = lax.axis_size(axis)
    return lax.ppermute(array, axis, [(i, i + by) for i in range(size) if 0 <= i + by < size])


def ring_moved(array, by):
    size = lax.axis_size("gx")
    pairs = [(i, i // RING * RING + (i + by) % RING) for i in range(size)]
    return lax.ppermute(array, "gx", pairs)


def lane_iota(shape, dim):
    return lax.broadcasted_iota(jnp.int32, shape, dim)


def started(copies, sems):
    copies = [pltpu.make_async_copy(source, to, sems.at[n]) for n, (source, to) in enumerate(copies)]
    for copy in copies:
        copy.start()
    return copies


def encode_kernel(flags, coupling, phase_one, phase_two, hop_one, hop_two, *refs):
    outs, (held, first_row, bonds, sems) = refs[:RING], refs[RING:]
    hops, phases = (hop_one, hop_two), (phase_one, phase_two)
    pending = started(
        [(hops[n].at[1, 0:8, :], first_row.at[n]) for n in range(2)]
        + [(hops[n].at[2], bonds.at[n]) for n in range(2)]
        + [(phases[n].at[(flags[0, 0] + d) % RING], held.at[d, n]) for d in range(RING) for n in range(2)],
        sems,
    )
    for copy in pending[:4]:
        copy.wait()
    live = flags[0, 8]
    lane = lane_iota((1, T), 1)
    code = jnp.zeros((1, T), jnp.int32)
    at = jnp.zeros((1, T), jnp.int32)
    for k in range(KS):
        owner, target = flags[0, 10 + k], flags[0, 10 + KS + k]
        strip = (owner // flags[0, 9] - flags[0, 5] + 1) * 4 + owner % flags[0, 9] - flags[0, 6] + 1
        here = (lane == k) & (k < live)
        code = jnp.where(here, strip + 16, code)
        at = jnp.where(here, target, at)
    weights = jnp.where(lane_iota((32, 256), 1) // 32 < live, coupling[...].T, 0.0)
    weights = coded(weights, COUPLING_UNIT)
    edges = [first_row[n, 0:1, :] for n in range(2)] + [bonds[n].T[0:1, :] for n in range(2)]
    edges = coded(jnp.concatenate(edges + [jnp.zeros((12, T), F32)], 0) - HOP_MID, HOP_UNIT).astype(jnp.int32)
    row = lane_iota((16, T), 0)
    words = jnp.where(row == CODE - 64, code, jnp.where(row == AT - 64, at, jnp.where(row < 4, edges, 0)))
    for d, out in enumerate(outs):
        for layer in range(2):
            pending[4 + d * 2 + layer].wait()
            for a in range(2):
                to = (layer * 2 + a) * T
                out[to : to + T, :] = coded(held[d, layer, a], PHASE_UNIT)
        out[PHASE_ROWS : PHASE_ROWS + 32, :] = weights[:, :T]
        out[PHASE_ROWS + 32 : PHASE_ROWS + 64, :] = weights[:, T:]
        out[PHASE_ROWS + 64 :, :] = words.astype(I16)


def pack_kernel(hop_one, hop_two, onsite_one, onsite_two, out, held, sems):
    fields = ((hop_one, onsite_one), (hop_two, onsite_two))
    pending = started(
        [
            (hop.at[n] if n < 3 else site.at[n - 3], held.at[layer, n])
            for layer, (hop, site) in enumerate(fields)
            for n in range(5)
        ],
        sems,
    )
    for layer in range(2):
        for n in range(5):
            at = layer * 5 + n
            pending[at].wait()
            value = held[layer, n]
            value = coded(value - HOP_MID, HOP_UNIT) if n < 3 else coded(value, SITE_UNIT)
            out[at * T : (at + 1) * T, :] = value


def region_kernel(flags, part0, part1, part2, part3, region, *edge_blocks):
    z = flags[0, 0]
    for d, part in enumerate((part0, part1, part2, part3)):
        region[(z + RING - d) % RING] = part[...]
    for slot in range(2):
        edge_blocks[slot][...] = region[edge_row(flags, slot) // (HALO - 1) * (RING - 1)]


def operators_kernel(flags, part0, part1, part2, part3, ops):
    z = flags[0, 0]
    for d, part in enumerate((part0, part1, part2, part3)):
        at = pl.ds(pl.multiple_of((z + RING - d) % RING * T, T), T)
        for layer in range(2):
            for n in range(5):
                base = (layer * 5 + n) * T
                raw = decoded(part[base : base + T, :])
                ops[layer, n, at, :] = raw * HOP_UNIT + HOP_MID if n < 3 else raw * SITE_UNIT


OWN, CROSS, NEAR = 0, 1, 2


def neighbourhood(own, ends, cross, cross_ends, near, near_ends):
    def block(row, side):
        if row in SLOTS:
            return (ends, cross_ends, near_ends)[side].at[SLOTS.index(row)]
        return (own, cross, near)[side].at[row - 1]

    return block


SLOTS = ("A", "B")
ROWS = (1, 2, 3, 4) + SLOTS


def edge_row(flags, slot):
    return flags[0, 7] if slot == 0 else HALO - 1 - flags[0, 7]


def row_of(flags, row):
    return edge_row(flags, SLOTS.index(row)) if row in SLOTS else row


def rows_of(rb):
    if isinstance(rb, int):
        return slice(rb * T, (rb + 1) * T)
    return pl.ds(pl.multiple_of(rb * T, T), T)


def column_of(flags, side):
    return 1 if side == OWN else flags[0, 3] if side == CROSS else 2 - flags[0, 3]


def build_kernel(flags, *refs):
    ops_in, idx, bd1, bd2, ops, codes = refs[6:]
    block = neighbourhood(*refs[:6])
    rows, cols = lane_iota((32, 256), 0), lane_iota((32, 256), 1)
    place = ((rows // 16 == cols // 128) & (rows % 16 == cols % 16)).astype(BF16)
    i, j = lane_iota((256, 256), 0), lane_iota((256, 256), 1)
    mask1 = (i // 32) == ((j // 16) % 8)
    mask2 = ((i // 16) % 8) == (j // 32)
    first = (((0,), (0,)), ((), ()))

    def spread(a, b, mask):
        full = lax.dot_general(a, b, first, preferred_element_type=F32)
        return jnp.where(mask, full, 0.0).astype(BF16)

    codes[...] = jnp.zeros_like(codes)
    for side in (OWN, CROSS, NEAR):
        for row in ROWS:
            home = row_of(flags, row) * 3 + column_of(flags, side)
            ref = block(row, side)
            c = jnp.concatenate([decoded(ref[PHASE_ROWS + n : PHASE_ROWS + n + 32, :]) for n in (0, 32)], 1)
            c = c * COUPLING_UNIT
            high = c.astype(BF16)
            low = (c - high.astype(F32)).astype(BF16)
            bd1[home, 0:256, :] = spread(high, place, mask1)
            bd1[home, 256:512, :] = spread(low, place, mask1)
            if side == OWN and row not in SLOTS:
                bd2[row - 1, 0:256, :] = spread(place, high, mask2)
                bd2[row - 1, 256:512, :] = spread(place, low, mask2)
            words = ref[PHASE_ROWS + 64 : PHASE_ROWS + 80, :].astype(jnp.int32)
            codes[0, pl.ds(home, 1), :] = words[CODE - 64 : CODE - 63, :]
            codes[1, pl.ds(home, 1), :] = words[AT - 64 : AT - 63, :]

    code, at = codes[0], codes[1]
    home = lane_iota((24, T), 0)
    active = code >= 16
    rb = home // 3 + jnp.where(active, ((code >> 2) & 3) - 1, 0)
    cb = home % 3 + jnp.where(active, (code & 3) - 1, 0)
    lands = active & (cb == 1) & (rb >= 1) & (rb <= RING)
    idx[LAND : LAND + 24, :] = jnp.where(lands, (rb - 1) * T + at, -1)
    some = jnp.max(jnp.where(lands, 1.0, 0.0), axis=1, keepdims=True)
    idx[ANY : ANY + 24, :] = jnp.broadcast_to(some, (24, T)).astype(jnp.int32)
    idx[SRC_ROW : SRC_ROW + 24, :] = jnp.clip(rb * T + at, 0, HALO * T - SR)
    idx[SRC_COL : SRC_COL + 24, :] = jnp.clip(cb, 0, 2)
    mine = active & (home % 3 == 1) & (home // 3 >= 1) & (home // 3 <= RING)
    source = jnp.where(mine, rb * 3 + cb, -1)
    idx[USED : USED + 24, :] = jnp.zeros((24, T), jnp.int32)
    for n in range(HOMES):
        hit = jnp.where(source == n, 1.0, 0.0)
        used = jnp.max(jnp.max(hit, axis=1, keepdims=True), axis=0, keepdims=True)
        idx[USED + n : USED + n + 1, :] = jnp.broadcast_to(used, (1, T)).astype(jnp.int32)

    ops[:, 0:5] = ops_in[...]
    lane = lane_iota((T, T), 1)

    def edge(ref, row):
        words = decoded(ref[PHASE_ROWS + 64 : PHASE_ROWS + 80, :])
        return words[row - 64 : row - 63, :] * HOP_UNIT + HOP_MID

    for layer in range(2):
        ops[layer, 5, 0 : RING * T - 1, :] = ops_in[layer, 1, 1 : RING * T, :]
        below = [edge(block(slot, OWN), ROW_EDGE + layer) for slot in SLOTS]
        ops[layer, 5, RING * T - 1 : RING * T, :] = jnp.where(
            jnp.broadcast_to(flags[0, 7], (1, T)) == HALO - 1, below[0], below[1]
        )
        for r in range(RING):
            rows = slice(r * T, (r + 1) * T)
            far, close = [edge(block(r + 1, side), COL_EDGE + layer) for side in (CROSS, NEAR)]
            right = jnp.where(jnp.broadcast_to(flags[0, 3], (1, T)) == 2, far, close)
            column = jnp.broadcast_to(right, (T, T)).T
            ops[layer, 6, rows, :] = jnp.where(lane == T - 1, column, pltpu.roll(ops_in[layer, 2, rows, :], T - 1, 1))


def cos_sin(code):
    q = code.astype(jnp.int32)
    quarter = (q + 8192) >> 14
    r = (q - (quarter << 14)).astype(F32) * PHASE_UNIT
    r2 = r * r
    s = r * (1.0 + r2 * (-1.6666654611e-1 + r2 * (8.3321608736e-3 + r2 * -1.9515295891e-4)))
    c = 1.0 + r2 * (-0.5 + r2 * (4.166664568298827e-2 + r2 * (-1.388731625493765e-3 + r2 * 2.443315711809948e-5)))
    odd = (quarter & 1) == 1
    cos_v = jnp.where(odd, s, c)
    sin_v = jnp.where(odd, c, s)
    cos_v = jnp.where(((quarter + 1) & 2) == 2, -cos_v, cos_v)
    sin_v = jnp.where((quarter & 2) == 2, -sin_v, sin_v)
    return cos_v, sin_v


def zero_kernel(region, zero_out, narrow_out):
    for rb in range(RING):
        rows = slice(rb * T, (rb + 1) * T)
        for layer in range(2):
            for a in range(2):
                at = (layer * 2 + a) * T
                pair = cos_sin(region[rb, at : at + T, :])
                for p in range(2):
                    zero_out[layer, a, p, rows, :] = pair[p]
                    narrow_out[rb, layer, a * T : (a + 1) * T, p * T : (p + 1) * T] = pair[p].astype(BF16)


def step_kernel(first, last, *refs):
    refs = list(refs)
    around = neighbourhood(*refs[2:8])
    flags, idx, bd1, bd2, ops = refs[:2] + refs[8:11]
    refs = refs[11:]
    prev = None if first else refs.pop(0)
    wide_out = refs.pop(0) if first else None
    if last:
        parts = refs[:RING]
        refs = refs[RING:]
        narrow_out = refs.pop()
    else:
        narrow_out, *edge_blocks = refs[:3]
        refs = refs[3:]
        parts = []
        if not first:
            parts = refs[:RING]
            refs = refs[RING:]
    fu, fv, fvs, gathered, terms, acc1, acc2 = refs[:7]
    xv = refs[7] if first else None

    def halves(p):
        return slice(p * T, (p + 1) * T)

    def decode(layer, row, side, a, edge):
        at = pl.multiple_of((layer * 2 + a) * T, T)
        pair = cos_sin(around(row, side)[pl.ds(at, T), :])
        if side == OWN:
            factor = flags[0, 1 + SLOTS.index(row)].astype(F32)
        else:
            factor = flags[0, 4].astype(F32) if side == CROSS else 1.0
        rb, cb = row_of(flags, row), column_of(flags, side)
        for p in range(2):
            value = (pair[p] * factor).astype(BF16)
            if layer == 0:
                fu[cb, a, p, rows_of(rb), :] = value.astype(F32)
                continue
            xv[rb * 3 + cb, pl.ds(pl.multiple_of(a * T, T), T), halves(p)] = value
            if side == OWN:
                fv[a, p, rows_of(rb), :] = value.astype(F32)
            elif edge:
                fvs[cb // 2, p, rows_of(rb - 1), :] = value.astype(F32)

    def widen(layer, row, side, a, edge):
        ref = around(row, side).at[layer]
        at = pl.ds(pl.multiple_of(a * T, T), T)
        rb, cb = row_of(flags, row), column_of(flags, side)
        for p in range(2):
            value = ref[at, halves(p)].astype(F32)
            if layer == 0:
                fu[cb, a, p, rows_of(rb), :] = value
            elif side == OWN:
                fv[a, p, rows_of(rb), :] = value
            elif edge:
                fvs[cb // 2, p, rows_of(rb - 1), :] = value

    for side, row in [(side, row) for side in (OWN, CROSS, NEAR) for row in ROWS]:
        cb = column_of(flags, side)
        for layer in range(2):
            if side == OWN and row not in SLOTS:
                for a in range(2):
                    widen(layer, row, side, a, False)
                continue
            edge = None
            if side == OWN:
                edge = 1 - row_of(flags, row) // (HALO - 1)
            elif row not in SLOTS:
                edge = 1 - cb // 2
            load = decode if first else widen
            if edge is not None:
                load(layer, row, side, edge, True)
            if layer == 1 and not first:
                continue

            @pl.when(idx[(USED if layer == 0 else ANY) + row_of(flags, row) * 3 + cb, 0] > 0)
            def _():
                for a in range(2) if edge is None else (1 - edge,):
                    load(layer, row, side, a, False)

    for r in range(RING):
        home = (r + 1) * 3 + 1
        for k in range(KS):
            row = idx[SRC_ROW + home, k]
            col = idx[SRC_COL + home, k]
            for a in range(2):
                for p in range(2):
                    piece = fu[col, a, p, pl.ds(row, SR), :].astype(BF16)
                    gathered[k * 32 + a * SR : k * 32 + (a + 1) * SR, p * T : (p + 1) * T] = piece
        both = jnp.dot(bd2[r], gathered[...], preferred_element_type=F32)
        summed = both[:256] + both[256:]
        for b in range(2):
            for p in range(2):
                acc2[b, p, r * T : (r + 1) * T, :] = summed[b * T : (b + 1) * T, p * T : (p + 1) * T]

    acc1[...] = jnp.zeros_like(acc1)
    for side, row in [(side, row) for side in (OWN, CROSS, NEAR) for row in ROWS]:
        home = row_of(flags, row) * 3 + column_of(flags, side)

        @pl.when(idx[ANY + home, 0] > 0)
        def _():
            decoded_here = first and (side != OWN or row in SLOTS)
            source = xv[home] if decoded_here else around(row, side)[1]
            both = jnp.dot(bd1[home], source, preferred_element_type=F32)
            terms[...] = both[:256] + both[256:]
            for k in range(KS):
                landing = idx[LAND + home, k]

                @pl.when(landing >= 0)
                def _():
                    for a in range(2):
                        for p in range(2):
                            at = (a, p, pl.ds(landing, SR), slice(None))
                            acc1[at] = acc1[at] + terms[
                                k * 32 + a * SR : k * 32 + (a + 1) * SR, p * T : (p + 1) * T
                            ]

    lane = lane_iota((T, T), 1)
    for layer in range(2):
        acc = (acc1, acc2)[layer]

        def field(a, p, low):
            if layer == 0:
                return fu[1, a, p, low : low + T, :]
            return fv[a, p, low : low + T, :]

        def beside(a, p, r, cb):
            if layer == 0:
                return fu[cb, a, p, (r + 1) * T : (r + 2) * T, :]
            return fvs[cb // 2, p, r * T : (r + 1) * T, :]

        for r in range(RING):
            rows = slice(r * T, (r + 1) * T)
            h0, h1, h2, e0, e1, h1s, h2s = [ops[layer, n, rows, :] for n in range(7)]
            for p in range(2):
                base = (r + 1) * T
                w0, w1 = field(0, p, base), field(1, p, base)
                before = jnp.where(lane == 0, pltpu.roll(beside(1, p, r, 0), 1, 1), pltpu.roll(w1, 1, 1))
                after = jnp.where(
                    lane == T - 1, pltpu.roll(beside(0, p, r, 2), T - 1, 1), pltpu.roll(w0, T - 1, 1)
                )
                upper = e0 * w0 + h0 * w1 + h1 * field(1, p, base - 1) + h2 * before + acc[0, p, rows, :]
                lower = e1 * w1 + h0 * w0 + h1s * field(0, p, base + 1) + h2s * after + acc[1, p, rows, :]
                for a, value in enumerate((upper, lower)):
                    if first:
                        wide_out[layer, a, p, rows, :] = value
                    else:
                        value = 2.0 * value - prev[layer, a, p, rows, :]
                    narrow_out[r, layer, a * T : (a + 1) * T, p * T : (p + 1) * T] = value.astype(BF16)

    if not last:
        for slot in range(2):
            edge_blocks[slot][...] = narrow_out[edge_row(flags, slot) // (HALO - 1) * (RING - 1)]
    for d, part in enumerate(parts):
        part[...] = narrow_out[(flags[0, 0] + d) % RING]


def result_kernel(shifts, flags, *refs):
    parts, refs = refs[: len(shifts)], refs[len(shifts) :]
    if shifts[0]:
        refs = refs[2:]
    outs, (held, sems) = refs[:2], refs[2:]
    pending = []
    for n, (d, part) in enumerate(zip(shifts, parts)):
        state = (flags[0, 0] + RING - d) % RING
        for layer, out in enumerate(outs):
            for p in range(2):
                for a in range(2):
                    value = part[layer, a * T : (a + 1) * T, p * T : (p + 1) * T]
                    held[n, layer, p, a] = value.astype(F32)
            copy = pltpu.make_async_copy(held.at[n, layer], out.at[state], sems.at[n * 2 + layer])
            copy.start()
            pending.append(copy)
    for copy in pending:
        copy.wait()


HBM = pl.BlockSpec(memory_space=pltpu.HBM)
SMEM = pl.BlockSpec(memory_space=pltpu.SMEM)
VMEM = pl.BlockSpec(memory_space=pltpu.VMEM)
PARAMS = pltpu.CompilerParams(vmem_limit_bytes=VMEM_LIMIT)
WIDE = jax.ShapeDtypeStruct((2, 2, 2, RING * T, T), F32)
NARROW = jax.ShapeDtypeStruct((RING, 2, 2 * T, 2 * T), BF16)
BLOCK = jax.ShapeDtypeStruct((2, 2 * T, 2 * T), BF16)


def local(kernel, out_shape, scalars, *operands, far=(), scratch=()):
    return pl.pallas_call(
        kernel,
        out_shape=out_shape,
        in_specs=[SMEM] * len(scalars) + [VMEM] * len(operands) + [HBM] * len(far),
        out_specs=jax.tree.map(lambda _: VMEM, out_shape),
        scratch_shapes=list(scratch),
        compiler_params=PARAMS,
    )(*scalars, *operands, *(pltpu.with_memory_space_constraint(x, pltpu.HBM) for x in far))


def step(first, last, flags, idx, halo, bd1, bd2, ops, prev=None):
    scratch = [
        pltpu.VMEM((3, 2, 2, HALO * T, T), F32),
        pltpu.VMEM((2, 2, HALO * T, T), F32),
        pltpu.VMEM((2, 2, RING * T, T), F32),
        pltpu.VMEM((2 * T, 2 * T), BF16),
        pltpu.VMEM((2 * T, 2 * T), F32),
        pltpu.VMEM((2, 2, RING * T, T), F32),
        pltpu.VMEM((2, 2, RING * T, T), F32),
    ]
    if first:
        scratch.append(pltpu.VMEM((HOMES, 2 * T, 2 * T), BF16))
        out = (WIDE, NARROW, BLOCK, BLOCK)
    elif last:
        scratch.append(pltpu.VMEM(NARROW.shape, BF16))
        out = (BLOCK,) * RING
    else:
        out = (NARROW, BLOCK, BLOCK) + (BLOCK,) * RING
    operands = [*halo, bd1, bd2, ops] + ([] if first else [prev])
    return local(lambda *refs: step_kernel(first, last, *refs), out, (flags, idx), *operands, scratch=scratch)


def across(array, low):
    size = lax.axis_size("gy")
    pairs = [(i, i + 1) for i in range(low, size - 1, 2)]
    return lax.ppermute(array, "gy", pairs + [(j, i) for i, j in pairs])


def swapped_rows(array, low):
    size = lax.axis_size("gx")
    pairs = [(i, i + RING) for i in range(size - RING) if i // RING % 2 == low]
    return lax.ppermute(array, "gx", pairs + [(j, i) for i, j in pairs])


def halo_of(region, block_a, block_b):
    cross, near = across(region, 1), across(region, 0)
    ends = jnp.stack([swapped_rows(block_a, 0), swapped_rows(block_b, 1)])
    return (region, ends, cross, across(ends, 1), near, across(ends, 0))


def ring_exchanged(parts):
    return [parts[0]] + [ring_moved(parts[d], d) for d in range(1, RING)]


def written(flags, shifts, parts, before=()):
    count = len(shifts)
    return pl.pallas_call(
        lambda *refs: result_kernel(shifts, *refs),
        out_shape=(jax.ShapeDtypeStruct((RING, 2, 2, T, T), F32),) * 2,
        in_specs=[SMEM] + [VMEM] * count + [HBM] * len(before),
        out_specs=(HBM, HBM),
        scratch_shapes=[pltpu.VMEM((count, 2, 2, 2, T, T), F32), pltpu.SemaphoreType.DMA((2 * count,))],
        input_output_aliases={1 + count + n: n for n in range(len(before))},
        compiler_params=PARAMS,
    )(flags, *parts, *before)


def results(flags, parts):
    own = written(flags, (0,), parts[:1])
    return written(flags, (1, 2, 3), parts[1:], own)


def body(phase_one, phase_two, hop_one, hop_two, onsite_one, onsite_two, coupling, owner, target_row, live_strips):
    grid_row, grid_col = lax.axis_index("gx"), lax.axis_index("gy")
    rows_n, cols_n = lax.axis_size("gx"), lax.axis_size("gy")
    odd, ring = grid_col % 2, grid_row // RING
    crossing = jnp.where(odd == 1, grid_col < cols_n - 1, grid_col > 0)
    second = jnp.where(ring % 2 == 1, ring < rows_n // RING - 1, ring > 0)
    first_row = jnp.where(ring % 2 == 1, 0, HALO - 1)
    flags = [grid_row % RING, ring // 2 * 2 + 1 < rows_n // RING, second, 2 * odd, crossing, grid_row, grid_col]
    flags += [first_row, live_strips[0, 0], cols_n]
    flags = [jnp.asarray(f).astype(jnp.int32).reshape(1) for f in flags]
    flags = jnp.concatenate(flags + [owner[0, 0], target_row[0, 0]]).reshape(1, 10 + 2 * KS)

    cargo = jax.ShapeDtypeStruct((CARGO, T), I16)
    sends = local(
        encode_kernel,
        (cargo,) * RING,
        (flags,),
        coupling.reshape(2 * KS * SR, 2 * SR),
        far=(phase_one, phase_two, hop_one, hop_two),
        scratch=[
            pltpu.VMEM((RING, 2, 2, T, T), F32),
            pltpu.VMEM((2, 8, T), F32),
            pltpu.VMEM((2, T, T), F32),
            pltpu.SemaphoreType.DMA((4 + 2 * RING,)),
        ],
    )
    parts = ring_exchanged(sends)
    packed = local(
        pack_kernel,
        jax.ShapeDtypeStruct((10 * T, T), I16),
        (),
        far=(hop_one, hop_two, onsite_one, onsite_two),
        scratch=[pltpu.VMEM((2, 5, T, T), F32), pltpu.SemaphoreType.DMA((10,))],
    )
    parts, packed = lax.optimization_barrier((parts, packed))
    packs = ring_exchanged([packed] * RING)

    region = local(
        region_kernel, (jax.ShapeDtypeStruct((RING, CARGO, T), I16), cargo, cargo), (flags,), *parts
    )
    halo = halo_of(*region)
    zero, zero_narrow = local(zero_kernel, (WIDE, NARROW), (), region[0])
    ops = local(operators_kernel, jax.ShapeDtypeStruct((2, 5, RING * T, T), F32), (flags,), *packs)
    idx, bd1, bd2, ops = local(
        build_kernel,
        (
            jax.ShapeDtypeStruct((IDX_ROWS, T), jnp.int32),
            jax.ShapeDtypeStruct((HOMES, 512, 256), BF16),
            jax.ShapeDtypeStruct((RING, 512, 256), BF16),
            jax.ShapeDtypeStruct((2, 7, RING * T, T), F32),
        ),
        (flags,),
        *halo,
        ops,
        scratch=[pltpu.VMEM((2, 24, T), jnp.int32)],
    )

    one, *one_blocks = step(True, False, flags, idx, (zero_narrow, *halo[1:]), bd1, bd2, ops)
    *two_blocks, part0, part1, part2, part3 = step(
        False, False, flags, idx, halo_of(*one_blocks), bd1, bd2, ops, zero
    )
    got1, got3 = ring_moved(part1, 1), ring_moved(part3, 3)
    halo, got1, got3, part2 = lax.optimization_barrier((halo_of(*two_blocks), got1, got3, part2))
    got2 = ring_moved(part2, 2)
    three_parts = step(False, True, flags, idx, halo, bd1, bd2, ops, one)
    three_parts, got2 = lax.optimization_barrier((three_parts, got2))
    two_a, two_b = results(flags, (part0, got1, got2, got3))
    three_a, three_b = results(flags, ring_exchanged(three_parts))
    return two_a, two_b, three_a, three_b


def solution(mesh):
    field = P(None, None, "gx", "gy")
    site = P(None, "gx", "gy")
    out = P(None, None, None, "gx", "gy")
    return jax.shard_map(
        body,
        mesh=mesh,
        in_specs=(
            field,
            field,
            site,
            site,
            site,
            site,
            P("gx", "gy", None, None, None, None, None),
            P("gx", "gy", None),
            P("gx", "gy", None),
            P("gx", "gy"),
        ),
        out_specs=(out, out, out, out),
        check_vma=False,
    )
```

time: 157 us -> 138 us (0.88); the launches traced: 155 us -> 138 us
  starting transfers between devices: 60.9 us -> 45.5 us
  Pallas kernels: 27.8 us -> 34.1 us
  local copies, waits for them, and re-layouts: 6.18 us -> 1.89 us
  waiting for transfers between devices: 57.3 us -> 54.2 us
    ppermute x18, starting transfers between devices: 43.5 us -> 27.6 us  [the longest x6 13.9 us: swapped_rows(): return lax.ppermute(array, 'gx', pairs + [(j, i) for i, j in pairs])]
    ppermute x18, waiting for transfers between devices: 36.4 us -> 26.9 us  [the longest x6 18.3 us: swapped_rows(): return lax.ppermute(array, 'gx', pairs + [(j, i) for i, j in pairs])]
    ppermute x12, waiting for transfers between devices: 20.8 us -> 27.3 us  [ring_moved(): return lax.ppermute(array, 'gx', pairs)]
    pallas_call x0 -> x4, Pallas kernels: none -> 6.22 us  [written(): pl.pallas_call(lambda *refs: result_kernel(shifts, *refs), out_shape=(jax...]
    unnamed x13 -> x0, local copies, waits for them, and re-layouts: 3.07 us -> none
    slice x2 -> x0, local copies, waits for them, and re-layouts: 1.98 us -> none  [the longest x1 1.03 us: body(): hop_one[2, :, 0]]
    pallas_call x11 -> x9, Pallas kernels: 27.8 us -> 27.9 us  [local(): pl.pallas_call(kernel, out_shape=out_shape, in_specs=[SMEM] * len(scalars...]
  transfers between devices with their start and end apart: 30 -> 30, of which waited for: 14 -> 16; matrix products, arithmetic and copies ran while one was open for 0% -> 0% of each run, Pallas kernels for 6% -> 10%
where the time goes in v1:
time: 138 us
  waiting for transfers between devices  54.2 us (39%)
  starting transfers between devices  45.5 us (33%)
  Pallas kernels  34.1 us (25%)
  local copies, waits for them, and re-layouts  1.89 us (1%)
  between operations  1.83 us (1%)
    pallas_call x9, Pallas kernels, local(): pl.pallas_call(kernel, out_shape=out_shape, in_specs=[SMEM] * len(scalars...  27.9 us
    ppermute x12, waiting for transfers between devices, ring_moved(): return lax.ppermute(array, 'gx', pairs)  27.3 us
    ppermute x6, waiting for transfers between devices, swapped_rows(): return lax.ppermute(array, 'gx', pairs + [(j, i) for i, j in pairs])  18.3 us
    ppermute x12, starting transfers between devices, ring_moved(): return lax.ppermute(array, 'gx', pairs)  17.9 us
    ppermute x6, starting transfers between devices, swapped_rows(): return lax.ppermute(array, 'gx', pairs + [(j, i) for i, j in pairs])  13.9 us
    ppermute x12, starting transfers between devices, across(): return lax.ppermute(array, 'gy', pairs + [(j, i) for i, j in pairs])  13.8 us
    ppermute x12, waiting for transfers between devices, across(): return lax.ppermute(array, 'gy', pairs + [(j, i) for i, j in pairs])  8.59 us
    pallas_call x4, Pallas kernels, written(): pl.pallas_call(lambda *refs: result_kernel(shifts, *refs), out_shape=(jax...  6.22 us
  transfers between devices with their start and end apart: 30, of which 16 were waited for; matrix products, arithmetic and copies ran while one was open for 0% of the time, Pallas kernels for 10%

profile of v1, /device:TPU:10, one launch (start us, length us, event | category | flops | bytes accessed | tf_op | source)
XLA Modules:
  0.0 137.7 jit_solution(17802619549520029674)
XLA Ops:
  7.3 3.6 %collective-permute-start.1 = (s16[592,128]{1,0:T(8,128)(2,1)S(1)}, s16[592,128]{1,0:T(8,128)(2,1)S(1)}, u32[]{:S(2)}, u32[]{:S(2)}) collective-permute-start(s16[592,128]{1,0:T(8,128)(2,1)S(1)} %get-tuple-element.61), channel_id=1, source_target_pairs={{0,16},{8,24},{16,0},{24,8},{32,48},{40,56},{48,32},{56,40},{64,80... | collective-permute-start | bytes 454664 | tf_op jit(solution)/shard_map/ppermute | solution.py:50
  13.3 4.4 %collective-permute-done.1.part2 = s16[592,128]{1,0:T(8,128)(2,1)S(1)} collective-permute-done((s16[592,128]{1,0:T(8,128)(2,1)S(1)}, s16[592,128]{1,0:T(8,128)(2,1)S(1)}, u32[]{:S(2)}, u32[]{:S(2)}) %collective-permute-start.1) | collective-permute-done | bytes 151584 | tf_op jit(solution)/shard_map/ppermute | solution.py:50
  18.9 2.2 %collective-permute-start.11 = (s16[1280,128]{1,0:T(8,128)(2,1)S(1)}, s16[1280,128]{1,0:T(8,128)(2,1)S(1)}, u32[]{:S(2)}, u32[]{:S(2)}) collective-permute-start(s16[1280,128]{1,0:T(8,128)(2,1)S(1)} %shard_map.130.part0), channel_id=1, source_target_pairs={{0,24},{8,0},{16,8},{24,16},{32,56},{40,32},{48,40},{56,48},{64,88... | collective-permute-start | bytes 983048 | tf_op jit(solution)/shard_map/ppermute | solution.py:50
  22.2 2.5 %collective-permute-start.5 = (s16[4,592,128]{2,1,0:T(8,128)(2,1)S(1)}, s16[4,592,128]{2,1,0:T(8,128)(2,1)S(1)}, u32[]{:S(2)}, u32[]{:S(2)}) collective-permute-start(s16[4,592,128]{2,1,0:T(8,128)(2,1)S(1)} %get-tuple-element.67.refs_0_.region), channel_id=1, source_target_pairs={{1,2},{3,4},{5,6},{2,1},{4,3},{6,5},{9,10},{11,12},{13,14},{10,9},... | collective-permute-start | bytes 1818632 | tf_op jit(solution)/shard_map/ppermute | solution.py:494
  24.8 4.3 %collective-permute-start.4 = (s16[592,128]{1,0:T(8,128)(2,1)S(1)}, s16[592,128]{1,0:T(8,128)(2,1)S(1)}, u32[]{:S(2)}, u32[]{:S(2)}) collective-permute-start(s16[592,128]{1,0:T(8,128)(2,1)S(1)} %get-tuple-element.69), channel_id=1, source_target_pairs={{32,64},{40,72},{48,80},{56,88},{64,32},{72,40},{80,48},{88,56},{3... | collective-permute-start | bytes 454664 | tf_op jit(solution)/shard_map/ppermute | solution.py:500
  29.1 4.5 %collective-permute-done.4 = s16[592,128]{1,0:T(8,128)(2,1)S(1)} collective-permute-done((s16[592,128]{1,0:T(8,128)(2,1)S(1)}, s16[592,128]{1,0:T(8,128)(2,1)S(1)}, u32[]{:S(2)}, u32[]{:S(2)}) %collective-permute-start.4) | collective-permute-done | bytes 151584 | tf_op jit(solution)/shard_map/ppermute | solution.py:500
  34.5 2.5 %collective-permute-start.6 = (s16[2,592,128]{2,1,0:T(8,128)(2,1)S(1)}, s16[2,592,128]{2,1,0:T(8,128)(2,1)S(1)}, u32[]{:S(2)}, u32[]{:S(2)}) collective-permute-start(s16[2,592,128]{2,1,0:T(8,128)(2,1)S(1)} %pad_add_fusion.refs_1_.refs_3_), channel_id=1, source_target_pairs={{1,2},{3,4},{5,6},{2,1},{4,3},{6,5},{9,10},{11,12},{13,14},{10,9},... | collective-permute-start | bytes 909320 | tf_op jit(solution)/shard_map/ppermute | solution.py:494
  38.4 6.2 %collective-permute-done.9.part1 = s16[1280,128]{1,0:T(8,128)(2,1)S(1)} collective-permute-done((s16[1280,128]{1,0:T(8,128)(2,1)S(1)}, s16[1280,128]{1,0:T(8,128)(2,1)S(1)}, u32[]{:S(2)}, u32[]{:S(2)}) %collective-permute-start.9) | collective-permute-done | bytes 327712 | tf_op jit(solution)/shard_map/ppermute | solution.py:50
  45.4 2.4 %shard_map.133 = (s32[120,128]{1,0:T(8,128)S(1)}, bf16[18,512,256]{2,1,0:T(8,128)(2,1)S(1)}, bf16[4,512,256]{2,1,0:T(8,128)(2,1)S(1)}, f32[2,7,512,128]{3,2,1,0:T(8,128)S(1)}) custom-call(s32[1,26]{1,0:T(1,128)S(1)} %bitcast.22, s16[4,592,128]{2,1,0:T(8,128)(2,1)S(1)} %get-tuple-element.67.refs_0_.region, ...), custom_call_target="tpu_custom_call" | custom-call | tf_op jit(solution)/shard_map/pallas_call | solution.py:459
  47.9 8.2 %shard_map.135 = (f32[2,2,2,512,128]{4,3,2,1,0:T(8,128)S(1)}, bf16[4,2,256,256]{3,2,1,0:T(8,128)(2,1)S(1)}, bf16[2,256,256]{2,1,0:T(8,128)(2,1)S(1)}, bf16[2,256,256]{2,1,0:T(8,128)(2,1)S(1)}) custom-call(s32[1,26]{1,0:T(1,128)S(1)} %bitcast.23, s32[120,128]{1,0:T(8,128)S(1)} %get-tuple-element.71.refs_1_, ...), custom_call_target="tpu_custom_call" | custom-call | tf_op jit(solution)/shard_map/pallas_call | solution.py:459
  58.2 4.5 %collective-permute-start.13 = (bf16[2,256,256]{2,1,0:T(8,128)(2,1)S(1)}, bf16[2,256,256]{2,1,0:T(8,128)(2,1)S(1)}, u32[]{:S(2)}, u32[]{:S(2)}) collective-permute-start(bf16[2,256,256]{2,1,0:T(8,128)(2,1)S(1)} %get-tuple-element.78), channel_id=1, source_target_pairs={{32,64},{40,72},{48,80},{56,88},{64,32},{72,40},{80,48},{88,56},{3... | collective-permute-start | bytes 786440 | tf_op jit(solution)/shard_map/ppermute | solution.py:500
  62.7 3.9 %collective-permute-done.12 = bf16[2,256,256]{2,1,0:T(8,128)(2,1)S(1)} collective-permute-done((bf16[2,256,256]{2,1,0:T(8,128)(2,1)S(1)}, bf16[2,256,256]{2,1,0:T(8,128)(2,1)S(1)}, u32[]{:S(2)}, u32[]{:S(2)}) %collective-permute-start.12) | collective-permute-done | bytes 262176 | tf_op jit(solution)/shard_map/ppermute | solution.py:500
  66.6 2.8 %collective-permute-done.13 = bf16[2,256,256]{2,1,0:T(8,128)(2,1)S(1)} collective-permute-done((bf16[2,256,256]{2,1,0:T(8,128)(2,1)S(1)}, bf16[2,256,256]{2,1,0:T(8,128)(2,1)S(1)}, u32[]{:S(2)}, u32[]{:S(2)}) %collective-permute-start.13) | collective-permute-done | bytes 262176 | tf_op jit(solution)/shard_map/ppermute | solution.py:500
  72.0 8.6 %collective-permute-done.15.refs_5_ = bf16[2,2,256,256]{3,2,1,0:T(8,128)(2,1)S(1)} collective-permute-done((bf16[2,2,256,256]{3,2,1,0:T(8,128)(2,1)S(1)}, bf16[2,2,256,256]{3,2,1,0:T(8,128)(2,1)S(1)}, u32[]{:S(2)}, u32[]{:S(2)}) %collective-permute-start.15) | collective-permute-done | bytes 524320 | tf_op jit(solution)/shard_map/ppermute | solution.py:494
  80.6 5.7 %shard_map.136 = (bf16[4,2,256,256]{3,2,1,0:T(8,128)(2,1)S(1)}, bf16[2,256,256]{2,1,0:T(8,128)(2,1)S(1)}, bf16[2,256,256]{2,1,0:T(8,128)(2,1)S(1)}, bf16[2,256,2...) custom-call(s32[1,26]{1,0:T(1,128)S(1)} %bitcast.24, ...), custom_call_target="tpu_custom_call" | custom-call | tf_op jit(solution)/shard_map/pallas_call | solution.py:459
  88.4 4.3 %collective-permute-start.19 = (bf16[2,256,256]{2,1,0:T(8,128)(2,1)S(1)}, bf16[2,256,256]{2,1,0:T(8,128)(2,1)S(1)}, u32[]{:S(2)}, u32[]{:S(2)}) collective-permute-start(bf16[2,256,256]{2,1,0:T(8,128)(2,1)S(1)} %get-tuple-element.82), channel_id=1, source_target_pairs={{32,64},{40,72},{48,80},{56,88},{64,32},{72,40},{80,48},{88,56},{3... | collective-permute-start | bytes 786440 | tf_op jit(solution)/shard_map/ppermute | solution.py:500
  92.8 4.4 %collective-permute-done.18 = bf16[2,256,256]{2,1,0:T(8,128)(2,1)S(1)} collective-permute-done((bf16[2,256,256]{2,1,0:T(8,128)(2,1)S(1)}, bf16[2,256,256]{2,1,0:T(8,128)(2,1)S(1)}, u32[]{:S(2)}, u32[]{:S(2)}) %collective-permute-start.18) | collective-permute-done | bytes 262176 | tf_op jit(solution)/shard_map/ppermute | solution.py:500
  97.3 2.6 %collective-permute-done.19 = bf16[2,256,256]{2,1,0:T(8,128)(2,1)S(1)} collective-permute-done((bf16[2,256,256]{2,1,0:T(8,128)(2,1)S(1)}, bf16[2,256,256]{2,1,0:T(8,128)(2,1)S(1)}, u32[]{:S(2)}, u32[]{:S(2)}) %collective-permute-start.19) | collective-permute-done | bytes 262176 | tf_op jit(solution)/shard_map/ppermute | solution.py:500
  104.2 6.5 %collective-permute-done.25.refs_3_ = bf16[2,256,256]{2,1,0:T(8,128)(2,1)S(1)} collective-permute-done((bf16[2,256,256]{2,1,0:T(8,128)(2,1)S(1)}, bf16[2,256,256]{2,1,0:T(8,128)(2,1)S(1)}, u32[]{:S(2)}, u32[]{:S(2)}) %collective-permute-start.25) | collective-permute-done | bytes 262176 | tf_op jit(solution)/shard_map/ppermute | solution.py:50
  112.6 5.6 %shard_map.137 = (bf16[2,256,256]{2,1,0:T(8,128)(2,1)S(1)}, bf16[2,256,256]{2,1,0:T(8,128)(2,1)S(1)}, bf16[2,256,256]{2,1,0:T(8,128)(2,1)S(1)}, bf16[2,256,256]{2,1,0:T(8,128)(2,1)S(1)}) custom-call(s32[1,26]{1,0:T(1,128)S(1)} %bitcast.25, s32[120,128]{1,0:T(8,128)S(1)} %get-tuple-element.71.refs_1_, bf16[4,2,256,256]{3,2,1,0:T(8,128)(2,1)S(1)} %get-tuple-element.87.refs_2_, ...), custom_call_target="tpu_custom_call" | custom-call | tf_op jit(solution)/shard_map/pallas_call | solution.py:459
  118.2 2.5 %collective-permute-done.26.refs_2_ = bf16[2,256,256]{2,1,0:T(8,128)(2,1)S(1)} collective-permute-done((bf16[2,256,256]{2,1,0:T(8,128)(2,1)S(1)}, bf16[2,256,256]{2,1,0:T(8,128)(2,1)S(1)}, u32[]{:S(2)}, u32[]{:S(2)}) %collective-permute-start.26) | collective-permute-done | bytes 262176 | tf_op jit(solution)/shard_map/ppermute | solution.py:50
  121.0 3.8 %collective-permute-start.28 = (bf16[2,256,256]{2,1,0:T(8,128)(2,1)S(1)}, bf16[2,256,256]{2,1,0:T(8,128)(2,1)S(1)}, u32[]{:S(2)}, u32[]{:S(2)}) collective-permute-start(bf16[2,256,256]{2,1,0:T(8,128)(2,1)S(1)} %get-tuple-element.107), channel_id=1, source_target_pairs={{0,16},{8,24},{16,0},{24,8},{32,48},{40,56},{48,32},{56,40},{64,80... | collective-permute-start | bytes 786440 | tf_op jit(solution)/shard_map/ppermute | solution.py:50
  129.3 2.4 %collective-permute-done.27.refs_1_ = bf16[2,256,256]{2,1,0:T(8,128)(2,1)S(1)} collective-permute-done((bf16[2,256,256]{2,1,0:T(8,128)(2,1)S(1)}, bf16[2,256,256]{2,1,0:T(8,128)(2,1)S(1)}, u32[]{:S(2)}, u32[]{:S(2)}) %collective-permute-start.27) | collective-permute-done | bytes 262176 | tf_op jit(solution)/shard_map/ppermute | solution.py:50
  131.7 3.6 %collective-permute-done.28.refs_2_ = bf16[2,256,256]{2,1,0:T(8,128)(2,1)S(1)} collective-permute-done((bf16[2,256,256]{2,1,0:T(8,128)(2,1)S(1)}, bf16[2,256,256]{2,1,0:T(8,128)(2,1)S(1)}, u32[]{:S(2)}, u32[]{:S(2)}) %collective-permute-start.28) | collective-permute-done | bytes 262176 | tf_op jit(solution)/shard_map/ppermute | solution.py:50
  (54 shorter events, 33.7 us)
Async XLA Ops:
  7.3 10.5 %collective-permute-start.1 = (s16[592,128]{1,0:T(8,128)(2,1)S(1)}, s16[592,128]{1,0:T(8,128)(2,1)S(1)}, u32[]{:S(2)}, u32[]{:S(2)}) collective-permute-start(s16[592,128]{1,0:T(8,128)(2,1)S(1)} %get-tuple-element.61), channel_id=1, source_target_pairs={{0,16},{8,24},{16,0},{24,8},{32,48},{40,56},{48,32},{56,40},{64,80... | collective-permute-start | bytes 454664 | tf_op jit(solution)/shard_map/ppermute | solution.py:50
  18.9 15.6 %collective-permute-start.11 = (s16[1280,128]{1,0:T(8,128)(2,1)S(1)}, s16[1280,128]{1,0:T(8,128)(2,1)S(1)}, u32[]{:S(2)}, u32[]{:S(2)}) collective-permute-start(s16[1280,128]{1,0:T(8,128)(2,1)S(1)} %shard_map.130.part0), channel_id=1, source_target_pairs={{0,24},{8,0},{16,8},{24,16},{32,56},{40,32},{48,40},{56,48},{64,88... | collective-permute-start | bytes 983048 | tf_op jit(solution)/shard_map/ppermute | solution.py:50
  21.1 13.4 %collective-permute-start.10 = (s16[1280,128]{1,0:T(8,128)(2,1)S(1)}, s16[1280,128]{1,0:T(8,128)(2,1)S(1)}, u32[]{:S(2)}, u32[]{:S(2)}) collective-permute-start(s16[1280,128]{1,0:T(8,128)(2,1)S(1)} %shard_map.130.part0), channel_id=1, source_target_pairs={{0,16},{8,24},{16,0},{24,8},{32,48},{40,56},{48,32},{56,40},{64,80... | collective-permute-start | bytes 983048 | tf_op jit(solution)/shard_map/ppermute | solution.py:50
  22.2 23.2 %collective-permute-start.7 = (s16[4,592,128]{2,1,0:T(8,128)(2,1)S(1)}, s16[4,592,128]{2,1,0:T(8,128)(2,1)S(1)}, u32[]{:S(2)}, u32[]{:S(2)}) collective-permute-start(s16[4,592,128]{2,1,0:T(8,128)(2,1)S(1)} %get-tuple-element.67.refs_0_.region), channel_id=1, source_target_pairs={{0,1},{2,3},{4,5},{6,7},{1,0},{3,2},{5,4},{7,6},{8,9},{10,11},{12,... | collective-permute-start | bytes 1818632 | tf_op jit(solution)/shard_map/ppermute | solution.py:494
  22.2 23.2 %collective-permute-start.5 = (s16[4,592,128]{2,1,0:T(8,128)(2,1)S(1)}, s16[4,592,128]{2,1,0:T(8,128)(2,1)S(1)}, u32[]{:S(2)}, u32[]{:S(2)}) collective-permute-start(s16[4,592,128]{2,1,0:T(8,128)(2,1)S(1)} %get-tuple-element.67.refs_0_.region), channel_id=1, source_target_pairs={{1,2},{3,4},{5,6},{2,1},{4,3},{6,5},{9,10},{11,12},{13,14},{10,9},... | collective-permute-start | bytes 1818632 | tf_op jit(solution)/shard_map/ppermute | solution.py:494
  24.8 8.8 %collective-permute-start.4 = (s16[592,128]{1,0:T(8,128)(2,1)S(1)}, s16[592,128]{1,0:T(8,128)(2,1)S(1)}, u32[]{:S(2)}, u32[]{:S(2)}) collective-permute-start(s16[592,128]{1,0:T(8,128)(2,1)S(1)} %get-tuple-element.69), channel_id=1, source_target_pairs={{32,64},{40,72},{48,80},{56,88},{64,32},{72,40},{80,48},{88,56},{3... | collective-permute-start | bytes 454664 | tf_op jit(solution)/shard_map/ppermute | solution.py:500
  33.6 10.9 %collective-permute-start.9 = (s16[1280,128]{1,0:T(8,128)(2,1)S(1)}, s16[1280,128]{1,0:T(8,128)(2,1)S(1)}, u32[]{:S(2)}, u32[]{:S(2)}) collective-permute-start(s16[1280,128]{1,0:T(8,128)(2,1)S(1)} %shard_map.130.part0), channel_id=1, source_target_pairs={{0,8},{8,16},{16,24},{24,0},{32,40},{40,48},{48,56},{56,32},{64,72... | collective-permute-start | bytes 983048 | tf_op jit(solution)/shard_map/ppermute | solution.py:50
  34.5 10.9 %collective-permute-start.8 = (s16[2,592,128]{2,1,0:T(8,128)(2,1)S(1)}, s16[2,592,128]{2,1,0:T(8,128)(2,1)S(1)}, u32[]{:S(2)}, u32[]{:S(2)}) collective-permute-start(s16[2,592,128]{2,1,0:T(8,128)(2,1)S(1)} %pad_add_fusion.refs_1_.refs_3_), channel_id=1, source_target_pairs={{0,1},{2,3},{4,5},{6,7},{1,0},{3,2},{5,4},{7,6},{8,9},{10,11},{12,... | collective-permute-start | bytes 909320 | tf_op jit(solution)/shard_map/ppermute | solution.py:494
  34.5 10.9 %collective-permute-start.6 = (s16[2,592,128]{2,1,0:T(8,128)(2,1)S(1)}, s16[2,592,128]{2,1,0:T(8,128)(2,1)S(1)}, u32[]{:S(2)}, u32[]{:S(2)}) collective-permute-start(s16[2,592,128]{2,1,0:T(8,128)(2,1)S(1)} %pad_add_fusion.refs_1_.refs_3_), channel_id=1, source_target_pairs={{1,2},{3,4},{5,6},{2,1},{4,3},{6,5},{9,10},{11,12},{13,14},{10,9},... | collective-permute-start | bytes 909320 | tf_op jit(solution)/shard_map/ppermute | solution.py:494
  56.0 24.5 %collective-permute-start.16 = (bf16[4,2,256,256]{3,2,1,0:T(8,128)(2,1)S(1)}, bf16[4,2,256,256]{3,2,1,0:T(8,128)(2,1)S(1)}, u32[]{:S(2)}, u32[]{:S(2)}) collective-permute-start(bf16[4,2,256,256]{3,2,1,0:T(8,128)(2,1)S(1)} %get-tuple-element.76.refs_2_), channel_id=1, source_target_pairs={{0,1},{2,3},{4,5},{6,7},{1,0},{3,2},{5,4},{7,6},{8,9},{10,11},{12,... | collective-permute-start | bytes 3145736 | tf_op jit(solution)/shard_map/ppermute | solution.py:494
  56.1 24.4 %collective-permute-start.14 = (bf16[4,2,256,256]{3,2,1,0:T(8,128)(2,1)S(1)}, bf16[4,2,256,256]{3,2,1,0:T(8,128)(2,1)S(1)}, u32[]{:S(2)}, u32[]{:S(2)}) collective-permute-start(bf16[4,2,256,256]{3,2,1,0:T(8,128)(2,1)S(1)} %get-tuple-element.76.refs_2_), channel_id=1, source_target_pairs={{1,2},{3,4},{5,6},{2,1},{4,3},{6,5},{9,10},{11,12},{13,14},{10,9},... | collective-permute-start | bytes 3145736 | tf_op jit(solution)/shard_map/ppermute | solution.py:494
  58.2 11.2 %collective-permute-start.13 = (bf16[2,256,256]{2,1,0:T(8,128)(2,1)S(1)}, bf16[2,256,256]{2,1,0:T(8,128)(2,1)S(1)}, u32[]{:S(2)}, u32[]{:S(2)}) collective-permute-start(bf16[2,256,256]{2,1,0:T(8,128)(2,1)S(1)} %get-tuple-element.78), channel_id=1, source_target_pairs={{32,64},{40,72},{48,80},{56,88},{64,32},{72,40},{80,48},{88,56},{3... | collective-permute-start | bytes 786440 | tf_op jit(solution)/shard_map/ppermute | solution.py:500
  70.1 10.5 %collective-permute-start.15 = (bf16[2,2,256,256]{3,2,1,0:T(8,128)(2,1)S(1)}, bf16[2,2,256,256]{3,2,1,0:T(8,128)(2,1)S(1)}, u32[]{:S(2)}, u32[]{:S(2)}) collective-permute-start(bf16[2,2,256,256]{3,2,1,0:T(8,128)(2,1)S(1)} %pad_maximum_fusion.refs_3_), channel_id=1, source_target_pairs={{1,2},{3,4},{5,6},{2,1},{4,3},{6,5},{9,10},{11,12},{13,14},{10,9},... | collective-permute-start | bytes 1572872 | tf_op jit(solution)/shard_map/ppermute | solution.py:494
  86.3 24.4 %collective-permute-start.22 = (bf16[4,2,256,256]{3,2,1,0:T(8,128)(2,1)S(1)}, bf16[4,2,256,256]{3,2,1,0:T(8,128)(2,1)S(1)}, u32[]{:S(2)}, u32[]{:S(2)}) collective-permute-start(bf16[4,2,256,256]{3,2,1,0:T(8,128)(2,1)S(1)} %get-tuple-element.87.refs_2_), channel_id=1, source_target_pairs={{0,1},{2,3},{4,5},{6,7},{1,0},{3,2},{5,4},{7,6},{8,9},{10,11},{12,... | collective-permute-start | bytes 3145736 | tf_op jit(solution)/shard_map/ppermute | solution.py:494
  86.4 24.4 %collective-permute-start.20 = (bf16[4,2,256,256]{3,2,1,0:T(8,128)(2,1)S(1)}, bf16[4,2,256,256]{3,2,1,0:T(8,128)(2,1)S(1)}, u32[]{:S(2)}, u32[]{:S(2)}) collective-permute-start(bf16[4,2,256,256]{3,2,1,0:T(8,128)(2,1)S(1)} %get-tuple-element.87.refs_2_), channel_id=1, source_target_pairs={{1,2},{3,4},{5,6},{2,1},{4,3},{6,5},{9,10},{11,12},{13,14},{10,9},... | collective-permute-start | bytes 3145736 | tf_op jit(solution)/shard_map/ppermute | solution.py:494
  88.3 9.0 %collective-permute-start.18 = (bf16[2,256,256]{2,1,0:T(8,128)(2,1)S(1)}, bf16[2,256,256]{2,1,0:T(8,128)(2,1)S(1)}, u32[]{:S(2)}, u32[]{:S(2)}) collective-permute-start(bf16[2,256,256]{2,1,0:T(8,128)(2,1)S(1)} %get-tuple-element.81), channel_id=1, source_target_pairs={{0,32},{8,40},{16,48},{24,56},{64,96},{72,104},{80,112},{88,120},{... | collective-permute-start | bytes 786440 | tf_op jit(solution)/shard_map/ppermute | solution.py:500
  88.4 11.5 %collective-permute-start.19 = (bf16[2,256,256]{2,1,0:T(8,128)(2,1)S(1)}, bf16[2,256,256]{2,1,0:T(8,128)(2,1)S(1)}, u32[]{:S(2)}, u32[]{:S(2)}) collective-permute-start(bf16[2,256,256]{2,1,0:T(8,128)(2,1)S(1)} %get-tuple-element.82), channel_id=1, source_target_pairs={{32,64},{40,72},{48,80},{56,88},{64,32},{72,40},{80,48},{88,56},{3... | collective-permute-start | bytes 786440 | tf_op jit(solution)/shard_map/ppermute | solution.py:500
  92.7 9.9 %collective-permute-start.24 = (bf16[2,256,256]{2,1,0:T(8,128)(2,1)S(1)}, bf16[2,256,256]{2,1,0:T(8,128)(2,1)S(1)}, u32[]{:S(2)}, u32[]{:S(2)}) collective-permute-start(bf16[2,256,256]{2,1,0:T(8,128)(2,1)S(1)} %get-tuple-element.83), channel_id=1, source_target_pairs={{0,8},{8,16},{16,24},{24,0},{32,40},{40,48},{48,56},{56,32},{64,72... | collective-permute-start | bytes 786440 | tf_op jit(solution)/shard_map/ppermute | solution.py:50
  99.9 10.8 %collective-permute-start.23 = (bf16[2,2,256,256]{3,2,1,0:T(8,128)(2,1)S(1)}, bf16[2,2,256,256]{3,2,1,0:T(8,128)(2,1)S(1)}, u32[]{:S(2)}, u32[]{:S(2)}) collective-permute-start(bf16[2,2,256,256]{3,2,1,0:T(8,128)(2,1)S(1)} %pad_maximum_fusion.1.refs_3_), channel_id=1, source_target_pairs={{0,1},{2,3},{4,5},{6,7},{1,0},{3,2},{5,4},{7,6},{8,9},{10,11},{12,... | collective-permute-start | bytes 1572872 | tf_op jit(solution)/shard_map/ppermute | solution.py:494
  100.1 10.6 %collective-permute-start.21 = (bf16[2,2,256,256]{3,2,1,0:T(8,128)(2,1)S(1)}, bf16[2,2,256,256]{3,2,1,0:T(8,128)(2,1)S(1)}, u32[]{:S(2)}, u32[]{:S(2)}) collective-permute-start(bf16[2,2,256,256]{3,2,1,0:T(8,128)(2,1)S(1)} %pad_maximum_fusion.1.refs_3_), channel_id=1, source_target_pairs={{1,2},{3,4},{5,6},{2,1},{4,3},{6,5},{9,10},{11,12},{13,14},{10,9},... | collective-permute-start | bytes 1572872 | tf_op jit(solution)/shard_map/ppermute | solution.py:494
  110.8 10.0 %collective-permute-start.26 = (bf16[2,256,256]{2,1,0:T(8,128)(2,1)S(1)}, bf16[2,256,256]{2,1,0:T(8,128)(2,1)S(1)}, u32[]{:S(2)}, u32[]{:S(2)}) collective-permute-start(bf16[2,256,256]{2,1,0:T(8,128)(2,1)S(1)} %get-tuple-element.98), channel_id=1, source_target_pairs={{0,16},{8,24},{16,0},{24,8},{32,48},{40,56},{48,32},{56,40},{64,80... | collective-permute-start | bytes 786440 | tf_op jit(solution)/shard_map/ppermute | solution.py:50
  120.7 11.0 %collective-permute-start.27 = (bf16[2,256,256]{2,1,0:T(8,128)(2,1)S(1)}, bf16[2,256,256]{2,1,0:T(8,128)(2,1)S(1)}, u32[]{:S(2)}, u32[]{:S(2)}) collective-permute-start(bf16[2,256,256]{2,1,0:T(8,128)(2,1)S(1)} %get-tuple-element.106), channel_id=1, source_target_pairs={{0,8},{8,16},{16,24},{24,0},{32,40},{40,48},{48,56},{56,32},{64,72... | collective-permute-start | bytes 786440 | tf_op jit(solution)/shard_map/ppermute | solution.py:50
  121.0 14.3 %collective-permute-start.28 = (bf16[2,256,256]{2,1,0:T(8,128)(2,1)S(1)}, bf16[2,256,256]{2,1,0:T(8,128)(2,1)S(1)}, u32[]{:S(2)}, u32[]{:S(2)}) collective-permute-start(bf16[2,256,256]{2,1,0:T(8,128)(2,1)S(1)} %get-tuple-element.107), channel_id=1, source_target_pairs={{0,16},{8,24},{16,0},{24,8},{32,48},{40,56},{48,32},{56,40},{64,80... | collective-permute-start | bytes 786440 | tf_op jit(solution)/shard_map/ppermute | solution.py:50
  124.8 10.9 %collective-permute-start.29 = (bf16[2,256,256]{2,1,0:T(8,128)(2,1)S(1)}, bf16[2,256,256]{2,1,0:T(8,128)(2,1)S(1)}, u32[]{:S(2)}, u32[]{:S(2)}) collective-permute-start(bf16[2,256,256]{2,1,0:T(8,128)(2,1)S(1)} %get-tuple-element.108), channel_id=1, source_target_pairs={{0,24},{8,0},{16,8},{24,16},{32,56},{40,32},{48,40},{56,48},{64,88... | collective-permute-start | bytes 786440 | tf_op jit(solution)/shard_map/ppermute | solution.py:50
  (6 other events, 40.5 us)

commit v2 on v1

--- a/solution.py
+++ b/solution.py
@@ -1,3 +1,4 @@
+import functools
 import math
 
 import jax
@@ -126,10 +127,11 @@
         edge_blocks[slot][...] = region[edge_row(flags, slot) // (HALO - 1) * (RING - 1)]
 
 
-def operators_kernel(flags, part0, part1, part2, part3, ops):
+def operators_kernel(flags, own, other, far, ops):
     z = flags[0, 0]
-    for d, part in enumerate((part0, part1, part2, part3)):
-        at = pl.ds(pl.multiple_of((z + RING - d) % RING * T, T), T)
+    blocks = ((own, z), (other, z + 1 - z % 2 * 2), (far.at[0], 3 - z), (far.at[1], 2 + z % 2 * 2 - z))
+    for part, place in blocks:
+        at = pl.ds(pl.multiple_of(place * T, T), T)
         for layer in range(2):
             for n in range(5):
                 base = (layer * 5 + n) * T
@@ -140,7 +142,7 @@
 OWN, CROSS, NEAR = 0, 1, 2
 
 
-def neighbourhood(own, ends, cross, cross_ends, near, near_ends):
+def neighbourhood(own, ends, near, near_ends, cross, cross_ends):
     def block(row, side):
         if row in SLOTS:
             return (ends, cross_ends, near_ends)[side].at[SLOTS.index(row)]
@@ -171,9 +173,7 @@
     return 1 if side == OWN else flags[0, 3] if side == CROSS else 2 - flags[0, 3]
 
 
-def build_kernel(flags, *refs):
-    ops_in, idx, bd1, bd2, ops, codes = refs[6:]
-    block = neighbourhood(*refs[:6])
+def coupling_tables(ref, home, bd1, bd2=None, n=None):
     rows, cols = lane_iota((32, 256), 0), lane_iota((32, 256), 1)
     place = ((rows // 16 == cols // 128) & (rows % 16 == cols % 16)).astype(BF16)
     i, j = lane_iota((256, 256), 0), lane_iota((256, 256), 1)
@@ -185,20 +185,27 @@
         full = lax.dot_general(a, b, first, preferred_element_type=F32)
         return jnp.where(mask, full, 0.0).astype(BF16)
 
+    c = jnp.concatenate([decoded(ref[PHASE_ROWS + m : PHASE_ROWS + m + 32, :]) for m in (0, 32)], 1)
+    c = c * COUPLING_UNIT
+    high = c.astype(BF16)
+    low = (c - high.astype(F32)).astype(BF16)
+    bd1[home, 0:256, :] = spread(high, place, mask1)
+    bd1[home, 256:512, :] = spread(low, place, mask1)
+    if bd2 is not None:
+        bd2[n, 0:256, :] = spread(place, high, mask2)
+        bd2[n, 256:512, :] = spread(place, low, mask2)
+
+
+def build_kernel(flags, *refs):
+    idx, bd1, ops, codes = refs[8:]
+    block = neighbourhood(*refs[:6])
     codes[...] = jnp.zeros_like(codes)
     for side in (OWN, CROSS, NEAR):
         for row in ROWS:
             home = row_of(flags, row) * 3 + column_of(flags, side)
             ref = block(row, side)
-            c = jnp.concatenate([decoded(ref[PHASE_ROWS + n : PHASE_ROWS + n + 32, :]) for n in (0, 32)], 1)
-            c = c * COUPLING_UNIT
-            high = c.astype(BF16)
-            low = (c - high.astype(F32)).astype(BF16)
-            bd1[home, 0:256, :] = spread(high, place, mask1)
-            bd1[home, 256:512, :] = spread(low, place, mask1)
-            if side == OWN and row not in SLOTS:
-                bd2[row - 1, 0:256, :] = spread(place, high, mask2)
-                bd2[row - 1, 256:512, :] = spread(place, low, mask2)
+            if side != OWN or row in SLOTS:
+                coupling_tables(ref, home, bd1)
             words = ref[PHASE_ROWS + 64 : PHASE_ROWS + 80, :].astype(jnp.int32)
             codes[0, pl.ds(home, 1), :] = words[CODE - 64 : CODE - 63, :]
             codes[1, pl.ds(home, 1), :] = words[AT - 64 : AT - 63, :]
@@ -222,7 +229,6 @@
         used = jnp.max(jnp.max(hit, axis=1, keepdims=True), axis=0, keepdims=True)
         idx[USED + n : USED + n + 1, :] = jnp.broadcast_to(used, (1, T)).astype(jnp.int32)
 
-    ops[:, 0:5] = ops_in[...]
     lane = lane_iota((T, T), 1)
 
     def edge(ref, row):
@@ -230,7 +236,7 @@
         return words[row - 64 : row - 63, :] * HOP_UNIT + HOP_MID
 
     for layer in range(2):
-        ops[layer, 5, 0 : RING * T - 1, :] = ops_in[layer, 1, 1 : RING * T, :]
+        ops[layer, 5, 0 : RING * T - 1, :] = ops[layer, 1, 1 : RING * T, :]
         below = [edge(block(slot, OWN), ROW_EDGE + layer) for slot in SLOTS]
         ops[layer, 5, RING * T - 1 : RING * T, :] = jnp.where(
             jnp.broadcast_to(flags[0, 7], (1, T)) == HALO - 1, below[0], below[1]
@@ -240,7 +246,7 @@
             far, close = [edge(block(r + 1, side), COL_EDGE + layer) for side in (CROSS, NEAR)]
             right = jnp.where(jnp.broadcast_to(flags[0, 3], (1, T)) == 2, far, close)
             column = jnp.broadcast_to(right, (T, T)).T
-            ops[layer, 6, rows, :] = jnp.where(lane == T - 1, column, pltpu.roll(ops_in[layer, 2, rows, :], T - 1, 1))
+            ops[layer, 6, rows, :] = jnp.where(lane == T - 1, column, pltpu.roll(ops[layer, 2, rows, :], T - 1, 1))
 
 
 def cos_sin(code):
@@ -258,38 +264,56 @@
     return cos_v, sin_v
 
 
-def zero_kernel(region, zero_out, narrow_out):
+def zero_kernel(region, zero_out, narrow_out, bd1, bd2):
     for rb in range(RING):
-        rows = slice(rb * T, (rb + 1) * T)
+        coupling_tables(region.at[rb], (rb + 1) * 3 + 1, bd1, bd2, rb)
         for layer in range(2):
             for a in range(2):
                 at = (layer * 2 + a) * T
                 pair = cos_sin(region[rb, at : at + T, :])
                 for p in range(2):
-                    zero_out[layer, a, p, rows, :] = pair[p]
+                    zero_out[layer, a, p, rows_of(rb), :] = pair[p]
                     narrow_out[rb, layer, a * T : (a + 1) * T, p * T : (p + 1) * T] = pair[p].astype(BF16)
 
 
-def step_kernel(first, last, *refs):
+def step_kernel(first, last, begin, end, *refs):
     refs = list(refs)
-    around = neighbourhood(*refs[2:8])
-    flags, idx, bd1, bd2, ops = refs[:2] + refs[8:11]
-    refs = refs[11:]
-    prev = None if first else refs.pop(0)
-    wide_out = refs.pop(0) if first else None
-    if last:
+    flags, idx = refs[:2]
+    refs = refs[2:]
+    own = ends = cross = cross_ends = near = near_ends = sums_in = sums_out = prev = wide_out = narrow_out = None
+    if begin:
+        own, ends, near, near_ends = refs[:4]
+        refs = refs[4:]
+    if end:
+        cross, cross_ends = refs[:2]
+        refs = refs[2:]
+    around = neighbourhood(own, ends, near, near_ends, cross, cross_ends)
+    bd1, bd2, ops = refs[:3]
+    refs = refs[3:]
+    sides = (OWN, NEAR) * begin + (CROSS,) * end
+    far_column = column_of(flags, CROSS)
+    here = [(begin and end) or (column_of(flags, CROSS if end else NEAR) == cb) for cb in (0, 2)]
+    if end and not begin:
+        sums_in = refs.pop(0)
+    if end and not first:
+        prev = refs.pop(0)
+    if first:
+        wide_out = refs.pop(0)
+    edge_blocks, parts = [], []
+    if not end:
+        sums_out = refs.pop(0)
+    elif last:
         parts = refs[:RING]
         refs = refs[RING:]
         narrow_out = refs.pop()
     else:
         narrow_out, *edge_blocks = refs[:3]
         refs = refs[3:]
-        parts = []
         if not first:
             parts = refs[:RING]
             refs = refs[RING:]
-    fu, fv, fvs, gathered, terms, acc1, acc2 = refs[:7]
-    xv = refs[7] if first else None
+    fu, fv, fvs, gathered, sources, terms_a, terms_b, acc1, acc2, homes, count = refs[:11]
+    xv = refs[11] if first else None
 
     def halves(p):
         return slice(p * T, (p + 1) * T)
@@ -326,7 +350,7 @@
             elif edge:
                 fvs[cb // 2, p, rows_of(rb - 1), :] = value
 
-    for side, row in [(side, row) for side in (OWN, CROSS, NEAR) for row in ROWS]:
+    for side, row in [(side, row) for side in sides for row in ROWS]:
         cb = column_of(flags, side)
         for layer in range(2):
             if side == OWN and row not in SLOTS:
@@ -349,42 +373,69 @@
                 for a in range(2) if edge is None else (1 - edge,):
                     load(layer, row, side, a, False)
 
+    if sums_in is not None:
+        acc1[:, :, 0 : RING * T, :] = sums_in[0]
+        acc2[...] = sums_in[1]
+    else:
+        acc1[...] = jnp.zeros_like(acc1)
+        acc2[...] = jnp.zeros_like(acc2)
     for r in range(RING):
         home = (r + 1) * 3 + 1
+        columns = [idx[SRC_COL + home, k] for k in range(KS)]
+        wanted = [(col == far_column) if end else (col != far_column) for col in columns]
         for k in range(KS):
-            row = idx[SRC_ROW + home, k]
-            col = idx[SRC_COL + home, k]
+            source = idx[SRC_ROW + home, k]
             for a in range(2):
                 for p in range(2):
-                    piece = fu[col, a, p, pl.ds(row, SR), :].astype(BF16)
-                    gathered[k * 32 + a * SR : k * 32 + (a + 1) * SR, p * T : (p + 1) * T] = piece
-        both = jnp.dot(bd2[r], gathered[...], preferred_element_type=F32)
+                    piece = fu[columns[k], a, p, pl.ds(source, SR), :]
+                    if not (begin and end):
+                        piece = jnp.where(wanted[k], piece, 0.0)
+                    gathered[r, k * 32 + a * SR : k * 32 + (a + 1) * SR, halves(p)] = piece.astype(BF16)
+    for r in range(RING):
+        both = jnp.dot(bd2[r], gathered[r], preferred_element_type=F32)
         summed = both[:256] + both[256:]
         for b in range(2):
             for p in range(2):
-                acc2[b, p, r * T : (r + 1) * T, :] = summed[b * T : (b + 1) * T, p * T : (p + 1) * T]
-
-    acc1[...] = jnp.zeros_like(acc1)
-    for side, row in [(side, row) for side in (OWN, CROSS, NEAR) for row in ROWS]:
+                acc2[b, p, rows_of(r), :] += summed[b * T : (b + 1) * T, halves(p)]
+
+    count[0] = 1
+    homes[0] = HOMES
+    for side, row in [(side, row) for side in sides for row in ROWS]:
         home = row_of(flags, row) * 3 + column_of(flags, side)
 
         @pl.when(idx[ANY + home, 0] > 0)
         def _():
+            n = count[0]
             decoded_here = first and (side != OWN or row in SLOTS)
-            source = xv[home] if decoded_here else around(row, side)[1]
-            both = jnp.dot(bd1[home], source, preferred_element_type=F32)
-            terms[...] = both[:256] + both[256:]
-            for k in range(KS):
-                landing = idx[LAND + home, k]
-
-                @pl.when(landing >= 0)
-                def _():
-                    for a in range(2):
-                        for p in range(2):
-                            at = (a, p, pl.ds(landing, SR), slice(None))
-                            acc1[at] = acc1[at] + terms[
-                                k * 32 + a * SR : k * 32 + (a + 1) * SR, p * T : (p + 1) * T
-                            ]
+            sources[n] = xv[home] if decoded_here else around(row, side)[1]
+            homes[n] = home
+            count[0] = n + 1
+
+    homes[count[0]] = HOMES
+
+    def product(n):
+        both = jnp.dot(bd1[jnp.minimum(homes[n], HOMES - 1)], sources[n], preferred_element_type=F32)
+        return both[:256] + both[256:]
+
+    def scatter(n, held):
+        for k in range(KS):
+            landing = idx[LAND + homes[n], k]
+            landing = jnp.where(landing < 0, RING * T, landing)
+            for a in range(2):
+                for p in range(2):
+                    at = (a, p, pl.ds(landing, SR), slice(None))
+                    acc1[at] = acc1[at] + held[k * 32 + a * SR : k * 32 + (a + 1) * SR, halves(p)]
+
+    def pair(j, carry):
+        terms_a[...] = product(2 * j + 1)
+        scatter(2 * j, terms_b)
+        terms_b[...] = product(2 * j + 2)
+        scatter(2 * j + 1, terms_a)
+        return carry
+
+    pairs = count[0] // 2
+    lax.fori_loop(0, pairs, pair, 0)
+    scatter(2 * pairs, terms_b)
 
     lane = lane_iota((T, T), 1)
     for layer in range(2):
@@ -401,25 +452,32 @@
             return fvs[cb // 2, p, r * T : (r + 1) * T, :]
 
         for r in range(RING):
-            rows = slice(r * T, (r + 1) * T)
+            rows = rows_of(r)
             h0, h1, h2, e0, e1, h1s, h2s = [ops[layer, n, rows, :] for n in range(7)]
             for p in range(2):
-                base = (r + 1) * T
-                w0, w1 = field(0, p, base), field(1, p, base)
-                before = jnp.where(lane == 0, pltpu.roll(beside(1, p, r, 0), 1, 1), pltpu.roll(w1, 1, 1))
-                after = jnp.where(
-                    lane == T - 1, pltpu.roll(beside(0, p, r, 2), T - 1, 1), pltpu.roll(w0, T - 1, 1)
-                )
-                upper = e0 * w0 + h0 * w1 + h1 * field(1, p, base - 1) + h2 * before + acc[0, p, rows, :]
-                lower = e1 * w1 + h0 * w0 + h1s * field(0, p, base + 1) + h2s * after + acc[1, p, rows, :]
+                upper, lower = acc[0, p, rows, :], acc[1, p, rows, :]
+                before = jnp.where((lane == 0) & here[0], pltpu.roll(beside(1, p, r, 0), 1, 1), 0.0)
+                after = jnp.where((lane == T - 1) & here[1], pltpu.roll(beside(0, p, r, 2), T - 1, 1), 0.0)
+                if begin:
+                    base = (r + 1) * T
+                    w0, w1 = field(0, p, base), field(1, p, base)
+                    upper = upper + (e0 * w0 + h0 * w1 + h1 * field(1, p, base - 1))
+                    lower = lower + (e1 * w1 + h0 * w0 + h1s * field(0, p, base + 1))
+                    before = jnp.where(lane == 0, before, pltpu.roll(w1, 1, 1))
+                    after = jnp.where(lane == T - 1, after, pltpu.roll(w0, T - 1, 1))
+                upper = upper + h2 * before
+                lower = lower + h2s * after
                 for a, value in enumerate((upper, lower)):
+                    if not end:
+                        sums_out[layer, a, p, rows, :] = value
+                        continue
                     if first:
                         wide_out[layer, a, p, rows, :] = value
                     else:
                         value = 2.0 * value - prev[layer, a, p, rows, :]
-                    narrow_out[r, layer, a * T : (a + 1) * T, p * T : (p + 1) * T] = value.astype(BF16)
-
-    if not last:
+                    narrow_out[r, layer, a * T : (a + 1) * T, halves(p)] = value.astype(BF16)
+
+    if edge_blocks:
         for slot in range(2):
             edge_blocks[slot][...] = narrow_out[edge_row(flags, slot) // (HALO - 1) * (RING - 1)]
     for d, part in enumerate(parts):
@@ -455,7 +513,7 @@
 BLOCK = jax.ShapeDtypeStruct((2, 2 * T, 2 * T), BF16)
 
 
-def local(kernel, out_shape, scalars, *operands, far=(), scratch=()):
+def local(kernel, out_shape, scalars, *operands, far=(), scratch=(), cost=None, alias=None):
     return pl.pallas_call(
         kernel,
         out_shape=out_shape,
@@ -463,29 +521,46 @@
         out_specs=jax.tree.map(lambda _: VMEM, out_shape),
         scratch_shapes=list(scratch),
         compiler_params=PARAMS,
+        cost_estimate=cost,
+        input_output_aliases=alias or {},
     )(*scalars, *operands, *(pltpu.with_memory_space_constraint(x, pltpu.HBM) for x in far))
 
 
-def step(first, last, flags, idx, halo, bd1, bd2, ops, prev=None):
+def step(first, last, begin, end, flags, idx, halo, *rest):
     scratch = [
         pltpu.VMEM((3, 2, 2, HALO * T, T), F32),
         pltpu.VMEM((2, 2, HALO * T, T), F32),
         pltpu.VMEM((2, 2, RING * T, T), F32),
-        pltpu.VMEM((2 * T, 2 * T), BF16),
+        pltpu.VMEM((RING, 2 * T, 2 * T), BF16),
+        pltpu.VMEM((HOMES + 2, 2 * T, 2 * T), BF16),
         pltpu.VMEM((2 * T, 2 * T), F32),
+        pltpu.VMEM((2 * T, 2 * T), F32),
+        pltpu.VMEM((2, 2, RING * T + SR, T), F32),
         pltpu.VMEM((2, 2, RING * T, T), F32),
-        pltpu.VMEM((2, 2, RING * T, T), F32),
+        pltpu.SMEM((HOMES + 2,), jnp.int32),
+        pltpu.SMEM((1,), jnp.int32),
     ]
     if first:
         scratch.append(pltpu.VMEM((HOMES, 2 * T, 2 * T), BF16))
         out = (WIDE, NARROW, BLOCK, BLOCK)
+    elif not end:
+        out = WIDE
     elif last:
         scratch.append(pltpu.VMEM(NARROW.shape, BF16))
         out = (BLOCK,) * RING
     else:
         out = (NARROW, BLOCK, BLOCK) + (BLOCK,) * RING
-    operands = [*halo, bd1, bd2, ops] + ([] if first else [prev])
-    return local(lambda *refs: step_kernel(first, last, *refs), out, (flags, idx), *operands, scratch=scratch)
+    halo = halo[: 6 if end else 4][0 if begin else 4 :]
+    kernel = functools.partial(step_kernel, first, last, begin, end)
+    moved_bytes = sum(math.prod(x.shape) * x.dtype.itemsize for x in (*halo, *rest, *jax.tree.leaves(out)))
+    products = 2 * (RING + HALO) * 512 * 256 * 256
+    cost = pl.CostEstimate(flops=products, bytes_accessed=moved_bytes, transcendentals=0)
+    return local(kernel, out, (flags, idx), *halo, *rest, scratch=scratch, cost=cost)
+
+
+def halved_step(last, flags, idx, halo, tables, prev):
+    sums = step(False, last, True, False, flags, idx, halo, *tables)
+    return step(False, last, False, True, flags, idx, halo, *tables, sums, prev)
 
 
 def across(array, low):
@@ -500,10 +575,17 @@
     return lax.ppermute(array, "gx", pairs + [(j, i) for i, j in pairs])
 
 
-def halo_of(region, block_a, block_b):
+def halo_of(region, block_a, block_b, beside=()):
     cross, near = across(region, 1), across(region, 0)
     ends = jnp.stack([swapped_rows(block_a, 0), swapped_rows(block_b, 1)])
-    return (region, ends, cross, across(ends, 1), near, across(ends, 0))
+    ends, beside = lax.optimization_barrier((ends, beside))
+    return (region, ends, near, across(ends, 0), cross, across(ends, 1)), beside
+
+
+def ring_swapped(array, partner):
+    size = lax.axis_size("gx")
+    pairs = [(i, i // RING * RING + partner[i % RING]) for i in range(size)]
+    return lax.ppermute(array, "gx", pairs)
 
 
 def ring_exchanged(parts):
@@ -523,9 +605,11 @@
     )(flags, *parts, *before)
 
 
-def results(flags, parts):
-    own = written(flags, (0,), parts[:1])
-    return written(flags, (1, 2, 3), parts[1:], own)
+def results(flags, parts, groups):
+    out = ()
+    for shifts in groups:
+        out = written(flags, shifts, [parts[d] for d in shifts], out)
+    return out
 
 
 def body(phase_one, phase_two, hop_one, hop_two, onsite_one, onsite_two, coupling, owner, target_row, live_strips):
@@ -562,40 +646,41 @@
         far=(hop_one, hop_two, onsite_one, onsite_two),
         scratch=[pltpu.VMEM((2, 5, T, T), F32), pltpu.SemaphoreType.DMA((10,))],
     )
-    parts, packed = lax.optimization_barrier((parts, packed))
-    packs = ring_exchanged([packed] * RING)
+    other = ring_swapped(packed, (1, 0, 3, 2))
+    parts, other = lax.optimization_barrier((parts, other))
+    packs = (packed, other, ring_swapped(jnp.stack([packed, other]), (3, 2, 1, 0)))
 
     region = local(
         region_kernel, (jax.ShapeDtypeStruct((RING, CARGO, T), I16), cargo, cargo), (flags,), *parts
     )
-    halo = halo_of(*region)
-    zero, zero_narrow = local(zero_kernel, (WIDE, NARROW), (), region[0])
-    ops = local(operators_kernel, jax.ShapeDtypeStruct((2, 5, RING * T, T), F32), (flags,), *packs)
-    idx, bd1, bd2, ops = local(
+    table = jax.ShapeDtypeStruct((HOMES, 512, 256), BF16)
+    early = local(
+        zero_kernel, (WIDE, NARROW, table, jax.ShapeDtypeStruct((RING, 512, 256), BF16)), (), region[0]
+    )
+    halo, (zero, zero_narrow, bd1, bd2) = halo_of(*region, early)
+    ops_shape = jax.ShapeDtypeStruct((2, 7, RING * T, T), F32)
+    ops = local(operators_kernel, ops_shape, (flags,), *packs)
+    idx, bd1, ops = local(
         build_kernel,
-        (
-            jax.ShapeDtypeStruct((IDX_ROWS, T), jnp.int32),
-            jax.ShapeDtypeStruct((HOMES, 512, 256), BF16),
-            jax.ShapeDtypeStruct((RING, 512, 256), BF16),
-            jax.ShapeDtypeStruct((2, 7, RING * T, T), F32),
-        ),
+        (jax.ShapeDtypeStruct((IDX_ROWS, T), jnp.int32), table, ops_shape),
         (flags,),
         *halo,
+        bd1,
         ops,
         scratch=[pltpu.VMEM((2, 24, T), jnp.int32)],
-    )
-
-    one, *one_blocks = step(True, False, flags, idx, (zero_narrow, *halo[1:]), bd1, bd2, ops)
-    *two_blocks, part0, part1, part2, part3 = step(
-        False, False, flags, idx, halo_of(*one_blocks), bd1, bd2, ops, zero
-    )
-    got1, got3 = ring_moved(part1, 1), ring_moved(part3, 3)
-    halo, got1, got3, part2 = lax.optimization_barrier((halo_of(*two_blocks), got1, got3, part2))
-    got2 = ring_moved(part2, 2)
-    three_parts = step(False, True, flags, idx, halo, bd1, bd2, ops, one)
-    three_parts, got2 = lax.optimization_barrier((three_parts, got2))
-    two_a, two_b = results(flags, (part0, got1, got2, got3))
-    three_a, three_b = results(flags, ring_exchanged(three_parts))
+        alias={7: 1, 8: 2},
+    )
+
+    tables = (bd1, bd2, ops)
+    one, *one_blocks = step(True, False, True, True, flags, idx, (zero_narrow, *halo[1:]), *tables)
+    *two_blocks, part0, part1, part2, part3 = halved_step(
+        False, flags, idx, halo_of(*one_blocks)[0], tables, zero
+    )
+    got = ring_exchanged((part0, part1, part2, part3))
+    three_parts = halved_step(True, flags, idx, halo_of(*two_blocks)[0], tables, one)
+    three_parts, got = lax.optimization_barrier((three_parts, got))
+    two_a, two_b = results(flags, got, ((0,), (1, 2, 3)))
+    three_a, three_b = results(flags, ring_exchanged(three_parts), ((0,), (1,), (2,), (3,)))
     return two_a, two_b, three_a, three_b
 
 

time: 138 us -> 130 us (0.942)
  waiting for transfers between devices: 54.2 us -> 37.8 us
  Pallas kernels: 34.1 us -> 40.8 us
    ppermute x12 -> x9, waiting for transfers between devices: 27.3 us -> 13.5 us  [ring_moved(): return lax.ppermute(array, 'gx', pairs)]
    ppermute x6, waiting for transfers between devices: 18.3 us -> 13.2 us  [swapped_rows(): return lax.ppermute(array, 'gx', pairs + [(j, i) for i, j in pairs])]
    pallas_call x9 -> x11, Pallas kernels: 27.9 us -> 32.3 us  [local(): pl.pallas_call(kernel, out_shape=out_shape, in_specs=[SMEM] * len(scalars...]
    ppermute x12 -> x9, starting transfers between devices: 17.9 us -> 14.3 us  [ring_moved(): return lax.ppermute(array, 'gx', pairs)]
    ppermute x0 -> x2, starting transfers between devices: none -> 2.75 us  [ring_swapped(): return lax.ppermute(array, 'gx', pairs)]
    ppermute x12, waiting for transfers between devices: 8.59 us -> 11.2 us  [across(): return lax.ppermute(array, 'gy', pairs + [(j, i) for i, j in pairs])]
    ppermute x12, starting transfers between devices: 13.8 us -> 16.3 us  [across(): return lax.ppermute(array, 'gy', pairs + [(j, i) for i, j in pairs])]
    pallas_call x4 -> x6, Pallas kernels: 6.22 us -> 8.57 us  [written(): pl.pallas_call(lambda *refs: result_kernel(shifts, *refs), out_shape=(jax...]
  transfers between devices with their start and end apart: 30 -> 29, of which waited for: 16 -> 13; matrix products, arithmetic and copies ran while one was open for 0% -> 2% of each run, Pallas kernels for 10% -> 20%
where the time goes in v2:
time: 130 us; the launch traced here: 129 us
  starting transfers between devices  46.6 us (36%)
  Pallas kernels  40.8 us (31%)
  waiting for transfers between devices  37.8 us (29%)
  local copies, waits for them, and re-layouts  1.89 us (1%)
  between operations  1.75 us (1%)
    pallas_call x11, Pallas kernels, local(): pl.pallas_call(kernel, out_shape=out_shape, in_specs=[SMEM] * len(scalars...  32.3 us
    ppermute x12, starting transfers between devices, across(): return lax.ppermute(array, 'gy', pairs + [(j, i) for i, j in pairs])  16.3 us
    ppermute x9, starting transfers between devices, ring_moved(): return lax.ppermute(array, 'gx', pairs)  14.3 us
    ppermute x9, waiting for transfers between devices, ring_moved(): return lax.ppermute(array, 'gx', pairs)  13.5 us
    ppermute x6, starting transfers between devices, swapped_rows(): return lax.ppermute(array, 'gx', pairs + [(j, i) for i, j in pairs])  13.2 us
    ppermute x6, waiting for transfers between devices, swapped_rows(): return lax.ppermute(array, 'gx', pairs + [(j, i) for i, j in pairs])  13.2 us
    ppermute x12, waiting for transfers between devices, across(): return lax.ppermute(array, 'gy', pairs + [(j, i) for i, j in pairs])  11.2 us
    pallas_call x6, Pallas kernels, written(): pl.pallas_call(lambda *refs: result_kernel(shifts, *refs), out_shape=(jax...  8.57 us
  transfers between devices with their start and end apart: 29, of which 13 were waited for; matrix products, arithmetic and copies ran while one was open for 2% of the time, Pallas kernels for 20%

profile of v2, /device:TPU:10, one launch (start us, length us, event | category | flops | bytes accessed | tf_op | source)
XLA Modules:
  0.0 129.1 jit_solution(11108753399441464547)
XLA Ops:
  1.9 2.0 %collective-permute-start.3 = (s16[1280,128]{1,0:T(8,128)(2,1)S(1)}, s16[1280,128]{1,0:T(8,128)(2,1)S(1)}, u32[]{:S(2)}, u32[]{:S(2)}) collective-permute-start(s16[1280,128]{1,0:T(8,128)(2,1)S(1)} %shard_map.130.own), channel_id=1, source_target_pairs={{0,8},{8,0},{16,24},{24,16},{32,40},{40,32},{48,56},{56,48},{64,72... | collective-permute-start | bytes 983048 | tf_op jit(solution)/shard_map/ppermute | solution.py:588
  6.4 2.0 %shard_map.129 = (s16[592,128]{1,0:T(8,128)(2,1)S(1)}, s16[592,128]{1,0:T(8,128)(2,1)S(1)}, s16[592,128]{1,0:T(8,128)(2,1)S(1)}, s16[592,128]{1,0:T(8,128)(2,1)S(1)}) custom-call(s32[1,26]{1,0:T(1,128)S(1)} %bitcast.23, f32[256,32]{1,0:T(8,128)S(1)} %reshape.66.coupling, f32[4,2,128,128]{3,2,1,0:T(8,128)} %phase_one.1, f32[4,2,128,128]{3,2,1,0:T(8,128)} %phase_two.1, ...), custom_call_target="tpu_custom_call" | custom-call | tf_op jit(solution)/shard_map/pallas_call | solution.py:517
  8.6 3.9 %collective-permute-start.1 = (s16[592,128]{1,0:T(8,128)(2,1)S(1)}, s16[592,128]{1,0:T(8,128)(2,1)S(1)}, u32[]{:S(2)}, u32[]{:S(2)}) collective-permute-start(s16[592,128]{1,0:T(8,128)(2,1)S(1)} %get-tuple-element.65), channel_id=1, source_target_pairs={{0,16},{8,24},{16,0},{24,8},{32,48},{40,56},{48,32},{56,40},{64,80... | collective-permute-start | bytes 454664 | tf_op jit(solution)/shard_map/ppermute | solution.py:51
  12.5 2.2 %collective-permute-start.2 = (s16[592,128]{1,0:T(8,128)(2,1)S(1)}, s16[592,128]{1,0:T(8,128)(2,1)S(1)}, u32[]{:S(2)}, u32[]{:S(2)}) collective-permute-start(s16[592,128]{1,0:T(8,128)(2,1)S(1)} %get-tuple-element.66), channel_id=1, source_target_pairs={{0,24},{8,0},{16,8},{24,16},{32,56},{40,32},{48,40},{56,48},{64,88... | collective-permute-start | bytes 454664 | tf_op jit(solution)/shard_map/ppermute | solution.py:51
  15.2 6.1 %collective-permute-done.1.part2 = s16[592,128]{1,0:T(8,128)(2,1)S(1)} collective-permute-done((s16[592,128]{1,0:T(8,128)(2,1)S(1)}, s16[592,128]{1,0:T(8,128)(2,1)S(1)}, u32[]{:S(2)}, u32[]{:S(2)}) %collective-permute-start.1) | collective-permute-done | bytes 151584 | tf_op jit(solution)/shard_map/ppermute | solution.py:51
  26.8 4.3 %collective-permute-start.5 = (s16[592,128]{1,0:T(8,128)(2,1)S(1)}, s16[592,128]{1,0:T(8,128)(2,1)S(1)}, u32[]{:S(2)}, u32[]{:S(2)}) collective-permute-start(s16[592,128]{1,0:T(8,128)(2,1)S(1)} %get-tuple-element.73), channel_id=1, source_target_pairs={{32,64},{40,72},{48,80},{56,88},{64,32},{72,40},{80,48},{88,56},{3... | collective-permute-start | bytes 454664 | tf_op jit(solution)/shard_map/ppermute | solution.py:575
  31.2 2.2 %shard_map.132 = (f32[2,2,2,512,128]{4,3,2,1,0:T(8,128)S(1)}, bf16[4,2,256,256]{3,2,1,0:T(8,128)(2,1)S(1)}, bf16[18,512,256]{2,1,0:T(8,128)(2,1)S(1)}, bf16[4,512,256]{2,1,0:T(8,128)(2,1)S(1)}) custom-call(s16[4,592,128]{2,1,0:T(8,128)(2,1)S(1)} %get-tuple-element.71.region.refs_0_), custom_call_target="tpu_custom_call" | custom-call | tf_op jit(solution)/shard_map/pallas_call | solution.py:517
  39.3 4.0 %collective-permute-done.9.refs_5_.refs_7_ = s16[2,592,128]{2,1,0:T(8,128)(2,1)S(1)} collective-permute-done((s16[2,592,128]{2,1,0:T(8,128)(2,1)S(1)}, s16[2,592,128]{2,1,0:T(8,128)(2,1)S(1)}, u32[]{:S(2)}, u32[]{:S(2)}) %collective-permute-start.9) | collective-permute-done | bytes 303136 | tf_op jit(solution)/shard_map/ppermute | solution.py:569
  45.0 7.6 %shard_map.135 = (f32[2,2,2,512,128]{4,3,2,1,0:T(8,128)S(1)}, bf16[4,2,256,256]{3,2,1,0:T(8,128)(2,1)S(1)}, bf16[2,256,256]{2,1,0:T(8,128)(2,1)S(1)}, bf16[2,256,256]{2,1,0:T(8,128)(2,1)S(1)}) custom-call(s32[1,26]{1,0:T(1,128)S(1)} %bitcast.27, s32[120,128]{1,0:T(8,128)S(1)} %get-tuple-element.81.refs_1_, ...), custom_call_target="tpu_custom_call" | custom-call | flops 671088640 | bytes 16277504 | tf_op jit(solution)/shard_map/pallas_call | solution.py:517
  54.8 4.0 %collective-permute-start.13 = (bf16[2,256,256]{2,1,0:T(8,128)(2,1)S(1)}, bf16[2,256,256]{2,1,0:T(8,128)(2,1)S(1)}, u32[]{:S(2)}, u32[]{:S(2)}) collective-permute-start(bf16[2,256,256]{2,1,0:T(8,128)(2,1)S(1)} %get-tuple-element.88), channel_id=1, source_target_pairs={{32,64},{40,72},{48,80},{56,88},{64,32},{72,40},{80,48},{88,56},{3... | collective-permute-start | bytes 786440 | tf_op jit(solution)/shard_map/ppermute | solution.py:575
  58.8 5.0 %collective-permute-done.12 = bf16[2,256,256]{2,1,0:T(8,128)(2,1)S(1)} collective-permute-done((bf16[2,256,256]{2,1,0:T(8,128)(2,1)S(1)}, bf16[2,256,256]{2,1,0:T(8,128)(2,1)S(1)}, u32[]{:S(2)}, u32[]{:S(2)}) %collective-permute-start.12) | collective-permute-done | bytes 262176 | tf_op jit(solution)/shard_map/ppermute | solution.py:575
  68.1 4.8 %shard_map.136.refs_7_ = f32[2,2,2,512,128]{4,3,2,1,0:T(8,128)S(1)} custom-call(s32[1,26]{1,0:T(1,128)S(1)} %bitcast.28, s32[120,128]{1,0:T(8,128)S(1)} %get-tuple-element.81.refs_1_, bf16[4,2,256,256]{3,2,1,0:T(8,128)(2,1)S(1)} %get-tuple-element.86.refs_2_, bf16[2,2,256,256]{3,2,1,0:T(8,128)(2,1)S(1)} %pad_maximum_fusion.refs_3_, ...), custom_call_target="tpu_custom_call" | custom-call | flops 671088640 | bytes 14680064 | tf_op jit(solution)/shard_map/pallas_call | solution.py:517
  72.9 3.8 %collective-permute-done.14.refs_3_ = bf16[2,2,256,256]{3,2,1,0:T(8,128)(2,1)S(1)} collective-permute-done((bf16[2,2,256,256]{3,2,1,0:T(8,128)(2,1)S(1)}, bf16[2,2,256,256]{3,2,1,0:T(8,128)(2,1)S(1)}, u32[]{:S(2)}, u32[]{:S(2)}) %collective-permute-start.14) | collective-permute-done | bytes 524320 | tf_op jit(solution)/shard_map/ppermute | solution.py:569
  76.6 3.1 %shard_map.137 = (bf16[4,2,256,256]{3,2,1,0:T(8,128)(2,1)S(1)}, bf16[2,256,256]{2,1,0:T(8,128)(2,1)S(1)}, bf16[2,256,256]{2,1,0:T(8,128)(2,1)S(1)}, bf16[2,256,2...) custom-call(s32[1,26]{1,0:T(1,128)S(1)} %bitcast.29, ...), custom_call_target="tpu_custom_call" | custom-call | flops 671088640 | bytes 17825792 | tf_op jit(solution)/shard_map/pallas_call | solution.py:517
  80.2 4.4 %collective-permute-start.19 = (bf16[2,256,256]{2,1,0:T(8,128)(2,1)S(1)}, bf16[2,256,256]{2,1,0:T(8,128)(2,1)S(1)}, u32[]{:S(2)}, u32[]{:S(2)}) collective-permute-start(bf16[2,256,256]{2,1,0:T(8,128)(2,1)S(1)} %get-tuple-element.92), channel_id=1, source_target_pairs={{32,64},{40,72},{48,80},{56,88},{64,32},{72,40},{80,48},{88,56},{3... | collective-permute-start | bytes 786440 | tf_op jit(solution)/shard_map/ppermute | solution.py:575
  86.5 2.0 %collective-permute-done.18 = bf16[2,256,256]{2,1,0:T(8,128)(2,1)S(1)} collective-permute-done((bf16[2,256,256]{2,1,0:T(8,128)(2,1)S(1)}, bf16[2,256,256]{2,1,0:T(8,128)(2,1)S(1)}, u32[]{:S(2)}, u32[]{:S(2)}) %collective-permute-start.18) | collective-permute-done | bytes 262176 | tf_op jit(solution)/shard_map/ppermute | solution.py:575
  88.6 2.6 %collective-permute-done.19 = bf16[2,256,256]{2,1,0:T(8,128)(2,1)S(1)} collective-permute-done((bf16[2,256,256]{2,1,0:T(8,128)(2,1)S(1)}, bf16[2,256,256]{2,1,0:T(8,128)(2,1)S(1)}, u32[]{:S(2)}, u32[]{:S(2)}) %collective-permute-start.19) | collective-permute-done | bytes 262176 | tf_op jit(solution)/shard_map/ppermute | solution.py:575
  91.3 2.5 %collective-permute-start.20 = (bf16[2,2,256,256]{3,2,1,0:T(8,128)(2,1)S(1)}, bf16[2,2,256,256]{3,2,1,0:T(8,128)(2,1)S(1)}, u32[]{:S(2)}, u32[]{:S(2)}) collective-permute-start(bf16[2,2,256,256]{3,2,1,0:T(8,128)(2,1)S(1)} %pad_maximum_fusion.1.refs_3_), channel_id=1, source_target_pairs={{1,2},{3,4},{5,6},{2,1},{4,3},{6,5},{9,10},{11,12},{13,14},{10,9},... | collective-permute-start | bytes 1572872 | tf_op jit(solution)/shard_map/ppermute | solution.py:569
  94.3 3.6 %collective-permute-start.24 = (bf16[2,256,256]{2,1,0:T(8,128)(2,1)S(1)}, bf16[2,256,256]{2,1,0:T(8,128)(2,1)S(1)}, u32[]{:S(2)}, u32[]{:S(2)}) collective-permute-start(bf16[2,256,256]{2,1,0:T(8,128)(2,1)S(1)} %get-tuple-element.100), channel_id=1, source_target_pairs={{0,16},{8,24},{16,0},{24,8},{32,48},{40,56},{48,32},{56,40},{64,80... | collective-permute-start | bytes 786440 | tf_op jit(solution)/shard_map/ppermute | solution.py:51
  97.9 5.0 %shard_map.138.refs_7_ = f32[2,2,2,512,128]{4,3,2,1,0:T(8,128)S(1)} custom-call(s32[1,26]{1,0:T(1,128)S(1)} %bitcast.30, s32[120,128]{1,0:T(8,128)S(1)} %get-tuple-element.81.refs_1_, bf16[4,2,256,256]{3,2,1,0:T(8,128)(2,1)S(1)} %get-tuple-element.90.refs_2_, bf16[2,2,256,256]{3,2,1,0:T(8,128)(2,1)S(1)} %pad_maximum_fusion.1.refs_3_, ...), custom_call_target="tpu_custom_call" | custom-call | flops 671088640 | bytes 14680064 | tf_op jit(solution)/shard_map/pallas_call | solution.py:517
  102.9 3.4 %collective-permute-done.20.refs_3_ = bf16[2,2,256,256]{3,2,1,0:T(8,128)(2,1)S(1)} collective-permute-done((bf16[2,2,256,256]{3,2,1,0:T(8,128)(2,1)S(1)}, bf16[2,2,256,256]{3,2,1,0:T(8,128)(2,1)S(1)}, u32[]{:S(2)}, u32[]{:S(2)}) %collective-permute-start.20) | collective-permute-done | bytes 524320 | tf_op jit(solution)/shard_map/ppermute | solution.py:569
  106.3 3.1 %shard_map.139 = (bf16[2,256,256]{2,1,0:T(8,128)(2,1)S(1)}, bf16[2,256,256]{2,1,0:T(8,128)(2,1)S(1)}, bf16[2,256,256]{2,1,0:T(8,128)(2,1)S(1)}, bf16[2,256,256]{2,1,0:T(8,128)(2,1)S(1)}) custom-call(s32[1,26]{1,0:T(1,128)S(1)} %bitcast.31, s32[120,128]{1,0:T(8,128)S(1)} %get-tuple-element.81.refs_1_, ...), custom_call_target="tpu_custom_call" | custom-call | flops 671088640 | bytes 16252928 | tf_op jit(solution)/shard_map/pallas_call | solution.py:517
  110.5 3.8 %collective-permute-start.27 = (bf16[2,256,256]{2,1,0:T(8,128)(2,1)S(1)}, bf16[2,256,256]{2,1,0:T(8,128)(2,1)S(1)}, u32[]{:S(2)}, u32[]{:S(2)}) collective-permute-start(bf16[2,256,256]{2,1,0:T(8,128)(2,1)S(1)} %get-tuple-element.111), channel_id=1, source_target_pairs={{0,16},{8,24},{16,0},{24,8},{32,48},{40,56},{48,32},{56,40},{64,80... | collective-permute-start | bytes 786440 | tf_op jit(solution)/shard_map/ppermute | solution.py:51
  121.0 5.2 %collective-permute-done.27.refs_1_ = bf16[2,256,256]{2,1,0:T(8,128)(2,1)S(1)} collective-permute-done((bf16[2,256,256]{2,1,0:T(8,128)(2,1)S(1)}, bf16[2,256,256]{2,1,0:T(8,128)(2,1)S(1)}, u32[]{:S(2)}, u32[]{:S(2)}) %collective-permute-start.27) | collective-permute-done | bytes 262176 | tf_op jit(solution)/shard_map/ppermute | solution.py:51
  (57 shorter events, 36.7 us)
Async XLA Ops:
  1.9 19.5 %collective-permute-start.3 = (s16[1280,128]{1,0:T(8,128)(2,1)S(1)}, s16[1280,128]{1,0:T(8,128)(2,1)S(1)}, u32[]{:S(2)}, u32[]{:S(2)}) collective-permute-start(s16[1280,128]{1,0:T(8,128)(2,1)S(1)} %shard_map.130.own), channel_id=1, source_target_pairs={{0,8},{8,0},{16,24},{24,16},{32,40},{40,32},{48,56},{56,48},{64,72... | collective-permute-start | bytes 983048 | tf_op jit(solution)/shard_map/ppermute | solution.py:588
  8.6 12.7 %collective-permute-start.1 = (s16[592,128]{1,0:T(8,128)(2,1)S(1)}, s16[592,128]{1,0:T(8,128)(2,1)S(1)}, u32[]{:S(2)}, u32[]{:S(2)}) collective-permute-start(s16[592,128]{1,0:T(8,128)(2,1)S(1)} %get-tuple-element.65), channel_id=1, source_target_pairs={{0,16},{8,24},{16,0},{24,8},{32,48},{40,56},{48,32},{56,40},{64,80... | collective-permute-start | bytes 454664 | tf_op jit(solution)/shard_map/ppermute | solution.py:51
  12.5 8.9 %collective-permute-start.2 = (s16[592,128]{1,0:T(8,128)(2,1)S(1)}, s16[592,128]{1,0:T(8,128)(2,1)S(1)}, u32[]{:S(2)}, u32[]{:S(2)}) collective-permute-start(s16[592,128]{1,0:T(8,128)(2,1)S(1)} %get-tuple-element.66), channel_id=1, source_target_pairs={{0,24},{8,0},{16,8},{24,16},{32,56},{40,32},{48,40},{56,48},{64,88... | collective-permute-start | bytes 454664 | tf_op jit(solution)/shard_map/ppermute | solution.py:51
  21.4 17.0 %collective-permute-start.10 = (s16[2,1280,128]{2,1,0:T(8,128)(2,1)S(1)}, s16[2,1280,128]{2,1,0:T(8,128)(2,1)S(1)}, u32[]{:S(2)}, u32[]{:S(2)}) collective-permute-start(s16[2,1280,128]{2,1,0:T(8,128)(2,1)S(1)} %pad_add_fusion), channel_id=1, source_target_pairs={{0,24},{8,16},{16,8},{24,0},{32,56},{40,48},{48,40},{56,32},{64,88... | collective-permute-start | bytes 1966088 | tf_op jit(solution)/shard_map/ppermute | solution.py:588
  22.8 20.4 %collective-permute-start.8 = (s16[4,592,128]{2,1,0:T(8,128)(2,1)S(1)}, s16[4,592,128]{2,1,0:T(8,128)(2,1)S(1)}, u32[]{:S(2)}, u32[]{:S(2)}) collective-permute-start(s16[4,592,128]{2,1,0:T(8,128)(2,1)S(1)} %get-tuple-element.71.region.refs_0_), channel_id=1, source_target_pairs={{1,2},{3,4},{5,6},{2,1},{4,3},{6,5},{9,10},{11,12},{13,14},{10,9},... | collective-permute-start | bytes 1818632 | tf_op jit(solution)/shard_map/ppermute | solution.py:569
  24.7 18.5 %collective-permute-start.6 = (s16[4,592,128]{2,1,0:T(8,128)(2,1)S(1)}, s16[4,592,128]{2,1,0:T(8,128)(2,1)S(1)}, u32[]{:S(2)}, u32[]{:S(2)}) collective-permute-start(s16[4,592,128]{2,1,0:T(8,128)(2,1)S(1)} %get-tuple-element.71.region.refs_0_), channel_id=1, source_target_pairs={{0,1},{2,3},{4,5},{6,7},{1,0},{3,2},{5,4},{7,6},{8,9},{10,11},{12,... | collective-permute-start | bytes 1818632 | tf_op jit(solution)/shard_map/ppermute | solution.py:569
  26.8 8.2 %collective-permute-start.5 = (s16[592,128]{1,0:T(8,128)(2,1)S(1)}, s16[592,128]{1,0:T(8,128)(2,1)S(1)}, u32[]{:S(2)}, u32[]{:S(2)}) collective-permute-start(s16[592,128]{1,0:T(8,128)(2,1)S(1)} %get-tuple-element.73), channel_id=1, source_target_pairs={{32,64},{40,72},{48,80},{56,88},{64,32},{72,40},{80,48},{88,56},{3... | collective-permute-start | bytes 454664 | tf_op jit(solution)/shard_map/ppermute | solution.py:575
  35.1 8.1 %collective-permute-start.9 = (s16[2,592,128]{2,1,0:T(8,128)(2,1)S(1)}, s16[2,592,128]{2,1,0:T(8,128)(2,1)S(1)}, u32[]{:S(2)}, u32[]{:S(2)}) collective-permute-start(s16[2,592,128]{2,1,0:T(8,128)(2,1)S(1)} %pad_add_fusion.1.refs_1_.refs_3_), channel_id=1, source_target_pairs={{1,2},{3,4},{5,6},{2,1},{4,3},{6,5},{9,10},{11,12},{13,14},{10,9},... | collective-permute-start | bytes 909320 | tf_op jit(solution)/shard_map/ppermute | solution.py:569
  52.6 15.5 %collective-permute-start.15 = (bf16[4,2,256,256]{3,2,1,0:T(8,128)(2,1)S(1)}, bf16[4,2,256,256]{3,2,1,0:T(8,128)(2,1)S(1)}, u32[]{:S(2)}, u32[]{:S(2)}) collective-permute-start(bf16[4,2,256,256]{3,2,1,0:T(8,128)(2,1)S(1)} %get-tuple-element.86.refs_2_), channel_id=1, source_target_pairs={{0,1},{2,3},{4,5},{6,7},{1,0},{3,2},{5,4},{7,6},{8,9},{10,11},{12,... | collective-permute-start | bytes 3145736 | tf_op jit(solution)/shard_map/ppermute | solution.py:569
  52.7 23.9 %collective-permute-start.11 = (bf16[4,2,256,256]{3,2,1,0:T(8,128)(2,1)S(1)}, bf16[4,2,256,256]{3,2,1,0:T(8,128)(2,1)S(1)}, u32[]{:S(2)}, u32[]{:S(2)}) collective-permute-start(bf16[4,2,256,256]{3,2,1,0:T(8,128)(2,1)S(1)} %get-tuple-element.86.refs_2_), channel_id=1, source_target_pairs={{1,2},{3,4},{5,6},{2,1},{4,3},{6,5},{9,10},{11,12},{13,14},{10,9},... | collective-permute-start | bytes 3145736 | tf_op jit(solution)/shard_map/ppermute | solution.py:569
  54.7 9.1 %collective-permute-start.12 = (bf16[2,256,256]{2,1,0:T(8,128)(2,1)S(1)}, bf16[2,256,256]{2,1,0:T(8,128)(2,1)S(1)}, u32[]{:S(2)}, u32[]{:S(2)}) collective-permute-start(bf16[2,256,256]{2,1,0:T(8,128)(2,1)S(1)} %get-tuple-element.87), channel_id=1, source_target_pairs={{0,32},{8,40},{16,48},{24,56},{64,96},{72,104},{80,112},{88,120},{... | collective-permute-start | bytes 786440 | tf_op jit(solution)/shard_map/ppermute | solution.py:575
  54.8 10.8 %collective-permute-start.13 = (bf16[2,256,256]{2,1,0:T(8,128)(2,1)S(1)}, bf16[2,256,256]{2,1,0:T(8,128)(2,1)S(1)}, u32[]{:S(2)}, u32[]{:S(2)}) collective-permute-start(bf16[2,256,256]{2,1,0:T(8,128)(2,1)S(1)} %get-tuple-element.88), channel_id=1, source_target_pairs={{32,64},{40,72},{48,80},{56,88},{64,32},{72,40},{80,48},{88,56},{3... | collective-permute-start | bytes 786440 | tf_op jit(solution)/shard_map/ppermute | solution.py:575
  66.2 10.5 %collective-permute-start.14 = (bf16[2,2,256,256]{3,2,1,0:T(8,128)(2,1)S(1)}, bf16[2,2,256,256]{3,2,1,0:T(8,128)(2,1)S(1)}, u32[]{:S(2)}, u32[]{:S(2)}) collective-permute-start(bf16[2,2,256,256]{3,2,1,0:T(8,128)(2,1)S(1)} %pad_maximum_fusion.refs_3_), channel_id=1, source_target_pairs={{1,2},{3,4},{5,6},{2,1},{4,3},{6,5},{9,10},{11,12},{13,14},{10,9},... | collective-permute-start | bytes 1572872 | tf_op jit(solution)/shard_map/ppermute | solution.py:569
  79.7 18.2 %collective-permute-start.21 = (bf16[4,2,256,256]{3,2,1,0:T(8,128)(2,1)S(1)}, bf16[4,2,256,256]{3,2,1,0:T(8,128)(2,1)S(1)}, u32[]{:S(2)}, u32[]{:S(2)}) collective-permute-start(bf16[4,2,256,256]{3,2,1,0:T(8,128)(2,1)S(1)} %get-tuple-element.90.refs_2_), channel_id=1, source_target_pairs={{0,1},{2,3},{4,5},{6,7},{1,0},{3,2},{5,4},{7,6},{8,9},{10,11},{12,... | collective-permute-start | bytes 3145736 | tf_op jit(solution)/shard_map/ppermute | solution.py:569
  80.2 8.3 %collective-permute-start.18 = (bf16[2,256,256]{2,1,0:T(8,128)(2,1)S(1)}, bf16[2,256,256]{2,1,0:T(8,128)(2,1)S(1)}, u32[]{:S(2)}, u32[]{:S(2)}) collective-permute-start(bf16[2,256,256]{2,1,0:T(8,128)(2,1)S(1)} %get-tuple-element.91), channel_id=1, source_target_pairs={{0,32},{8,40},{16,48},{24,56},{64,96},{72,104},{80,112},{88,120},{... | collective-permute-start | bytes 786440 | tf_op jit(solution)/shard_map/ppermute | solution.py:575
  80.2 10.9 %collective-permute-start.19 = (bf16[2,256,256]{2,1,0:T(8,128)(2,1)S(1)}, bf16[2,256,256]{2,1,0:T(8,128)(2,1)S(1)}, u32[]{:S(2)}, u32[]{:S(2)}) collective-permute-start(bf16[2,256,256]{2,1,0:T(8,128)(2,1)S(1)} %get-tuple-element.92), channel_id=1, source_target_pairs={{32,64},{40,72},{48,80},{56,88},{64,32},{72,40},{80,48},{88,56},{3... | collective-permute-start | bytes 786440 | tf_op jit(solution)/shard_map/ppermute | solution.py:575
  84.6 21.7 %collective-permute-start.17 = (bf16[4,2,256,256]{3,2,1,0:T(8,128)(2,1)S(1)}, bf16[4,2,256,256]{3,2,1,0:T(8,128)(2,1)S(1)}, u32[]{:S(2)}, u32[]{:S(2)}) collective-permute-start(bf16[4,2,256,256]{3,2,1,0:T(8,128)(2,1)S(1)} %get-tuple-element.90.refs_2_), channel_id=1, source_target_pairs={{1,2},{3,4},{5,6},{2,1},{4,3},{6,5},{9,10},{11,12},{13,14},{10,9},... | collective-permute-start | bytes 3145736 | tf_op jit(solution)/shard_map/ppermute | solution.py:569
  91.3 15.0 %collective-permute-start.20 = (bf16[2,2,256,256]{3,2,1,0:T(8,128)(2,1)S(1)}, bf16[2,2,256,256]{3,2,1,0:T(8,128)(2,1)S(1)}, u32[]{:S(2)}, u32[]{:S(2)}) collective-permute-start(bf16[2,2,256,256]{3,2,1,0:T(8,128)(2,1)S(1)} %pad_maximum_fusion.1.refs_3_), channel_id=1, source_target_pairs={{1,2},{3,4},{5,6},{2,1},{4,3},{6,5},{9,10},{11,12},{13,14},{10,9},... | collective-permute-start | bytes 1572872 | tf_op jit(solution)/shard_map/ppermute | solution.py:569
  93.8 15.7 %collective-permute-start.23 = (bf16[2,256,256]{2,1,0:T(8,128)(2,1)S(1)}, bf16[2,256,256]{2,1,0:T(8,128)(2,1)S(1)}, u32[]{:S(2)}, u32[]{:S(2)}) collective-permute-start(bf16[2,256,256]{2,1,0:T(8,128)(2,1)S(1)} %get-tuple-element.99), channel_id=1, source_target_pairs={{0,8},{8,16},{16,24},{24,0},{32,40},{40,48},{48,56},{56,32},{64,72... | collective-permute-start | bytes 786440 | tf_op jit(solution)/shard_map/ppermute | solution.py:51
  94.3 16.0 %collective-permute-start.24 = (bf16[2,256,256]{2,1,0:T(8,128)(2,1)S(1)}, bf16[2,256,256]{2,1,0:T(8,128)(2,1)S(1)}, u32[]{:S(2)}, u32[]{:S(2)}) collective-permute-start(bf16[2,256,256]{2,1,0:T(8,128)(2,1)S(1)} %get-tuple-element.100), channel_id=1, source_target_pairs={{0,16},{8,24},{16,0},{24,8},{32,48},{40,56},{48,32},{56,40},{64,80... | collective-permute-start | bytes 786440 | tf_op jit(solution)/shard_map/ppermute | solution.py:51
  97.9 12.4 %collective-permute-start.25 = (bf16[2,256,256]{2,1,0:T(8,128)(2,1)S(1)}, bf16[2,256,256]{2,1,0:T(8,128)(2,1)S(1)}, u32[]{:S(2)}, u32[]{:S(2)}) collective-permute-start(bf16[2,256,256]{2,1,0:T(8,128)(2,1)S(1)} %get-tuple-element.101), channel_id=1, source_target_pairs={{0,24},{8,0},{16,8},{24,16},{32,56},{40,32},{48,40},{56,48},{64,88... | collective-permute-start | bytes 786440 | tf_op jit(solution)/shard_map/ppermute | solution.py:51
  110.4 9.2 %collective-permute-start.28 = (bf16[2,256,256]{2,1,0:T(8,128)(2,1)S(1)}, bf16[2,256,256]{2,1,0:T(8,128)(2,1)S(1)}, u32[]{:S(2)}, u32[]{:S(2)}) collective-permute-start(bf16[2,256,256]{2,1,0:T(8,128)(2,1)S(1)} %get-tuple-element.112), channel_id=1, source_target_pairs={{0,8},{8,16},{16,24},{24,0},{32,40},{40,48},{48,56},{56,32},{64,72... | collective-permute-start | bytes 786440 | tf_op jit(solution)/shard_map/ppermute | solution.py:51
  110.5 15.7 %collective-permute-start.27 = (bf16[2,256,256]{2,1,0:T(8,128)(2,1)S(1)}, bf16[2,256,256]{2,1,0:T(8,128)(2,1)S(1)}, u32[]{:S(2)}, u32[]{:S(2)}) collective-permute-start(bf16[2,256,256]{2,1,0:T(8,128)(2,1)S(1)} %get-tuple-element.111), channel_id=1, source_target_pairs={{0,16},{8,24},{16,0},{24,8},{32,48},{40,56},{48,32},{56,40},{64,80... | collective-permute-start | bytes 786440 | tf_op jit(solution)/shard_map/ppermute | solution.py:51
  114.3 13.2 %collective-permute-start.26 = (bf16[2,256,256]{2,1,0:T(8,128)(2,1)S(1)}, bf16[2,256,256]{2,1,0:T(8,128)(2,1)S(1)}, u32[]{:S(2)}, u32[]{:S(2)}) collective-permute-start(bf16[2,256,256]{2,1,0:T(8,128)(2,1)S(1)} %get-tuple-element.110), channel_id=1, source_target_pairs={{0,24},{8,0},{16,8},{24,16},{32,56},{40,32},{48,40},{56,48},{64,88... | collective-permute-start | bytes 786440 | tf_op jit(solution)/shard_map/ppermute | solution.py:51
  (5 other events, 25.5 us)

commit v3 on v2

--- a/solution.py
+++ b/solution.py
@@ -196,17 +196,49 @@
         bd2[n, 256:512, :] = spread(place, low, mask2)
 
 
-def build_kernel(flags, *refs):
+def near_kernel(flags, own, ends, near, near_ends, bd1_in, ops_in, bd1, ops):
+    block = neighbourhood(own, ends, near, near_ends, None, None)
+    for side in (OWN, NEAR):
+        for row in SLOTS if side == OWN else ROWS:
+            coupling_tables(block(row, side), row_of(flags, row) * 3 + column_of(flags, side), bd1)
+    lane = lane_iota((T, T), 1)
+    for layer in range(2):
+        ops[layer, 5, 0 : RING * T - 1, :] = ops[layer, 1, 1 : RING * T, :]
+        below = [bond_edge(block(slot, OWN), ROW_EDGE + layer) for slot in SLOTS]
+        ops[layer, 5, RING * T - 1 : RING * T, :] = jnp.where(
+            jnp.broadcast_to(flags[0, 7], (1, T)) == HALO - 1, below[0], below[1]
+        )
+        for r in range(RING):
+            column = jnp.broadcast_to(bond_edge(near.at[r], COL_EDGE + layer), (T, T)).T
+            ops[layer, 6, rows_of(r), :] = jnp.where(
+                lane == T - 1, column, pltpu.roll(ops[layer, 2, rows_of(r), :], T - 1, 1)
+            )
+
+
+def bond_edge(ref, row):
+    words = decoded(ref[PHASE_ROWS + 64 : PHASE_ROWS + 80, :])
+    return words[row - 64 : row - 63, :] * HOP_UNIT + HOP_MID
+
+
+def cross_kernel(flags, *refs):
     idx, bd1, ops, codes = refs[8:]
     block = neighbourhood(*refs[:6])
+    for row in ROWS:
+        coupling_tables(block(row, CROSS), row_of(flags, row) * 3 + column_of(flags, CROSS), bd1)
+    lane = lane_iota((T, T), 1)
+    is_right = flags[0, 3] == 2
+    for layer in range(2):
+        for r in range(RING):
+            column = jnp.broadcast_to(bond_edge(block(r + 1, CROSS), COL_EDGE + layer), (T, T)).T
+            ops[layer, 6, rows_of(r), :] = jnp.where(
+                (lane == T - 1) & is_right, column, ops[layer, 6, rows_of(r), :]
+            )
+
     codes[...] = jnp.zeros_like(codes)
     for side in (OWN, CROSS, NEAR):
         for row in ROWS:
             home = row_of(flags, row) * 3 + column_of(flags, side)
-            ref = block(row, side)
-            if side != OWN or row in SLOTS:
-                coupling_tables(ref, home, bd1)
-            words = ref[PHASE_ROWS + 64 : PHASE_ROWS + 80, :].astype(jnp.int32)
+            words = block(row, side)[PHASE_ROWS + 64 : PHASE_ROWS + 80, :].astype(jnp.int32)
             codes[0, pl.ds(home, 1), :] = words[CODE - 64 : CODE - 63, :]
             codes[1, pl.ds(home, 1), :] = words[AT - 64 : AT - 63, :]
 
@@ -228,25 +260,6 @@
         hit = jnp.where(source == n, 1.0, 0.0)
         used = jnp.max(jnp.max(hit, axis=1, keepdims=True), axis=0, keepdims=True)
         idx[USED + n : USED + n + 1, :] = jnp.broadcast_to(used, (1, T)).astype(jnp.int32)
-
-    lane = lane_iota((T, T), 1)
-
-    def edge(ref, row):
-        words = decoded(ref[PHASE_ROWS + 64 : PHASE_ROWS + 80, :])
-        return words[row - 64 : row - 63, :] * HOP_UNIT + HOP_MID
-
-    for layer in range(2):
-        ops[layer, 5, 0 : RING * T - 1, :] = ops[layer, 1, 1 : RING * T, :]
-        below = [edge(block(slot, OWN), ROW_EDGE + layer) for slot in SLOTS]
-        ops[layer, 5, RING * T - 1 : RING * T, :] = jnp.where(
-            jnp.broadcast_to(flags[0, 7], (1, T)) == HALO - 1, below[0], below[1]
-        )
-        for r in range(RING):
-            rows = slice(r * T, (r + 1) * T)
-            far, close = [edge(block(r + 1, side), COL_EDGE + layer) for side in (CROSS, NEAR)]
-            right = jnp.where(jnp.broadcast_to(flags[0, 3], (1, T)) == 2, far, close)
-            column = jnp.broadcast_to(right, (T, T)).T
-            ops[layer, 6, rows, :] = jnp.where(lane == T - 1, column, pltpu.roll(ops[layer, 2, rows, :], T - 1, 1))
 
 
 def cos_sin(code):
@@ -648,11 +661,12 @@
     )
     other = ring_swapped(packed, (1, 0, 3, 2))
     parts, other = lax.optimization_barrier((parts, other))
-    packs = (packed, other, ring_swapped(jnp.stack([packed, other]), (3, 2, 1, 0)))
 
     region = local(
         region_kernel, (jax.ShapeDtypeStruct((RING, CARGO, T), I16), cargo, cargo), (flags,), *parts
     )
+    region, both = lax.optimization_barrier((region, jnp.stack([packed, other])))
+    packs = (packed, other, ring_swapped(both, (3, 2, 1, 0)))
     table = jax.ShapeDtypeStruct((HOMES, 512, 256), BF16)
     early = local(
         zero_kernel, (WIDE, NARROW, table, jax.ShapeDtypeStruct((RING, 512, 256), BF16)), (), region[0]
@@ -660,8 +674,9 @@
     halo, (zero, zero_narrow, bd1, bd2) = halo_of(*region, early)
     ops_shape = jax.ShapeDtypeStruct((2, 7, RING * T, T), F32)
     ops = local(operators_kernel, ops_shape, (flags,), *packs)
+    bd1, ops = local(near_kernel, (table, ops_shape), (flags,), *halo[:4], bd1, ops, alias={5: 0, 6: 1})
     idx, bd1, ops = local(
-        build_kernel,
+        cross_kernel,
         (jax.ShapeDtypeStruct((IDX_ROWS, T), jnp.int32), table, ops_shape),
         (flags,),
         *halo,

time: 130 us -> 129 us (level)
  starting transfers between devices: 46.6 us -> 42.7 us
  waiting for transfers between devices: 37.8 us -> 39.9 us
    ppermute x12, waiting for transfers between devices: 11.2 us -> 8.95 us  [across(): return lax.ppermute(array, 'gy', pairs + [(j, i) for i, j in pairs])]
    ppermute x6, waiting for transfers between devices: 13.2 us -> 15.3 us  [swapped_rows(): return lax.ppermute(array, 'gx', pairs + [(j, i) for i, j in pairs])]
    ppermute x6, starting transfers between devices: 13.2 us -> 11.1 us  [swapped_rows(): return lax.ppermute(array, 'gx', pairs + [(j, i) for i, j in pairs])]
    ppermute x2, waiting for transfers between devices: 0.01 us -> 1.84 us  [ring_swapped(): return lax.ppermute(array, 'gx', pairs)]
    ppermute x12, starting transfers between devices: 16.3 us -> 14.5 us  [across(): return lax.ppermute(array, 'gy', pairs + [(j, i) for i, j in pairs])]
    pallas_call x11 -> x12, Pallas kernels: 32.3 us -> 33 us  [local(): pl.pallas_call(kernel, out_shape=out_shape, in_specs=[SMEM] * len(scalars...]
  transfers between devices with their start and end apart: 29 -> 29, of which waited for: 13 -> 14; matrix products, arithmetic and copies ran while one was open for 2% -> 2% of each run, Pallas kernels for 20% -> 21%
where the time goes in v3:
time: 129 us; the launch traced here: 128 us
  starting transfers between devices  42.7 us (33%)
  Pallas kernels  41.6 us (32%)
  waiting for transfers between devices  39.9 us (31%)
  local copies, waits for them, and re-layouts  1.89 us (1%)
  between operations  1.77 us (1%)
    pallas_call x12, Pallas kernels, local(): pl.pallas_call(kernel, out_shape=out_shape, in_specs=[SMEM] * len(scalars...  33 us
    ppermute x6, waiting for transfers between devices, swapped_rows(): return lax.ppermute(array, 'gx', pairs + [(j, i) for i, j in pairs])  15.3 us
    ppermute x12, starting transfers between devices, across(): return lax.ppermute(array, 'gy', pairs + [(j, i) for i, j in pairs])  14.5 us
    ppermute x9, starting transfers between devices, ring_moved(): return lax.ppermute(array, 'gx', pairs)  14.3 us
    ppermute x9, waiting for transfers between devices, ring_moved(): return lax.ppermute(array, 'gx', pairs)  13.8 us
    ppermute x6, starting transfers between devices, swapped_rows(): return lax.ppermute(array, 'gx', pairs + [(j, i) for i, j in pairs])  11.1 us
    ppermute x12, waiting for transfers between devices, across(): return lax.ppermute(array, 'gy', pairs + [(j, i) for i, j in pairs])  8.95 us
    pallas_call x6, Pallas kernels, written(): pl.pallas_call(lambda *refs: result_kernel(shifts, *refs), out_shape=(jax...  8.57 us
  transfers between devices with their start and end apart: 29, of which 14 were waited for; matrix products, arithmetic and copies ran while one was open for 2% of the time, Pallas kernels for 21%

profile of v3, /device:TPU:10, one launch (start us, length us, event | category | flops | bytes accessed | tf_op | source)
XLA Modules:
  0.0 128.0 jit_solution(10106354567317425984)
XLA Ops:
  6.4 2.0 %shard_map.129 = (s16[592,128]{1,0:T(8,128)(2,1)S(1)}, s16[592,128]{1,0:T(8,128)(2,1)S(1)}, s16[592,128]{1,0:T(8,128)(2,1)S(1)}, s16[592,128]{1,0:T(8,128)(2,1)S(1)}) custom-call(s32[1,26]{1,0:T(1,128)S(1)} %bitcast.23, f32[256,32]{1,0:T(8,128)S(1)} %reshape.66.coupling, f32[4,2,128,128]{3,2,1,0:T(8,128)} %phase_one.1, f32[4,2,128,128]{3,2,1,0:T(8,128)} %phase_two.1, ...), custom_call_target="tpu_custom_call" | custom-call | tf_op jit(solution)/shard_map/pallas_call | solution.py:530
  8.6 3.9 %collective-permute-start.1 = (s16[592,128]{1,0:T(8,128)(2,1)S(1)}, s16[592,128]{1,0:T(8,128)(2,1)S(1)}, u32[]{:S(2)}, u32[]{:S(2)}) collective-permute-start(s16[592,128]{1,0:T(8,128)(2,1)S(1)} %get-tuple-element.71), channel_id=1, source_target_pairs={{0,16},{8,24},{16,0},{24,8},{32,48},{40,56},{48,32},{56,40},{64,80... | collective-permute-start | bytes 454664 | tf_op jit(solution)/shard_map/ppermute | solution.py:51
  12.5 2.2 %collective-permute-start.2 = (s16[592,128]{1,0:T(8,128)(2,1)S(1)}, s16[592,128]{1,0:T(8,128)(2,1)S(1)}, u32[]{:S(2)}, u32[]{:S(2)}) collective-permute-start(s16[592,128]{1,0:T(8,128)(2,1)S(1)} %get-tuple-element.72), channel_id=1, source_target_pairs={{0,24},{8,0},{16,8},{24,16},{32,56},{40,32},{48,40},{56,48},{64,88... | collective-permute-start | bytes 454664 | tf_op jit(solution)/shard_map/ppermute | solution.py:51
  15.2 6.1 %collective-permute-done.1.part2 = s16[592,128]{1,0:T(8,128)(2,1)S(1)} collective-permute-done((s16[592,128]{1,0:T(8,128)(2,1)S(1)}, s16[592,128]{1,0:T(8,128)(2,1)S(1)}, u32[]{:S(2)}, u32[]{:S(2)}) %collective-permute-start.1) | collective-permute-done | bytes 151584 | tf_op jit(solution)/shard_map/ppermute | solution.py:51
  22.8 2.5 %collective-permute-start.8 = (s16[4,592,128]{2,1,0:T(8,128)(2,1)S(1)}, s16[4,592,128]{2,1,0:T(8,128)(2,1)S(1)}, u32[]{:S(2)}, u32[]{:S(2)}) collective-permute-start(s16[4,592,128]{2,1,0:T(8,128)(2,1)S(1)} %get-tuple-element.81.region.own.refs_0_), channel_id=1, source_target_pairs={{1,2},{3,4},{5,6},{2,1},{4,3},{6,5},{9,10},{11,12},{13,14},{10,9},... | collective-permute-start | bytes 1818632 | tf_op jit(solution)/shard_map/ppermute | solution.py:582
  25.9 4.3 %collective-permute-start.5 = (s16[592,128]{1,0:T(8,128)(2,1)S(1)}, s16[592,128]{1,0:T(8,128)(2,1)S(1)}, u32[]{:S(2)}, u32[]{:S(2)}) collective-permute-start(s16[592,128]{1,0:T(8,128)(2,1)S(1)} %get-tuple-element.83), channel_id=1, source_target_pairs={{32,64},{40,72},{48,80},{56,88},{64,32},{72,40},{80,48},{88,56},{3... | collective-permute-start | bytes 454664 | tf_op jit(solution)/shard_map/ppermute | solution.py:588
  30.2 2.2 %shard_map.132 = (f32[2,2,2,512,128]{4,3,2,1,0:T(8,128)S(1)}, bf16[4,2,256,256]{3,2,1,0:T(8,128)(2,1)S(1)}, bf16[18,512,256]{2,1,0:T(8,128)(2,1)S(1)}, bf16[4,512,256]{2,1,0:T(8,128)(2,1)S(1)}) custom-call(s16[4,592,128]{2,1,0:T(8,128)(2,1)S(1)} %get-tuple-element.81.region.own.refs_0_), custom_call_target="tpu_custom_call" | custom-call | tf_op jit(solution)/shard_map/pallas_call | solution.py:530
  32.4 2.6 %collective-permute-done.5 = s16[592,128]{1,0:T(8,128)(2,1)S(1)} collective-permute-done((s16[592,128]{1,0:T(8,128)(2,1)S(1)}, s16[592,128]{1,0:T(8,128)(2,1)S(1)}, u32[]{:S(2)}, u32[]{:S(2)}) %collective-permute-start.5) | collective-permute-done | bytes 151584 | tf_op jit(solution)/shard_map/ppermute | solution.py:588
  41.1 2.2 %collective-permute-done.9.refs_5_.refs_7_ = s16[2,592,128]{2,1,0:T(8,128)(2,1)S(1)} collective-permute-done((s16[2,592,128]{2,1,0:T(8,128)(2,1)S(1)}, s16[2,592,128]{2,1,0:T(8,128)(2,1)S(1)}, u32[]{:S(2)}, u32[]{:S(2)}) %collective-permute-start.9) | collective-permute-done | bytes 303136 | tf_op jit(solution)/shard_map/ppermute | solution.py:582
  44.5 7.8 %shard_map.136 = (f32[2,2,2,512,128]{4,3,2,1,0:T(8,128)S(1)}, bf16[4,2,256,256]{3,2,1,0:T(8,128)(2,1)S(1)}, bf16[2,256,256]{2,1,0:T(8,128)(2,1)S(1)}, bf16[2,256,256]{2,1,0:T(8,128)(2,1)S(1)}) custom-call(s32[1,26]{1,0:T(1,128)S(1)} %bitcast.28, s32[120,128]{1,0:T(8,128)S(1)} %get-tuple-element.93.refs_1_, ...), custom_call_target="tpu_custom_call" | custom-call | flops 671088640 | bytes 16277504 | tf_op jit(solution)/shard_map/pallas_call | solution.py:530
  54.6 3.3 %collective-permute-start.13 = (bf16[2,256,256]{2,1,0:T(8,128)(2,1)S(1)}, bf16[2,256,256]{2,1,0:T(8,128)(2,1)S(1)}, u32[]{:S(2)}, u32[]{:S(2)}) collective-permute-start(bf16[2,256,256]{2,1,0:T(8,128)(2,1)S(1)} %get-tuple-element.100), channel_id=1, source_target_pairs={{32,64},{40,72},{48,80},{56,88},{64,32},{72,40},{80,48},{88,56},{3... | collective-permute-start | bytes 786440 | tf_op jit(solution)/shard_map/ppermute | solution.py:588
  57.9 5.5 %collective-permute-done.12 = bf16[2,256,256]{2,1,0:T(8,128)(2,1)S(1)} collective-permute-done((bf16[2,256,256]{2,1,0:T(8,128)(2,1)S(1)}, bf16[2,256,256]{2,1,0:T(8,128)(2,1)S(1)}, u32[]{:S(2)}, u32[]{:S(2)}) %collective-permute-start.12) | collective-permute-done | bytes 262176 | tf_op jit(solution)/shard_map/ppermute | solution.py:588
  67.9 4.8 %shard_map.137.refs_7_ = f32[2,2,2,512,128]{4,3,2,1,0:T(8,128)S(1)} custom-call(s32[1,26]{1,0:T(1,128)S(1)} %bitcast.29, s32[120,128]{1,0:T(8,128)S(1)} %get-tuple-element.93.refs_1_, bf16[4,2,256,256]{3,2,1,0:T(8,128)(2,1)S(1)} %get-tuple-element.98.refs_2_, bf16[2,2,256,256]{3,2,1,0:T(8,128)(2,1)S(1)} %pad_maximum_fusion.refs_3_, ...), custom_call_target="tpu_custom_call" | custom-call | flops 671088640 | bytes 14680064 | tf_op jit(solution)/shard_map/pallas_call | solution.py:530
  72.7 3.8 %collective-permute-done.14.refs_3_ = bf16[2,2,256,256]{3,2,1,0:T(8,128)(2,1)S(1)} collective-permute-done((bf16[2,2,256,256]{3,2,1,0:T(8,128)(2,1)S(1)}, bf16[2,2,256,256]{3,2,1,0:T(8,128)(2,1)S(1)}, u32[]{:S(2)}, u32[]{:S(2)}) %collective-permute-start.14) | collective-permute-done | bytes 524320 | tf_op jit(solution)/shard_map/ppermute | solution.py:582
  76.5 3.1 %shard_map.138 = (bf16[4,2,256,256]{3,2,1,0:T(8,128)(2,1)S(1)}, bf16[2,256,256]{2,1,0:T(8,128)(2,1)S(1)}, bf16[2,256,256]{2,1,0:T(8,128)(2,1)S(1)}, bf16[2,256,2...) custom-call(s32[1,26]{1,0:T(1,128)S(1)} %bitcast.30, ...), custom_call_target="tpu_custom_call" | custom-call | flops 671088640 | bytes 17825792 | tf_op jit(solution)/shard_map/pallas_call | solution.py:530
  80.4 2.9 %collective-permute-start.19 = (bf16[2,256,256]{2,1,0:T(8,128)(2,1)S(1)}, bf16[2,256,256]{2,1,0:T(8,128)(2,1)S(1)}, u32[]{:S(2)}, u32[]{:S(2)}) collective-permute-start(bf16[2,256,256]{2,1,0:T(8,128)(2,1)S(1)} %get-tuple-element.104), channel_id=1, source_target_pairs={{32,64},{40,72},{48,80},{56,88},{64,32},{72,40},{80,48},{88,56},{3... | collective-permute-start | bytes 786440 | tf_op jit(solution)/shard_map/ppermute | solution.py:588
  85.2 3.4 %collective-permute-done.18 = bf16[2,256,256]{2,1,0:T(8,128)(2,1)S(1)} collective-permute-done((bf16[2,256,256]{2,1,0:T(8,128)(2,1)S(1)}, bf16[2,256,256]{2,1,0:T(8,128)(2,1)S(1)}, u32[]{:S(2)}, u32[]{:S(2)}) %collective-permute-start.18) | collective-permute-done | bytes 262176 | tf_op jit(solution)/shard_map/ppermute | solution.py:588
  90.7 2.3 %collective-permute-start.20 = (bf16[2,2,256,256]{3,2,1,0:T(8,128)(2,1)S(1)}, bf16[2,2,256,256]{3,2,1,0:T(8,128)(2,1)S(1)}, u32[]{:S(2)}, u32[]{:S(2)}) collective-permute-start(bf16[2,2,256,256]{3,2,1,0:T(8,128)(2,1)S(1)} %pad_maximum_fusion.1.refs_3_), channel_id=1, source_target_pairs={{1,2},{3,4},{5,6},{2,1},{4,3},{6,5},{9,10},{11,12},{13,14},{10,9},... | collective-permute-start | bytes 1572872 | tf_op jit(solution)/shard_map/ppermute | solution.py:582
  93.6 3.5 %collective-permute-start.24 = (bf16[2,256,256]{2,1,0:T(8,128)(2,1)S(1)}, bf16[2,256,256]{2,1,0:T(8,128)(2,1)S(1)}, u32[]{:S(2)}, u32[]{:S(2)}) collective-permute-start(bf16[2,256,256]{2,1,0:T(8,128)(2,1)S(1)} %get-tuple-element.112), channel_id=1, source_target_pairs={{0,16},{8,24},{16,0},{24,8},{32,48},{40,56},{48,32},{56,40},{64,80... | collective-permute-start | bytes 786440 | tf_op jit(solution)/shard_map/ppermute | solution.py:51
  97.1 5.0 %shard_map.139.refs_7_ = f32[2,2,2,512,128]{4,3,2,1,0:T(8,128)S(1)} custom-call(s32[1,26]{1,0:T(1,128)S(1)} %bitcast.31, s32[120,128]{1,0:T(8,128)S(1)} %get-tuple-element.93.refs_1_, bf16[4,2,256,256]{3,2,1,0:T(8,128)(2,1)S(1)} %get-tuple-element.102.refs_2_, bf16[2,2,256,256]{3,2,1,0:T(8,128)(2,1)S(1)} %pad_maximum_fusion.1.refs_3_, ...), custom_call_target="tpu_custom_call" | custom-call | flops 671088640 | bytes 14680064 | tf_op jit(solution)/shard_map/pallas_call | solution.py:530
  102.1 3.0 %collective-permute-done.20.refs_3_ = bf16[2,2,256,256]{3,2,1,0:T(8,128)(2,1)S(1)} collective-permute-done((bf16[2,2,256,256]{3,2,1,0:T(8,128)(2,1)S(1)}, bf16[2,2,256,256]{3,2,1,0:T(8,128)(2,1)S(1)}, u32[]{:S(2)}, u32[]{:S(2)}) %collective-permute-start.20) | collective-permute-done | bytes 524320 | tf_op jit(solution)/shard_map/ppermute | solution.py:582
  105.0 3.1 %shard_map.140 = (bf16[2,256,256]{2,1,0:T(8,128)(2,1)S(1)}, bf16[2,256,256]{2,1,0:T(8,128)(2,1)S(1)}, bf16[2,256,256]{2,1,0:T(8,128)(2,1)S(1)}, bf16[2,256,256]{2,1,0:T(8,128)(2,1)S(1)}) custom-call(s32[1,26]{1,0:T(1,128)S(1)} %bitcast.32, s32[120,128]{1,0:T(8,128)S(1)} %get-tuple-element.93.refs_1_, ...), custom_call_target="tpu_custom_call" | custom-call | flops 671088640 | bytes 16252928 | tf_op jit(solution)/shard_map/pallas_call | solution.py:530
  109.4 3.8 %collective-permute-start.27 = (bf16[2,256,256]{2,1,0:T(8,128)(2,1)S(1)}, bf16[2,256,256]{2,1,0:T(8,128)(2,1)S(1)}, u32[]{:S(2)}, u32[]{:S(2)}) collective-permute-start(bf16[2,256,256]{2,1,0:T(8,128)(2,1)S(1)} %get-tuple-element.123), channel_id=1, source_target_pairs={{0,16},{8,24},{16,0},{24,8},{32,48},{40,56},{48,32},{56,40},{64,80... | collective-permute-start | bytes 786440 | tf_op jit(solution)/shard_map/ppermute | solution.py:51
  120.1 5.0 %collective-permute-done.27.refs_1_ = bf16[2,256,256]{2,1,0:T(8,128)(2,1)S(1)} collective-permute-done((bf16[2,256,256]{2,1,0:T(8,128)(2,1)S(1)}, bf16[2,256,256]{2,1,0:T(8,128)(2,1)S(1)}, u32[]{:S(2)}, u32[]{:S(2)}) %collective-permute-start.27) | collective-permute-done | bytes 262176 | tf_op jit(solution)/shard_map/ppermute | solution.py:51
  (58 shorter events, 38.1 us)
Async XLA Ops:
  1.9 19.5 %collective-permute-start.3 = (s16[1280,128]{1,0:T(8,128)(2,1)S(1)}, s16[1280,128]{1,0:T(8,128)(2,1)S(1)}, u32[]{:S(2)}, u32[]{:S(2)}) collective-permute-start(s16[1280,128]{1,0:T(8,128)(2,1)S(1)} %shard_map.130.own), channel_id=1, source_target_pairs={{0,8},{8,0},{16,24},{24,16},{32,40},{40,32},{48,56},{56,48},{64,72... | collective-permute-start | bytes 983048 | tf_op jit(solution)/shard_map/ppermute | solution.py:601
  8.6 12.7 %collective-permute-start.1 = (s16[592,128]{1,0:T(8,128)(2,1)S(1)}, s16[592,128]{1,0:T(8,128)(2,1)S(1)}, u32[]{:S(2)}, u32[]{:S(2)}) collective-permute-start(s16[592,128]{1,0:T(8,128)(2,1)S(1)} %get-tuple-element.71), channel_id=1, source_target_pairs={{0,16},{8,24},{16,0},{24,8},{32,48},{40,56},{48,32},{56,40},{64,80... | collective-permute-start | bytes 454664 | tf_op jit(solution)/shard_map/ppermute | solution.py:51
  12.5 8.9 %collective-permute-start.2 = (s16[592,128]{1,0:T(8,128)(2,1)S(1)}, s16[592,128]{1,0:T(8,128)(2,1)S(1)}, u32[]{:S(2)}, u32[]{:S(2)}) collective-permute-start(s16[592,128]{1,0:T(8,128)(2,1)S(1)} %get-tuple-element.72), channel_id=1, source_target_pairs={{0,24},{8,0},{16,8},{24,16},{32,56},{40,32},{48,40},{56,48},{64,88... | collective-permute-start | bytes 454664 | tf_op jit(solution)/shard_map/ppermute | solution.py:51
  22.0 16.9 %collective-permute-start.10 = (s16[2,1280,128]{2,1,0:T(8,128)(2,1)S(1)}, s16[2,1280,128]{2,1,0:T(8,128)(2,1)S(1)}, u32[]{:S(2)}, u32[]{:S(2)}) collective-permute-start(s16[2,1280,128]{2,1,0:T(8,128)(2,1)S(1)} %pad_add_fusion), channel_id=1, source_target_pairs={{0,24},{8,16},{16,8},{24,0},{32,56},{40,48},{48,40},{56,32},{64,88... | collective-permute-start | bytes 1966088 | tf_op jit(solution)/shard_map/ppermute | solution.py:601
  22.8 17.0 %collective-permute-start.6 = (s16[4,592,128]{2,1,0:T(8,128)(2,1)S(1)}, s16[4,592,128]{2,1,0:T(8,128)(2,1)S(1)}, u32[]{:S(2)}, u32[]{:S(2)}) collective-permute-start(s16[4,592,128]{2,1,0:T(8,128)(2,1)S(1)} %get-tuple-element.81.region.own.refs_0_), channel_id=1, source_target_pairs={{0,1},{2,3},{4,5},{6,7},{1,0},{3,2},{5,4},{7,6},{8,9},{10,11},{12,... | collective-permute-start | bytes 1818632 | tf_op jit(solution)/shard_map/ppermute | solution.py:582
  22.8 20.5 %collective-permute-start.8 = (s16[4,592,128]{2,1,0:T(8,128)(2,1)S(1)}, s16[4,592,128]{2,1,0:T(8,128)(2,1)S(1)}, u32[]{:S(2)}, u32[]{:S(2)}) collective-permute-start(s16[4,592,128]{2,1,0:T(8,128)(2,1)S(1)} %get-tuple-element.81.region.own.refs_0_), channel_id=1, source_target_pairs={{1,2},{3,4},{5,6},{2,1},{4,3},{6,5},{9,10},{11,12},{13,14},{10,9},... | collective-permute-start | bytes 1818632 | tf_op jit(solution)/shard_map/ppermute | solution.py:582
  25.9 9.1 %collective-permute-start.5 = (s16[592,128]{1,0:T(8,128)(2,1)S(1)}, s16[592,128]{1,0:T(8,128)(2,1)S(1)}, u32[]{:S(2)}, u32[]{:S(2)}) collective-permute-start(s16[592,128]{1,0:T(8,128)(2,1)S(1)} %get-tuple-element.83), channel_id=1, source_target_pairs={{32,64},{40,72},{48,80},{56,88},{64,32},{72,40},{80,48},{88,56},{3... | collective-permute-start | bytes 454664 | tf_op jit(solution)/shard_map/ppermute | solution.py:588
  35.2 8.1 %collective-permute-start.9 = (s16[2,592,128]{2,1,0:T(8,128)(2,1)S(1)}, s16[2,592,128]{2,1,0:T(8,128)(2,1)S(1)}, u32[]{:S(2)}, u32[]{:S(2)}) collective-permute-start(s16[2,592,128]{2,1,0:T(8,128)(2,1)S(1)} %pad_add_fusion.1.ends.refs_1_.refs_3_), channel_id=1, source_target_pairs={{1,2},{3,4},{5,6},{2,1},{4,3},{6,5},{9,10},{11,12},{13,14},{10,9},... | collective-permute-start | bytes 909320 | tf_op jit(solution)/shard_map/ppermute | solution.py:582
  52.2 15.7 %collective-permute-start.15 = (bf16[4,2,256,256]{3,2,1,0:T(8,128)(2,1)S(1)}, bf16[4,2,256,256]{3,2,1,0:T(8,128)(2,1)S(1)}, u32[]{:S(2)}, u32[]{:S(2)}) collective-permute-start(bf16[4,2,256,256]{3,2,1,0:T(8,128)(2,1)S(1)} %get-tuple-element.98.refs_2_), channel_id=1, source_target_pairs={{0,1},{2,3},{4,5},{6,7},{1,0},{3,2},{5,4},{7,6},{8,9},{10,11},{12,... | collective-permute-start | bytes 3145736 | tf_op jit(solution)/shard_map/ppermute | solution.py:582
  52.6 23.8 %collective-permute-start.11 = (bf16[4,2,256,256]{3,2,1,0:T(8,128)(2,1)S(1)}, bf16[4,2,256,256]{3,2,1,0:T(8,128)(2,1)S(1)}, u32[]{:S(2)}, u32[]{:S(2)}) collective-permute-start(bf16[4,2,256,256]{3,2,1,0:T(8,128)(2,1)S(1)} %get-tuple-element.98.refs_2_), channel_id=1, source_target_pairs={{1,2},{3,4},{5,6},{2,1},{4,3},{6,5},{9,10},{11,12},{13,14},{10,9},... | collective-permute-start | bytes 3145736 | tf_op jit(solution)/shard_map/ppermute | solution.py:582
  54.5 8.9 %collective-permute-start.12 = (bf16[2,256,256]{2,1,0:T(8,128)(2,1)S(1)}, bf16[2,256,256]{2,1,0:T(8,128)(2,1)S(1)}, u32[]{:S(2)}, u32[]{:S(2)}) collective-permute-start(bf16[2,256,256]{2,1,0:T(8,128)(2,1)S(1)} %get-tuple-element.99), channel_id=1, source_target_pairs={{0,32},{8,40},{16,48},{24,56},{64,96},{72,104},{80,112},{88,120},{... | collective-permute-start | bytes 786440 | tf_op jit(solution)/shard_map/ppermute | solution.py:588
  54.6 10.7 %collective-permute-start.13 = (bf16[2,256,256]{2,1,0:T(8,128)(2,1)S(1)}, bf16[2,256,256]{2,1,0:T(8,128)(2,1)S(1)}, u32[]{:S(2)}, u32[]{:S(2)}) collective-permute-start(bf16[2,256,256]{2,1,0:T(8,128)(2,1)S(1)} %get-tuple-element.100), channel_id=1, source_target_pairs={{32,64},{40,72},{48,80},{56,88},{64,32},{72,40},{80,48},{88,56},{3... | collective-permute-start | bytes 786440 | tf_op jit(solution)/shard_map/ppermute | solution.py:588
  66.0 10.5 %collective-permute-start.14 = (bf16[2,2,256,256]{3,2,1,0:T(8,128)(2,1)S(1)}, bf16[2,2,256,256]{3,2,1,0:T(8,128)(2,1)S(1)}, u32[]{:S(2)}, u32[]{:S(2)}) collective-permute-start(bf16[2,2,256,256]{3,2,1,0:T(8,128)(2,1)S(1)} %pad_maximum_fusion.refs_3_), channel_id=1, source_target_pairs={{1,2},{3,4},{5,6},{2,1},{4,3},{6,5},{9,10},{11,12},{13,14},{10,9},... | collective-permute-start | bytes 1572872 | tf_op jit(solution)/shard_map/ppermute | solution.py:582
  79.6 17.5 %collective-permute-start.21 = (bf16[4,2,256,256]{3,2,1,0:T(8,128)(2,1)S(1)}, bf16[4,2,256,256]{3,2,1,0:T(8,128)(2,1)S(1)}, u32[]{:S(2)}, u32[]{:S(2)}) collective-permute-start(bf16[4,2,256,256]{3,2,1,0:T(8,128)(2,1)S(1)} %get-tuple-element.102.refs_2_), channel_id=1, source_target_pairs={{0,1},{2,3},{4,5},{6,7},{1,0},{3,2},{5,4},{7,6},{8,9},{10,11},{12,... | collective-permute-start | bytes 3145736 | tf_op jit(solution)/shard_map/ppermute | solution.py:582
  80.4 8.3 %collective-permute-start.18 = (bf16[2,256,256]{2,1,0:T(8,128)(2,1)S(1)}, bf16[2,256,256]{2,1,0:T(8,128)(2,1)S(1)}, u32[]{:S(2)}, u32[]{:S(2)}) collective-permute-start(bf16[2,256,256]{2,1,0:T(8,128)(2,1)S(1)} %get-tuple-element.103), channel_id=1, source_target_pairs={{0,32},{8,40},{16,48},{24,56},{64,96},{72,104},{80,112},{88,120},{... | collective-permute-start | bytes 786440 | tf_op jit(solution)/shard_map/ppermute | solution.py:588
  80.4 10.2 %collective-permute-start.19 = (bf16[2,256,256]{2,1,0:T(8,128)(2,1)S(1)}, bf16[2,256,256]{2,1,0:T(8,128)(2,1)S(1)}, u32[]{:S(2)}, u32[]{:S(2)}) collective-permute-start(bf16[2,256,256]{2,1,0:T(8,128)(2,1)S(1)} %get-tuple-element.104), channel_id=1, source_target_pairs={{32,64},{40,72},{48,80},{56,88},{64,32},{72,40},{80,48},{88,56},{3... | collective-permute-start | bytes 786440 | tf_op jit(solution)/shard_map/ppermute | solution.py:588
  83.3 21.7 %collective-permute-start.17 = (bf16[4,2,256,256]{3,2,1,0:T(8,128)(2,1)S(1)}, bf16[4,2,256,256]{3,2,1,0:T(8,128)(2,1)S(1)}, u32[]{:S(2)}, u32[]{:S(2)}) collective-permute-start(bf16[4,2,256,256]{3,2,1,0:T(8,128)(2,1)S(1)} %get-tuple-element.102.refs_2_), channel_id=1, source_target_pairs={{1,2},{3,4},{5,6},{2,1},{4,3},{6,5},{9,10},{11,12},{13,14},{10,9},... | collective-permute-start | bytes 3145736 | tf_op jit(solution)/shard_map/ppermute | solution.py:582
  90.7 14.3 %collective-permute-start.20 = (bf16[2,2,256,256]{3,2,1,0:T(8,128)(2,1)S(1)}, bf16[2,2,256,256]{3,2,1,0:T(8,128)(2,1)S(1)}, u32[]{:S(2)}, u32[]{:S(2)}) collective-permute-start(bf16[2,2,256,256]{3,2,1,0:T(8,128)(2,1)S(1)} %pad_maximum_fusion.1.refs_3_), channel_id=1, source_target_pairs={{1,2},{3,4},{5,6},{2,1},{4,3},{6,5},{9,10},{11,12},{13,14},{10,9},... | collective-permute-start | bytes 1572872 | tf_op jit(solution)/shard_map/ppermute | solution.py:582
  93.0 15.1 %collective-permute-start.23 = (bf16[2,256,256]{2,1,0:T(8,128)(2,1)S(1)}, bf16[2,256,256]{2,1,0:T(8,128)(2,1)S(1)}, u32[]{:S(2)}, u32[]{:S(2)}) collective-permute-start(bf16[2,256,256]{2,1,0:T(8,128)(2,1)S(1)} %get-tuple-element.111), channel_id=1, source_target_pairs={{0,8},{8,16},{16,24},{24,0},{32,40},{40,48},{48,56},{56,32},{64,72... | collective-permute-start | bytes 786440 | tf_op jit(solution)/shard_map/ppermute | solution.py:51
  93.6 15.8 %collective-permute-start.24 = (bf16[2,256,256]{2,1,0:T(8,128)(2,1)S(1)}, bf16[2,256,256]{2,1,0:T(8,128)(2,1)S(1)}, u32[]{:S(2)}, u32[]{:S(2)}) collective-permute-start(bf16[2,256,256]{2,1,0:T(8,128)(2,1)S(1)} %get-tuple-element.112), channel_id=1, source_target_pairs={{0,16},{8,24},{16,0},{24,8},{32,48},{40,56},{48,32},{56,40},{64,80... | collective-permute-start | bytes 786440 | tf_op jit(solution)/shard_map/ppermute | solution.py:51
  97.1 12.2 %collective-permute-start.25 = (bf16[2,256,256]{2,1,0:T(8,128)(2,1)S(1)}, bf16[2,256,256]{2,1,0:T(8,128)(2,1)S(1)}, u32[]{:S(2)}, u32[]{:S(2)}) collective-permute-start(bf16[2,256,256]{2,1,0:T(8,128)(2,1)S(1)} %get-tuple-element.113), channel_id=1, source_target_pairs={{0,24},{8,0},{16,8},{24,16},{32,56},{40,32},{48,40},{56,48},{64,88... | collective-permute-start | bytes 786440 | tf_op jit(solution)/shard_map/ppermute | solution.py:51
  109.3 9.4 %collective-permute-start.28 = (bf16[2,256,256]{2,1,0:T(8,128)(2,1)S(1)}, bf16[2,256,256]{2,1,0:T(8,128)(2,1)S(1)}, u32[]{:S(2)}, u32[]{:S(2)}) collective-permute-start(bf16[2,256,256]{2,1,0:T(8,128)(2,1)S(1)} %get-tuple-element.124), channel_id=1, source_target_pairs={{0,8},{8,16},{16,24},{24,0},{32,40},{40,48},{48,56},{56,32},{64,72... | collective-permute-start | bytes 786440 | tf_op jit(solution)/shard_map/ppermute | solution.py:51
  109.4 15.7 %collective-permute-start.27 = (bf16[2,256,256]{2,1,0:T(8,128)(2,1)S(1)}, bf16[2,256,256]{2,1,0:T(8,128)(2,1)S(1)}, u32[]{:S(2)}, u32[]{:S(2)}) collective-permute-start(bf16[2,256,256]{2,1,0:T(8,128)(2,1)S(1)} %get-tuple-element.123), channel_id=1, source_target_pairs={{0,16},{8,24},{16,0},{24,8},{32,48},{40,56},{48,32},{56,40},{64,80... | collective-permute-start | bytes 786440 | tf_op jit(solution)/shard_map/ppermute | solution.py:51
  113.3 13.2 %collective-permute-start.26 = (bf16[2,256,256]{2,1,0:T(8,128)(2,1)S(1)}, bf16[2,256,256]{2,1,0:T(8,128)(2,1)S(1)}, u32[]{:S(2)}, u32[]{:S(2)}) collective-permute-start(bf16[2,256,256]{2,1,0:T(8,128)(2,1)S(1)} %get-tuple-element.122), channel_id=1, source_target_pairs={{0,24},{8,0},{16,8},{24,16},{32,56},{40,32},{48,40},{56,48},{64,88... | collective-permute-start | bytes 786440 | tf_op jit(solution)/shard_map/ppermute | solution.py:51
  (5 other events, 24.0 us)

commit v4 on v3

--- a/solution.py
+++ b/solution.py
@@ -322,9 +322,6 @@
     else:
         narrow_out, *edge_blocks = refs[:3]
         refs = refs[3:]
-        if not first:
-            parts = refs[:RING]
-            refs = refs[RING:]
     fu, fv, fvs, gathered, sources, terms_a, terms_b, acc1, acc2, homes, count = refs[:11]
     xv = refs[11] if first else None
 
@@ -497,6 +494,11 @@
         part[...] = narrow_out[(flags[0, 0] + d) % RING]
 
 
+def parts_kernel(flags, narrow, *parts):
+    for d, part in enumerate(parts):
+        part[...] = narrow[(flags[0, 0] + d) % RING]
+
+
 def result_kernel(shifts, flags, *refs):
     parts, refs = refs[: len(shifts)], refs[len(shifts) :]
     if shifts[0]:
@@ -562,7 +564,7 @@
         scratch.append(pltpu.VMEM(NARROW.shape, BF16))
         out = (BLOCK,) * RING
     else:
-        out = (NARROW, BLOCK, BLOCK) + (BLOCK,) * RING
+        out = (NARROW, BLOCK, BLOCK)
     halo = halo[: 6 if end else 4][0 if begin else 4 :]
     kernel = functools.partial(step_kernel, first, last, begin, end)
     moved_bytes = sum(math.prod(x.shape) * x.dtype.itemsize for x in (*halo, *rest, *jax.tree.leaves(out)))
@@ -688,10 +690,10 @@
 
     tables = (bd1, bd2, ops)
     one, *one_blocks = step(True, False, True, True, flags, idx, (zero_narrow, *halo[1:]), *tables)
-    *two_blocks, part0, part1, part2, part3 = halved_step(
+    two_blocks = halved_step(
         False, flags, idx, halo_of(*one_blocks)[0], tables, zero
     )
-    got = ring_exchanged((part0, part1, part2, part3))
+    got = ring_exchanged(local(parts_kernel, (BLOCK,) * RING, (flags,), two_blocks[0]))
     three_parts = halved_step(True, flags, idx, halo_of(*two_blocks)[0], tables, one)
     three_parts, got = lax.optimization_barrier((three_parts, got))
     two_a, two_b = results(flags, got, ((0,), (1, 2, 3)))

time: 129 us -> 129 us (level)
    ppermute x6, starting transfers between devices: 11.1 us -> 12.8 us  [swapped_rows(): return lax.ppermute(array, 'gx', pairs + [(j, i) for i, j in pairs])]
    ppermute x6, waiting for transfers between devices: 15.3 us -> 14 us  [swapped_rows(): return lax.ppermute(array, 'gx', pairs + [(j, i) for i, j in pairs])]
    pallas_call x12 -> x13, Pallas kernels: 33 us -> 33.5 us  [local(): pl.pallas_call(kernel, out_shape=out_shape, in_specs=[SMEM] * len(scalars...]
where the time goes in v4:
time: 129 us
  starting transfers between devices  43.8 us (34%)
  Pallas kernels  42 us (33%)
  waiting for transfers between devices  38.8 us (30%)
  local copies, waits for them, and re-layouts  1.89 us (1%)
  between operations  1.78 us (1%)
    pallas_call x13, Pallas kernels, local(): pl.pallas_call(kernel, out_shape=out_shape, in_specs=[SMEM] * len(scalars...  33.5 us
    ppermute x9, starting transfers between devices, ring_moved(): return lax.ppermute(array, 'gx', pairs)  14.3 us
    ppermute x6, waiting for transfers between devices, swapped_rows(): return lax.ppermute(array, 'gx', pairs + [(j, i) for i, j in pairs])  14 us
    ppermute x12, starting transfers between devices, across(): return lax.ppermute(array, 'gy', pairs + [(j, i) for i, j in pairs])  14 us
    ppermute x9, waiting for transfers between devices, ring_moved(): return lax.ppermute(array, 'gx', pairs)  13.4 us
    ppermute x6, starting transfers between devices, swapped_rows(): return lax.ppermute(array, 'gx', pairs + [(j, i) for i, j in pairs])  12.8 us
    ppermute x12, waiting for transfers between devices, across(): return lax.ppermute(array, 'gy', pairs + [(j, i) for i, j in pairs])  9.63 us
    pallas_call x6, Pallas kernels, written(): pl.pallas_call(lambda *refs: result_kernel(shifts, *refs), out_shape=(jax...  8.57 us
  transfers between devices with their start and end apart: 29, of which 14 were waited for; matrix products, arithmetic and copies ran while one was open for 2% of the time, Pallas kernels for 21%

profile of v4, /device:TPU:10, one launch (start us, length us, event | category | flops | bytes accessed | tf_op | source)
XLA Modules:
  0.0 128.6 jit_solution(13366685308855403524)
XLA Ops:
  6.4 2.0 %shard_map.129 = (s16[592,128]{1,0:T(8,128)(2,1)S(1)}, s16[592,128]{1,0:T(8,128)(2,1)S(1)}, s16[592,128]{1,0:T(8,128)(2,1)S(1)}, s16[592,128]{1,0:T(8,128)(2,1)S(1)}) custom-call(s32[1,26]{1,0:T(1,128)S(1)} %bitcast.23, f32[256,32]{1,0:T(8,128)S(1)} %reshape.66.coupling, f32[4,2,128,128]{3,2,1,0:T(8,128)} %phase_one.1, f32[4,2,128,128]{3,2,1,0:T(8,128)} %phase_two.1, ...), custom_call_target="tpu_custom_call" | custom-call | tf_op jit(solution)/shard_map/pallas_call | solution.py:532
  8.6 3.9 %collective-permute-start.1 = (s16[592,128]{1,0:T(8,128)(2,1)S(1)}, s16[592,128]{1,0:T(8,128)(2,1)S(1)}, u32[]{:S(2)}, u32[]{:S(2)}) collective-permute-start(s16[592,128]{1,0:T(8,128)(2,1)S(1)} %get-tuple-element.71), channel_id=1, source_target_pairs={{0,16},{8,24},{16,0},{24,8},{32,48},{40,56},{48,32},{56,40},{64,80... | collective-permute-start | bytes 454664 | tf_op jit(solution)/shard_map/ppermute | solution.py:51
  12.5 2.2 %collective-permute-start.2 = (s16[592,128]{1,0:T(8,128)(2,1)S(1)}, s16[592,128]{1,0:T(8,128)(2,1)S(1)}, u32[]{:S(2)}, u32[]{:S(2)}) collective-permute-start(s16[592,128]{1,0:T(8,128)(2,1)S(1)} %get-tuple-element.72), channel_id=1, source_target_pairs={{0,24},{8,0},{16,8},{24,16},{32,56},{40,32},{48,40},{56,48},{64,88... | collective-permute-start | bytes 454664 | tf_op jit(solution)/shard_map/ppermute | solution.py:51
  15.2 6.1 %collective-permute-done.1.part2 = s16[592,128]{1,0:T(8,128)(2,1)S(1)} collective-permute-done((s16[592,128]{1,0:T(8,128)(2,1)S(1)}, s16[592,128]{1,0:T(8,128)(2,1)S(1)}, u32[]{:S(2)}, u32[]{:S(2)}) %collective-permute-start.1) | collective-permute-done | bytes 151584 | tf_op jit(solution)/shard_map/ppermute | solution.py:51
  22.8 2.5 %collective-permute-start.8 = (s16[4,592,128]{2,1,0:T(8,128)(2,1)S(1)}, s16[4,592,128]{2,1,0:T(8,128)(2,1)S(1)}, u32[]{:S(2)}, u32[]{:S(2)}) collective-permute-start(s16[4,592,128]{2,1,0:T(8,128)(2,1)S(1)} %get-tuple-element.81.region.own.refs_0_), channel_id=1, source_target_pairs={{1,2},{3,4},{5,6},{2,1},{4,3},{6,5},{9,10},{11,12},{13,14},{10,9},... | collective-permute-start | bytes 1818632 | tf_op jit(solution)/shard_map/ppermute | solution.py:584
  25.9 4.3 %collective-permute-start.5 = (s16[592,128]{1,0:T(8,128)(2,1)S(1)}, s16[592,128]{1,0:T(8,128)(2,1)S(1)}, u32[]{:S(2)}, u32[]{:S(2)}) collective-permute-start(s16[592,128]{1,0:T(8,128)(2,1)S(1)} %get-tuple-element.83), channel_id=1, source_target_pairs={{32,64},{40,72},{48,80},{56,88},{64,32},{72,40},{80,48},{88,56},{3... | collective-permute-start | bytes 454664 | tf_op jit(solution)/shard_map/ppermute | solution.py:590
  30.2 2.2 %shard_map.132 = (f32[2,2,2,512,128]{4,3,2,1,0:T(8,128)S(1)}, bf16[4,2,256,256]{3,2,1,0:T(8,128)(2,1)S(1)}, bf16[18,512,256]{2,1,0:T(8,128)(2,1)S(1)}, bf16[4,512,256]{2,1,0:T(8,128)(2,1)S(1)}) custom-call(s16[4,592,128]{2,1,0:T(8,128)(2,1)S(1)} %get-tuple-element.81.region.own.refs_0_), custom_call_target="tpu_custom_call" | custom-call | tf_op jit(solution)/shard_map/pallas_call | solution.py:532
  32.4 2.6 %collective-permute-done.5 = s16[592,128]{1,0:T(8,128)(2,1)S(1)} collective-permute-done((s16[592,128]{1,0:T(8,128)(2,1)S(1)}, s16[592,128]{1,0:T(8,128)(2,1)S(1)}, u32[]{:S(2)}, u32[]{:S(2)}) %collective-permute-start.5) | collective-permute-done | bytes 151584 | tf_op jit(solution)/shard_map/ppermute | solution.py:590
  41.1 2.2 %collective-permute-done.9.refs_5_.refs_7_ = s16[2,592,128]{2,1,0:T(8,128)(2,1)S(1)} collective-permute-done((s16[2,592,128]{2,1,0:T(8,128)(2,1)S(1)}, s16[2,592,128]{2,1,0:T(8,128)(2,1)S(1)}, u32[]{:S(2)}, u32[]{:S(2)}) %collective-permute-start.9) | collective-permute-done | bytes 303136 | tf_op jit(solution)/shard_map/ppermute | solution.py:584
  44.5 7.7 %shard_map.136 = (f32[2,2,2,512,128]{4,3,2,1,0:T(8,128)S(1)}, bf16[4,2,256,256]{3,2,1,0:T(8,128)(2,1)S(1)}, bf16[2,256,256]{2,1,0:T(8,128)(2,1)S(1)}, bf16[2,256,256]{2,1,0:T(8,128)(2,1)S(1)}) custom-call(s32[1,26]{1,0:T(1,128)S(1)} %bitcast.28, s32[120,128]{1,0:T(8,128)S(1)} %get-tuple-element.93.refs_1_, ...), custom_call_target="tpu_custom_call" | custom-call | flops 671088640 | bytes 16277504 | tf_op jit(solution)/shard_map/pallas_call | solution.py:532
  54.6 4.0 %collective-permute-start.13 = (bf16[2,256,256]{2,1,0:T(8,128)(2,1)S(1)}, bf16[2,256,256]{2,1,0:T(8,128)(2,1)S(1)}, u32[]{:S(2)}, u32[]{:S(2)}) collective-permute-start(bf16[2,256,256]{2,1,0:T(8,128)(2,1)S(1)} %get-tuple-element.100), channel_id=1, source_target_pairs={{32,64},{40,72},{48,80},{56,88},{64,32},{72,40},{80,48},{88,56},{3... | collective-permute-start | bytes 786440 | tf_op jit(solution)/shard_map/ppermute | solution.py:590
  58.6 4.9 %collective-permute-done.12 = bf16[2,256,256]{2,1,0:T(8,128)(2,1)S(1)} collective-permute-done((bf16[2,256,256]{2,1,0:T(8,128)(2,1)S(1)}, bf16[2,256,256]{2,1,0:T(8,128)(2,1)S(1)}, u32[]{:S(2)}, u32[]{:S(2)}) %collective-permute-start.12) | collective-permute-done | bytes 262176 | tf_op jit(solution)/shard_map/ppermute | solution.py:590
  67.9 4.5 %shard_map.137.refs_7_ = f32[2,2,2,512,128]{4,3,2,1,0:T(8,128)S(1)} custom-call(s32[1,26]{1,0:T(1,128)S(1)} %bitcast.29, s32[120,128]{1,0:T(8,128)S(1)} %get-tuple-element.93.refs_1_, bf16[4,2,256,256]{3,2,1,0:T(8,128)(2,1)S(1)} %get-tuple-element.98.refs_2_, bf16[2,2,256,256]{3,2,1,0:T(8,128)(2,1)S(1)} %pad_maximum_fusion.refs_3_, ...), custom_call_target="tpu_custom_call" | custom-call | flops 671088640 | bytes 14680064 | tf_op jit(solution)/shard_map/pallas_call | solution.py:532
  72.4 4.1 %collective-permute-done.14.refs_3_ = bf16[2,2,256,256]{3,2,1,0:T(8,128)(2,1)S(1)} collective-permute-done((bf16[2,2,256,256]{3,2,1,0:T(8,128)(2,1)S(1)}, bf16[2,2,256,256]{3,2,1,0:T(8,128)(2,1)S(1)}, u32[]{:S(2)}, u32[]{:S(2)}) %collective-permute-start.14) | collective-permute-done | bytes 524320 | tf_op jit(solution)/shard_map/ppermute | solution.py:584
  76.4 3.3 %shard_map.138 = (bf16[4,2,256,256]{3,2,1,0:T(8,128)(2,1)S(1)}, bf16[2,256,256]{2,1,0:T(8,128)(2,1)S(1)}, bf16[2,256,256]{2,1,0:T(8,128)(2,1)S(1)}) custom-call(s32[1,26]{1,0:T(1,128)S(1)} %bitcast.30, s32[120,128]{1,0:T(8,128)S(1)} %get-tuple-element.93.refs_1_, bf16[4,2,256,256]{3,2,1,0:T(8,128)(2,1)S(1)} %collective-permute-done.11.refs_2_, ...), custom_call_target="tpu_custom_call" | custom-call | flops 671088640 | bytes 16777216 | tf_op jit(solution)/shard_map/pallas_call | solution.py:532
  80.0 3.9 %collective-permute-start.19 = (bf16[2,256,256]{2,1,0:T(8,128)(2,1)S(1)}, bf16[2,256,256]{2,1,0:T(8,128)(2,1)S(1)}, u32[]{:S(2)}, u32[]{:S(2)}) collective-permute-start(bf16[2,256,256]{2,1,0:T(8,128)(2,1)S(1)} %get-tuple-element.104), channel_id=1, source_target_pairs={{32,64},{40,72},{48,80},{56,88},{64,32},{72,40},{80,48},{88,56},{3... | collective-permute-start | bytes 786440 | tf_op jit(solution)/shard_map/ppermute | solution.py:590
  85.9 2.7 %collective-permute-done.18 = bf16[2,256,256]{2,1,0:T(8,128)(2,1)S(1)} collective-permute-done((bf16[2,256,256]{2,1,0:T(8,128)(2,1)S(1)}, bf16[2,256,256]{2,1,0:T(8,128)(2,1)S(1)}, u32[]{:S(2)}, u32[]{:S(2)}) %collective-permute-start.18) | collective-permute-done | bytes 262176 | tf_op jit(solution)/shard_map/ppermute | solution.py:590
  88.6 2.1 %collective-permute-done.19 = bf16[2,256,256]{2,1,0:T(8,128)(2,1)S(1)} collective-permute-done((bf16[2,256,256]{2,1,0:T(8,128)(2,1)S(1)}, bf16[2,256,256]{2,1,0:T(8,128)(2,1)S(1)}, u32[]{:S(2)}, u32[]{:S(2)}) %collective-permute-start.19) | collective-permute-done | bytes 262176 | tf_op jit(solution)/shard_map/ppermute | solution.py:590
  94.1 3.5 %collective-permute-start.24 = (bf16[2,256,256]{2,1,0:T(8,128)(2,1)S(1)}, bf16[2,256,256]{2,1,0:T(8,128)(2,1)S(1)}, u32[]{:S(2)}, u32[]{:S(2)}) collective-permute-start(bf16[2,256,256]{2,1,0:T(8,128)(2,1)S(1)} %get-tuple-element.112), channel_id=1, source_target_pairs={{0,16},{8,24},{16,0},{24,8},{32,48},{40,56},{48,32},{56,40},{64,80... | collective-permute-start | bytes 786440 | tf_op jit(solution)/shard_map/ppermute | solution.py:51
  97.7 4.7 %shard_map.139.refs_7_ = f32[2,2,2,512,128]{4,3,2,1,0:T(8,128)S(1)} custom-call(s32[1,26]{1,0:T(1,128)S(1)} %bitcast.32, s32[120,128]{1,0:T(8,128)S(1)} %get-tuple-element.93.refs_1_, bf16[4,2,256,256]{3,2,1,0:T(8,128)(2,1)S(1)} %get-tuple-element.102.refs_2_.narrow, bf16[2,2,256,256]{3,2,1,0:T(8,128)(2,1)S(1)} %pad_maximum_fusion.1.refs_3_, ...), custom_call_target="tpu_custom_call" | custom-call | flops 671088640 | bytes 14680064 | tf_op jit(solution)/shard_map/pallas_call | solution.py:532
  102.3 3.3 %collective-permute-done.20.refs_3_ = bf16[2,2,256,256]{3,2,1,0:T(8,128)(2,1)S(1)} collective-permute-done((bf16[2,2,256,256]{3,2,1,0:T(8,128)(2,1)S(1)}, bf16[2,2,256,256]{3,2,1,0:T(8,128)(2,1)S(1)}, u32[]{:S(2)}, u32[]{:S(2)}) %collective-permute-start.20) | collective-permute-done | bytes 524320 | tf_op jit(solution)/shard_map/ppermute | solution.py:584
  105.7 3.4 %shard_map.140 = (bf16[2,256,256]{2,1,0:T(8,128)(2,1)S(1)}, bf16[2,256,256]{2,1,0:T(8,128)(2,1)S(1)}, bf16[2,256,256]{2,1,0:T(8,128)(2,1)S(1)}, bf16[2,256,256]{2,1,0:T(8,128)(2,1)S(1)}) custom-call(s32[1,26]{1,0:T(1,128)S(1)} %bitcast.33, s32[120,128]{1,0:T(8,128)S(1)} %get-tuple-element.93.refs_1_, ...), custom_call_target="tpu_custom_call" | custom-call | flops 671088640 | bytes 16252928 | tf_op jit(solution)/shard_map/pallas_call | solution.py:532
  110.0 3.8 %collective-permute-start.27 = (bf16[2,256,256]{2,1,0:T(8,128)(2,1)S(1)}, bf16[2,256,256]{2,1,0:T(8,128)(2,1)S(1)}, u32[]{:S(2)}, u32[]{:S(2)}) collective-permute-start(bf16[2,256,256]{2,1,0:T(8,128)(2,1)S(1)} %get-tuple-element.123), channel_id=1, source_target_pairs={{0,16},{8,24},{16,0},{24,8},{32,48},{40,56},{48,32},{56,40},{64,80... | collective-permute-start | bytes 786440 | tf_op jit(solution)/shard_map/ppermute | solution.py:51
  120.3 5.3 %collective-permute-done.27.refs_1_ = bf16[2,256,256]{2,1,0:T(8,128)(2,1)S(1)} collective-permute-done((bf16[2,256,256]{2,1,0:T(8,128)(2,1)S(1)}, bf16[2,256,256]{2,1,0:T(8,128)(2,1)S(1)}, u32[]{:S(2)}, u32[]{:S(2)}) %collective-permute-start.27) | collective-permute-done | bytes 262176 | tf_op jit(solution)/shard_map/ppermute | solution.py:51
  (59 shorter events, 37.4 us)
Async XLA Ops:
  1.9 19.5 %collective-permute-start.3 = (s16[1280,128]{1,0:T(8,128)(2,1)S(1)}, s16[1280,128]{1,0:T(8,128)(2,1)S(1)}, u32[]{:S(2)}, u32[]{:S(2)}) collective-permute-start(s16[1280,128]{1,0:T(8,128)(2,1)S(1)} %shard_map.130.own), channel_id=1, source_target_pairs={{0,8},{8,0},{16,24},{24,16},{32,40},{40,32},{48,56},{56,48},{64,72... | collective-permute-start | bytes 983048 | tf_op jit(solution)/shard_map/ppermute | solution.py:603
  8.6 12.7 %collective-permute-start.1 = (s16[592,128]{1,0:T(8,128)(2,1)S(1)}, s16[592,128]{1,0:T(8,128)(2,1)S(1)}, u32[]{:S(2)}, u32[]{:S(2)}) collective-permute-start(s16[592,128]{1,0:T(8,128)(2,1)S(1)} %get-tuple-element.71), channel_id=1, source_target_pairs={{0,16},{8,24},{16,0},{24,8},{32,48},{40,56},{48,32},{56,40},{64,80... | collective-permute-start | bytes 454664 | tf_op jit(solution)/shard_map/ppermute | solution.py:51
  12.5 8.9 %collective-permute-start.2 = (s16[592,128]{1,0:T(8,128)(2,1)S(1)}, s16[592,128]{1,0:T(8,128)(2,1)S(1)}, u32[]{:S(2)}, u32[]{:S(2)}) collective-permute-start(s16[592,128]{1,0:T(8,128)(2,1)S(1)} %get-tuple-element.72), channel_id=1, source_target_pairs={{0,24},{8,0},{16,8},{24,16},{32,56},{40,32},{48,40},{56,48},{64,88... | collective-permute-start | bytes 454664 | tf_op jit(solution)/shard_map/ppermute | solution.py:51
  22.0 16.9 %collective-permute-start.10 = (s16[2,1280,128]{2,1,0:T(8,128)(2,1)S(1)}, s16[2,1280,128]{2,1,0:T(8,128)(2,1)S(1)}, u32[]{:S(2)}, u32[]{:S(2)}) collective-permute-start(s16[2,1280,128]{2,1,0:T(8,128)(2,1)S(1)} %pad_add_fusion), channel_id=1, source_target_pairs={{0,24},{8,16},{16,8},{24,0},{32,56},{40,48},{48,40},{56,32},{64,88... | collective-permute-start | bytes 1966088 | tf_op jit(solution)/shard_map/ppermute | solution.py:603
  22.8 17.0 %collective-permute-start.6 = (s16[4,592,128]{2,1,0:T(8,128)(2,1)S(1)}, s16[4,592,128]{2,1,0:T(8,128)(2,1)S(1)}, u32[]{:S(2)}, u32[]{:S(2)}) collective-permute-start(s16[4,592,128]{2,1,0:T(8,128)(2,1)S(1)} %get-tuple-element.81.region.own.refs_0_), channel_id=1, source_target_pairs={{0,1},{2,3},{4,5},{6,7},{1,0},{3,2},{5,4},{7,6},{8,9},{10,11},{12,... | collective-permute-start | bytes 1818632 | tf_op jit(solution)/shard_map/ppermute | solution.py:584
  22.8 20.5 %collective-permute-start.8 = (s16[4,592,128]{2,1,0:T(8,128)(2,1)S(1)}, s16[4,592,128]{2,1,0:T(8,128)(2,1)S(1)}, u32[]{:S(2)}, u32[]{:S(2)}) collective-permute-start(s16[4,592,128]{2,1,0:T(8,128)(2,1)S(1)} %get-tuple-element.81.region.own.refs_0_), channel_id=1, source_target_pairs={{1,2},{3,4},{5,6},{2,1},{4,3},{6,5},{9,10},{11,12},{13,14},{10,9},... | collective-permute-start | bytes 1818632 | tf_op jit(solution)/shard_map/ppermute | solution.py:584
  25.9 9.1 %collective-permute-start.5 = (s16[592,128]{1,0:T(8,128)(2,1)S(1)}, s16[592,128]{1,0:T(8,128)(2,1)S(1)}, u32[]{:S(2)}, u32[]{:S(2)}) collective-permute-start(s16[592,128]{1,0:T(8,128)(2,1)S(1)} %get-tuple-element.83), channel_id=1, source_target_pairs={{32,64},{40,72},{48,80},{56,88},{64,32},{72,40},{80,48},{88,56},{3... | collective-permute-start | bytes 454664 | tf_op jit(solution)/shard_map/ppermute | solution.py:590
  35.2 8.1 %collective-permute-start.9 = (s16[2,592,128]{2,1,0:T(8,128)(2,1)S(1)}, s16[2,592,128]{2,1,0:T(8,128)(2,1)S(1)}, u32[]{:S(2)}, u32[]{:S(2)}) collective-permute-start(s16[2,592,128]{2,1,0:T(8,128)(2,1)S(1)} %pad_add_fusion.1.ends.refs_1_.refs_3_), channel_id=1, source_target_pairs={{1,2},{3,4},{5,6},{2,1},{4,3},{6,5},{9,10},{11,12},{13,14},{10,9},... | collective-permute-start | bytes 909320 | tf_op jit(solution)/shard_map/ppermute | solution.py:584
  52.1 15.8 %collective-permute-start.15 = (bf16[4,2,256,256]{3,2,1,0:T(8,128)(2,1)S(1)}, bf16[4,2,256,256]{3,2,1,0:T(8,128)(2,1)S(1)}, u32[]{:S(2)}, u32[]{:S(2)}) collective-permute-start(bf16[4,2,256,256]{3,2,1,0:T(8,128)(2,1)S(1)} %get-tuple-element.98.refs_2_), channel_id=1, source_target_pairs={{0,1},{2,3},{4,5},{6,7},{1,0},{3,2},{5,4},{7,6},{8,9},{10,11},{12,... | collective-permute-start | bytes 3145736 | tf_op jit(solution)/shard_map/ppermute | solution.py:584
  52.6 23.9 %collective-permute-start.11 = (bf16[4,2,256,256]{3,2,1,0:T(8,128)(2,1)S(1)}, bf16[4,2,256,256]{3,2,1,0:T(8,128)(2,1)S(1)}, u32[]{:S(2)}, u32[]{:S(2)}) collective-permute-start(bf16[4,2,256,256]{3,2,1,0:T(8,128)(2,1)S(1)} %get-tuple-element.98.refs_2_), channel_id=1, source_target_pairs={{1,2},{3,4},{5,6},{2,1},{4,3},{6,5},{9,10},{11,12},{13,14},{10,9},... | collective-permute-start | bytes 3145736 | tf_op jit(solution)/shard_map/ppermute | solution.py:584
  54.5 9.0 %collective-permute-start.12 = (bf16[2,256,256]{2,1,0:T(8,128)(2,1)S(1)}, bf16[2,256,256]{2,1,0:T(8,128)(2,1)S(1)}, u32[]{:S(2)}, u32[]{:S(2)}) collective-permute-start(bf16[2,256,256]{2,1,0:T(8,128)(2,1)S(1)} %get-tuple-element.99), channel_id=1, source_target_pairs={{0,32},{8,40},{16,48},{24,56},{64,96},{72,104},{80,112},{88,120},{... | collective-permute-start | bytes 786440 | tf_op jit(solution)/shard_map/ppermute | solution.py:590
  54.6 10.4 %collective-permute-start.13 = (bf16[2,256,256]{2,1,0:T(8,128)(2,1)S(1)}, bf16[2,256,256]{2,1,0:T(8,128)(2,1)S(1)}, u32[]{:S(2)}, u32[]{:S(2)}) collective-permute-start(bf16[2,256,256]{2,1,0:T(8,128)(2,1)S(1)} %get-tuple-element.100), channel_id=1, source_target_pairs={{32,64},{40,72},{48,80},{56,88},{64,32},{72,40},{80,48},{88,56},{3... | collective-permute-start | bytes 786440 | tf_op jit(solution)/shard_map/ppermute | solution.py:590
  66.0 10.5 %collective-permute-start.14 = (bf16[2,2,256,256]{3,2,1,0:T(8,128)(2,1)S(1)}, bf16[2,2,256,256]{3,2,1,0:T(8,128)(2,1)S(1)}, u32[]{:S(2)}, u32[]{:S(2)}) collective-permute-start(bf16[2,2,256,256]{3,2,1,0:T(8,128)(2,1)S(1)} %pad_maximum_fusion.refs_3_), channel_id=1, source_target_pairs={{1,2},{3,4},{5,6},{2,1},{4,3},{6,5},{9,10},{11,12},{13,14},{10,9},... | collective-permute-start | bytes 1572872 | tf_op jit(solution)/shard_map/ppermute | solution.py:584
  79.8 17.9 %collective-permute-start.21 = (bf16[4,2,256,256]{3,2,1,0:T(8,128)(2,1)S(1)}, bf16[4,2,256,256]{3,2,1,0:T(8,128)(2,1)S(1)}, u32[]{:S(2)}, u32[]{:S(2)}) collective-permute-start(bf16[4,2,256,256]{3,2,1,0:T(8,128)(2,1)S(1)} %get-tuple-element.102.refs_2_.narrow), channel_id=1, source_target_pairs={{0,1},{2,3},{4,5},{6,7},{1,0},{3,2},{5,4},{7,6},{8,9},{10,11},{12,... | collective-permute-start | bytes 3145736 | tf_op jit(solution)/shard_map/ppermute | solution.py:584
  80.0 8.7 %collective-permute-start.18 = (bf16[2,256,256]{2,1,0:T(8,128)(2,1)S(1)}, bf16[2,256,256]{2,1,0:T(8,128)(2,1)S(1)}, u32[]{:S(2)}, u32[]{:S(2)}) collective-permute-start(bf16[2,256,256]{2,1,0:T(8,128)(2,1)S(1)} %get-tuple-element.103), channel_id=1, source_target_pairs={{0,32},{8,40},{16,48},{24,56},{64,96},{72,104},{80,112},{88,120},{... | collective-permute-start | bytes 786440 | tf_op jit(solution)/shard_map/ppermute | solution.py:590
  80.0 10.8 %collective-permute-start.19 = (bf16[2,256,256]{2,1,0:T(8,128)(2,1)S(1)}, bf16[2,256,256]{2,1,0:T(8,128)(2,1)S(1)}, u32[]{:S(2)}, u32[]{:S(2)}) collective-permute-start(bf16[2,256,256]{2,1,0:T(8,128)(2,1)S(1)} %get-tuple-element.104), channel_id=1, source_target_pairs={{32,64},{40,72},{48,80},{56,88},{64,32},{72,40},{80,48},{88,56},{3... | collective-permute-start | bytes 786440 | tf_op jit(solution)/shard_map/ppermute | solution.py:590
  83.9 21.7 %collective-permute-start.17 = (bf16[4,2,256,256]{3,2,1,0:T(8,128)(2,1)S(1)}, bf16[4,2,256,256]{3,2,1,0:T(8,128)(2,1)S(1)}, u32[]{:S(2)}, u32[]{:S(2)}) collective-permute-start(bf16[4,2,256,256]{3,2,1,0:T(8,128)(2,1)S(1)} %get-tuple-element.102.refs_2_.narrow), channel_id=1, source_target_pairs={{1,2},{3,4},{5,6},{2,1},{4,3},{6,5},{9,10},{11,12},{13,14},{10,9},... | collective-permute-start | bytes 3145736 | tf_op jit(solution)/shard_map/ppermute | solution.py:584
  90.9 14.8 %collective-permute-start.20 = (bf16[2,2,256,256]{3,2,1,0:T(8,128)(2,1)S(1)}, bf16[2,2,256,256]{3,2,1,0:T(8,128)(2,1)S(1)}, u32[]{:S(2)}, u32[]{:S(2)}) collective-permute-start(bf16[2,2,256,256]{3,2,1,0:T(8,128)(2,1)S(1)} %pad_maximum_fusion.1.refs_3_), channel_id=1, source_target_pairs={{1,2},{3,4},{5,6},{2,1},{4,3},{6,5},{9,10},{11,12},{13,14},{10,9},... | collective-permute-start | bytes 1572872 | tf_op jit(solution)/shard_map/ppermute | solution.py:584
  93.6 15.5 %collective-permute-start.23 = (bf16[2,256,256]{2,1,0:T(8,128)(2,1)S(1)}, bf16[2,256,256]{2,1,0:T(8,128)(2,1)S(1)}, u32[]{:S(2)}, u32[]{:S(2)}) collective-permute-start(bf16[2,256,256]{2,1,0:T(8,128)(2,1)S(1)} %get-tuple-element.111), channel_id=1, source_target_pairs={{0,8},{8,16},{16,24},{24,0},{32,40},{40,48},{48,56},{56,32},{64,72... | collective-permute-start | bytes 786440 | tf_op jit(solution)/shard_map/ppermute | solution.py:51
  94.1 15.8 %collective-permute-start.24 = (bf16[2,256,256]{2,1,0:T(8,128)(2,1)S(1)}, bf16[2,256,256]{2,1,0:T(8,128)(2,1)S(1)}, u32[]{:S(2)}, u32[]{:S(2)}) collective-permute-start(bf16[2,256,256]{2,1,0:T(8,128)(2,1)S(1)} %get-tuple-element.112), channel_id=1, source_target_pairs={{0,16},{8,24},{16,0},{24,8},{32,48},{40,56},{48,32},{56,40},{64,80... | collective-permute-start | bytes 786440 | tf_op jit(solution)/shard_map/ppermute | solution.py:51
  97.7 12.2 %collective-permute-start.25 = (bf16[2,256,256]{2,1,0:T(8,128)(2,1)S(1)}, bf16[2,256,256]{2,1,0:T(8,128)(2,1)S(1)}, u32[]{:S(2)}, u32[]{:S(2)}) collective-permute-start(bf16[2,256,256]{2,1,0:T(8,128)(2,1)S(1)} %get-tuple-element.113), channel_id=1, source_target_pairs={{0,24},{8,0},{16,8},{24,16},{32,56},{40,32},{48,40},{56,48},{64,88... | collective-permute-start | bytes 786440 | tf_op jit(solution)/shard_map/ppermute | solution.py:51
  109.9 9.1 %collective-permute-start.28 = (bf16[2,256,256]{2,1,0:T(8,128)(2,1)S(1)}, bf16[2,256,256]{2,1,0:T(8,128)(2,1)S(1)}, u32[]{:S(2)}, u32[]{:S(2)}) collective-permute-start(bf16[2,256,256]{2,1,0:T(8,128)(2,1)S(1)} %get-tuple-element.124), channel_id=1, source_target_pairs={{0,8},{8,16},{16,24},{24,0},{32,40},{40,48},{48,56},{56,32},{64,72... | collective-permute-start | bytes 786440 | tf_op jit(solution)/shard_map/ppermute | solution.py:51
  110.0 15.7 %collective-permute-start.27 = (bf16[2,256,256]{2,1,0:T(8,128)(2,1)S(1)}, bf16[2,256,256]{2,1,0:T(8,128)(2,1)S(1)}, u32[]{:S(2)}, u32[]{:S(2)}) collective-permute-start(bf16[2,256,256]{2,1,0:T(8,128)(2,1)S(1)} %get-tuple-element.123), channel_id=1, source_target_pairs={{0,16},{8,24},{16,0},{24,8},{32,48},{40,56},{48,32},{56,40},{64,80... | collective-permute-start | bytes 786440 | tf_op jit(solution)/shard_map/ppermute | solution.py:51
  113.8 13.2 %collective-permute-start.26 = (bf16[2,256,256]{2,1,0:T(8,128)(2,1)S(1)}, bf16[2,256,256]{2,1,0:T(8,128)(2,1)S(1)}, u32[]{:S(2)}, u32[]{:S(2)}) collective-permute-start(bf16[2,256,256]{2,1,0:T(8,128)(2,1)S(1)} %get-tuple-element.122), channel_id=1, source_target_pairs={{0,24},{8,0},{16,8},{24,16},{32,56},{40,32},{48,40},{56,48},{64,88... | collective-permute-start | bytes 786440 | tf_op jit(solution)/shard_map/ppermute | solution.py:51
  (5 other events, 24.7 us)
